TPU v7x, 512 devices: a whole 4x4x16 slice. The times are simulated.
512 devices in a mesh: gx: 16 (over x, y), gy: 32 (over z, core).
Axes of the slice: x: 4, y: 4, z: 16, core: 2. Of those that a mesh axis runs over, the one named last changes fastest.
Arguments:
- vol_rhs: float32 [2, 120, 524288], P(None, None, ('gx', 'gy')), may hold values from -6 to 6
- trace_in: float32 [2, 36, 1048576], P(None, None, ('gx', 'gy')), may hold values from -6 to 6
- pml_flag: int32 [524288], P(('gx', 'gy')), may hold values 0 or 1
- stretch: float32 [524288], P(('gx', 'gy')), may hold values from 0.5 to 4
- cond_op: float32 [4, 2, 36, 120], replicated, may hold values from -0.375 to 0.375
- skel_op: float32 [7, 2, 36, 36], replicated, may hold values from -1 to 4
- block_coef: float32 [7, 2, 1048576], P(None, None, ('gx', 'gy')), may hold values from -27 to 27
- recon_op: float32 [2, 120, 120], replicated, may hold values from -0.375 to 0.375
- lift_op: float32 [4, 2, 120, 36], replicated, may hold values from -0.375 to 0.375
- elem_face: int32 [4, 524288], P(None, ('gx', 'gy')), may hold values from 0 to 4095, as said below
- adjacency: int32 [6, 1048576], P(None, ('gx', 'gy')), may hold values from -1 to 4095, as said below
- halo_list: int32 [8, 131072], P(None, ('gx', 'gy')), may hold values from -1 to 2047, as said below
Outputs:
- trace_out: float32 [2, 36, 1048576], P(None, None, ('gx', 'gy'))
- volume_out: float32 [2, 120, 524288], P(None, None, ('gx', 'gy'))
Inputs may be any that keep to these rules, and one draw needn't show every extreme that they name: The list of direction d of partition p is halo_list[d, p * 256 .. (p + 1) * 256 - 1], local face numbers of p: its live entries are distinct and come first, -1 fills the rest; lists towards a position outside the grid are empty; in every draw some list is full. `elem_face`: every ghost slot named is a live entry of the list of an existing partition. `adjacency`: every ghost slot named is a live entry of the list of an existing partition; each face has 3 or 6 live entries, first, then -1.
All inputs are finite; a program needn't handle non-finite values. No bound on the sum of `pml_flag` on one device may be relied on, other than what follows from the above.
Results may differ from a plain program's by a relative error of at most 0.0003.
Values sent between devices are 32-bit elements; how exact they have to be, the bound alone decides.
No kernel may reach another device: no remote copies, remote signals or barrier semaphores. Data moves between devices by JAX's collectives and lax.ppermute only.
A program may use at most 128 MiB of HBM per device.

v0:
```python
import functools

import jax
import jax.numpy as jnp
from jax import lax
from jax.experimental import pallas as pl
from jax.experimental.pallas import tpu as pltpu
from jax.sharding import PartitionSpec as P

F32 = jnp.float32
BF16 = jnp.bfloat16
HALF = 40
ROWS = 2 * HALF
LANES = 128
PAD = 8
DIRS = 8
UNROLL = 16
MIB = 1 << 20


def split(values):
    high = values.astype(BF16)
    return high, (values - high.astype(F32)).astype(BF16)


def dot(left, right, left_dim=1, right_dim=0):
    return lax.dot_general(
        left, right, (((left_dim,), (right_dim,)), ((), ())), preferred_element_type=F32
    )


def half_rolled(block, height):
    wide = jnp.concatenate(
        [block, jnp.zeros((height, LANES - block.shape[1]), F32)], axis=1
    )
    return wide, pltpu.roll(wide, HALF, 1)


def gather_rows(count, index_of, source, target, base=0):
    def some(step, carry):
        first = step * UNROLL
        for extra in range(UNROLL):
            row = index_of(first + extra)
            target[pl.ds(base + first + extra, 1), :] = source[pl.ds(row + PAD, 1), :]
        return carry

    lax.fori_loop(0, count // UNROLL, some, 0)


def parcel_of(rows):
    return rows.T[:ROWS]


def rows_of(parcel):
    halo = parcel.shape[1]
    return jnp.concatenate([parcel, jnp.zeros((LANES - ROWS, halo), F32)], axis=0).T


def scaled_volume(vol, flag, stretch, scaled):
    nv = vol.shape[1]
    tilt = flag[...].astype(F32) * stretch[...]
    real, imag = vol[0], vol[1]
    fill = jnp.zeros((LANES - nv, vol.shape[2]), F32)
    scaled[0:nv, :] = real - tilt * imag
    scaled[nv:LANES, :] = fill
    scaled[LANES : LANES + nv, :] = imag + tilt * real
    scaled[LANES + nv : 2 * LANES, :] = fill


def prepare_kernel(
    vol, flag, stretch, trace, cond_op, elem_face, halo_list,
    table, own_sum, up, mid, down,
    scaled, turned, matrix, matrix_hi, matrix_lo, parts, sums0, sums1, sums2, sums3, picked,
):
    nq, faces = trace.shape[1], trace.shape[2]
    nv, elems = vol.shape[1], vol.shape[2]
    halo = halo_list.shape[1]
    turned[...] = jnp.zeros_like(turned)
    turned[0:nq, :] = trace[0]
    turned[HALF : HALF + nq, :] = trace[1]
    table[0:PAD, :] = jnp.zeros((PAD, LANES), F32)
    for first in range(0, faces, LANES):
        table[PAD + first : PAD + first + LANES, :] = turned[:, first : first + LANES].T
    scaled_volume(vol, flag, stretch, scaled)
    matrix[...] = jnp.zeros_like(matrix)
    for corner in range(4):
        low = corner * LANES
        matrix[low : low + nq, 0:nv] = cond_op[corner, 0]
        matrix[low : low + nq, LANES : LANES + nv] = -cond_op[corner, 1]
        matrix[low + HALF : low + HALF + nq, 0:nv] = cond_op[corner, 1]
        matrix[low + HALF : low + HALF + nq, LANES : LANES + nv] = cond_op[corner, 0]
    high, rest = split(matrix[...])
    matrix_hi[...] = high
    matrix_lo[...] = rest
    for first in range(0, elems, LANES):
        stop = first + LANES
        columns = jnp.concatenate(
            [scaled[0:LANES, first:stop].T, scaled[LANES : 2 * LANES, first:stop].T], axis=1
        )
        high, rest = split(columns)
        product = (
            dot(high, matrix_hi[...], 1, 1)
            + dot(rest, matrix_hi[...], 1, 1)
            + dot(high, matrix_lo[...], 1, 1)
        )
        for corner in range(4):
            parts[corner, first:stop, :] = product[:, corner * LANES : (corner + 1) * LANES]
    sums = (sums0, sums1, sums2, sums3)
    for total in sums:
        total[...] = jnp.zeros_like(total)

    def add_some(step, carry):
        for extra in range(4):
            elem = step * 4 + extra
            for corner in range(4):
                slot = elem_face[corner, elem]
                total = sums[corner]
                total[pl.ds(slot, 1), :] = (
                    total[pl.ds(slot, 1), :] + parts[corner, pl.ds(elem, 1), :]
                )
        return carry

    lax.fori_loop(0, elems // 4, add_some, 0)

    def summed(first, size):
        stop = first + size
        return (sums0[first:stop] + sums1[first:stop]) + (sums2[first:stop] + sums3[first:stop])

    own_sum[...] = summed(0, faces)
    for direction in range(DIRS):
        gather_rows(
            halo, lambda j: halo_list[direction, j], table, picked, direction * halo
        )
    for direction in range(DIRS):
        parcel = parcel_of(picked[direction * halo : (direction + 1) * halo, :])
        back = parcel_of(summed(faces + direction * halo, halo))
        if direction < 3:
            down[direction] = parcel
            up[3 + direction] = back
        elif direction < 5:
            mid[direction - 3] = parcel
            mid[direction - 1] = back
        else:
            up[direction - 5] = parcel
            down[direction - 2] = back


def skeleton_matrix(skel_op, matrix):
    nq = skel_op.shape[2]
    for block in range(skel_op.shape[0]):
        real, real_moved = half_rolled(skel_op[block, 0], nq)
        imag, imag_moved = half_rolled(skel_op[block, 1], nq)
        fill = jnp.zeros((HALF - nq, LANES), F32)
        whole = jnp.concatenate([real - imag_moved, fill, imag + real_moved, fill], axis=0)
        high, rest = split(whole)
        low = block * 2 * ROWS
        matrix[low : low + 2 * ROWS, :] = jnp.concatenate(
            [
                jnp.concatenate([high, high], axis=1),
                jnp.concatenate([rest, jnp.zeros_like(rest)], axis=1),
            ],
            axis=0,
        )


def skeleton_tile(matrix, block_coef, source_of, first, size):
    real_sum = jnp.zeros((HALF, size), F32)
    imag_sum = jnp.zeros((HALF, size), F32)
    for block in range(block_coef.shape[0]):
        high, rest = split(source_of(block, first, size))
        low = block * 2 * ROWS
        product = dot(
            matrix[low : low + 2 * ROWS, :], jnp.concatenate([high, rest], axis=1), 1, 1
        )
        real = product[0:HALF] + product[ROWS : ROWS + HALF]
        imag = product[HALF:ROWS] + product[ROWS + HALF : 2 * ROWS]
        coef_real = block_coef[block, 0:1, pl.ds(first, size)]
        coef_imag = block_coef[block, 1:2, pl.ds(first, size)]
        real_sum = real_sum + (coef_real * real - coef_imag * imag)
        imag_sum = imag_sum + (coef_real * imag + coef_imag * real)
    return real_sum, imag_sum


def gather_neighbours(adjacency, slots, picked):
    count, faces = adjacency.shape
    for neighbour in range(count):
        gather_rows(
            faces, lambda j: adjacency[neighbour, j], slots, picked, neighbour * faces
        )


def residual_kernel(
    table, own_sum, up, down, right, left, skel_op, block_coef, adjacency, halo_list,
    slots, rest_table, res_up, res_mid, res_down,
    picked, matrix, back, sums0, sums1, sums2, sums3,
):
    faces = adjacency.shape[1]
    halo = halo_list.shape[1]
    ghosts = (left[0], down[1], right[0], left[1], right[1], left[2], up[1], right[2])
    slots[0 : PAD + faces, :] = table[...]
    for direction in range(DIRS):
        first = PAD + faces + direction * halo
        slots[first : first + halo, :] = rows_of(ghosts[direction])
    returned = (right[3], up[4], left[3], right[4], left[4], right[5], down[4], left[5])
    for direction in range(DIRS):
        back[direction] = rows_of(returned[direction])
    skeleton_matrix(skel_op, matrix)
    gather_neighbours(adjacency, slots, picked)
    tile = 256

    def source_of(block, first, size):
        if block == 0:
            return slots[pl.ds(PAD + first, size), :]
        return picked[pl.ds((block - 1) * faces + first, size), :]

    def some(step, carry):
        first = pl.multiple_of(step * tile, tile)
        real, imag = skeleton_tile(matrix, block_coef, source_of, first, tile)
        applied = rows_of(jnp.concatenate([real, imag], axis=0))
        sums0[pl.ds(PAD + first, tile), :] = own_sum[pl.ds(first, tile), :] - applied
        return carry

    lax.fori_loop(0, faces // tile, some, 0)
    sums0[0:PAD, :] = jnp.zeros((PAD, LANES), F32)
    others = (sums1, sums2, sums3)
    for total in others:
        total[...] = jnp.zeros_like(total)
    sums = (sums0,) + others

    def add_some(step, carry):
        for extra in range(2):
            entry = step * 2 + extra
            for direction in range(DIRS):
                face = halo_list[direction, entry] + PAD
                total = sums[direction % 4]
                total[pl.ds(face, 1), :] = (
                    total[pl.ds(face, 1), :] + back[direction, pl.ds(entry, 1), :]
                )
        return carry

    lax.fori_loop(0, halo // 2, add_some, 0)
    rest_table[...] = (sums0[...] + sums1[...]) + (sums2[...] + sums3[...])
    rest_table[0:PAD, :] = jnp.zeros((PAD, LANES), F32)
    for direction in range(DIRS):
        gather_rows(
            halo, lambda j: halo_list[direction, j], rest_table, picked, direction * halo
        )
    for direction in range(DIRS):
        parcel = parcel_of(picked[direction * halo : (direction + 1) * halo, :])
        if direction < 3:
            res_down[direction] = parcel
        elif direction < 5:
            res_mid[direction - 3] = parcel
        else:
            res_up[direction - 5] = parcel


def turn_kernel(rest_table, turned):
    for first in range(0, turned.shape[1], LANES):
        turned[:, first : first + LANES] = parcel_of(
            rest_table[PAD + first : PAD + first + LANES, :]
        )


def recon_kernel(vol, flag, stretch, recon_op, base, scaled, matrix):
    nv, elems = vol.shape[1], vol.shape[2]
    scaled_volume(vol, flag, stretch, scaled)
    matrix[...] = jnp.zeros_like(matrix)
    matrix[0:nv, 0:nv] = recon_op[0]
    matrix[0:nv, LANES : LANES + nv] = -recon_op[1]
    matrix[LANES : LANES + nv, 0:nv] = recon_op[1]
    matrix[LANES : LANES + nv, LANES : LANES + nv] = recon_op[0]
    high, rest = split(matrix[...])
    for first in range(0, elems, 256):
        wanted, fine = split(scaled[:, first : first + 256])
        product = dot(high, wanted) + dot(high, fine) + dot(rest, wanted)
        base[0, :, first : first + 256] = product[0:nv]
        base[1, :, first : first + 256] = product[LANES : LANES + nv]


def image_kernel(
    rest_table, turned, up, down, right, left, skel_op, block_coef, adjacency,
    slots, partial,
    picked, matrix,
):
    faces = adjacency.shape[1]
    halo = up.shape[2]
    ghosts = (left[0], down[1], right[0], left[1], right[1], left[2], up[1], right[2])
    slots[0 : PAD + faces, :] = rest_table[...]
    for direction in range(DIRS):
        first = PAD + faces + direction * halo
        slots[first : first + halo, :] = rows_of(ghosts[direction])
    skeleton_matrix(skel_op, matrix)
    gather_neighbours(adjacency, slots, picked)
    tile = 256

    def source_of(block, first, size):
        if block == 0:
            return slots[pl.ds(PAD + first, size), :]
        return picked[pl.ds((block - 1) * faces + first, size), :]

    def some(step, carry):
        first = pl.multiple_of(step * tile, tile)
        real, imag = skeleton_tile(matrix, block_coef, source_of, first, tile)
        rest_real = turned[0:HALF, pl.ds(first, tile)]
        rest_imag = turned[HALF:ROWS, pl.ds(first, tile)]
        return (
            carry[0] + (real * rest_real + imag * rest_imag),
            carry[1] + (real * rest_imag - imag * rest_real),
            carry[2] + (real * real + imag * imag),
        )

    zero = jnp.zeros((HALF, tile), F32)
    totals = lax.fori_loop(0, faces // tile, some, (zero, zero, zero))
    lane = lax.broadcasted_iota(jnp.int32, (1, LANES), 1)
    line = jnp.zeros((1, LANES), F32)
    for place in range(3):
        line = line + jnp.where(lane == place, jnp.sum(totals[place]), 0.0)
    partial[...] = line


def finish_kernel(
    gathered, trace, turned, slots_trace, slots_rest, lift_op, base, elem_face,
    trace_out, volume_out,
    slots, picked, matrix,
):
    nq = trace.shape[1]
    nv, elems = base.shape[1], base.shape[2]
    line = jnp.sum(gathered[...], axis=0, keepdims=True)
    lane = lax.broadcasted_iota(jnp.int32, (1, LANES), 1)
    entry = [
        jnp.sum(jnp.where(lane == place, line, 0.0), axis=1, keepdims=True)
        for place in range(3)
    ]
    step_real = entry[0] / entry[2]
    step_imag = entry[1] / entry[2]
    rest_real = turned[0:nq, :]
    rest_imag = turned[HALF : HALF + nq, :]
    trace_out[0] = trace[0] + (step_real * rest_real - step_imag * rest_imag)
    trace_out[1] = trace[1] + (step_real * rest_imag + step_imag * rest_real)
    for block in range(4):
        real, real_moved = half_rolled(lift_op[block, 0], nv)
        imag, imag_moved = half_rolled(lift_op[block, 1], nv)
        fill = jnp.zeros((LANES - nv, LANES), F32)
        high, rest = split(
            jnp.concatenate([real - imag_moved, fill, imag + real_moved, fill], axis=0)
        )
        low = block * 4 * LANES
        matrix[low : low + 4 * LANES, :] = jnp.concatenate(
            [
                jnp.concatenate([high, high], axis=1),
                jnp.concatenate([rest, jnp.zeros_like(rest)], axis=1),
            ],
            axis=0,
        )
    size = 256
    is_real = lax.broadcasted_iota(jnp.int32, (size, LANES), 1) < HALF

    def new_rows(step, carry):
        first = pl.multiple_of(PAD + step * size, PAD)
        rest_rows = slots_rest[pl.ds(first, size), :]
        turn = jnp.where(
            is_real, -pltpu.roll(rest_rows, LANES - HALF, 1), pltpu.roll(rest_rows, HALF, 1)
        )
        slots[pl.ds(first, size), :] = slots_trace[pl.ds(first, size), :] + (
            step_real * rest_rows + step_imag * turn
        )
        return carry

    lax.fori_loop(0, (slots.shape[0] - PAD) // size, new_rows, 0)
    for corner in range(4):
        gather_rows(elems, lambda j: elem_face[corner, j], slots, picked, corner * elems)
    for first in range(0, elems, size):
        total = jnp.zeros((2 * LANES, size), F32)
        for corner in range(4):
            low = corner * elems + first
            rows = jnp.concatenate(
                [picked[low : low + size, 0:LANES]], axis=1
            )
            high, rest = split(rows)
            at = corner * 4 * LANES
            product = dot(
                matrix[at : at + 4 * LANES, :], jnp.concatenate([high, rest], axis=1), 1, 1
            )
            total = total + (product[0 : 2 * LANES] + product[2 * LANES : 4 * LANES])
        stop = first + size
        volume_out[0, :, first:stop] = base[0, :, first:stop] - total[0:nv]
        volume_out[1, :, first:stop] = base[1, :, first:stop] - total[LANES : LANES + nv]


def call(kernel, name, args, out_shapes, scratch, scalars=(), cost=1000000):
    vmem = pl.BlockSpec(memory_space=pltpu.VMEM)
    smem = pl.BlockSpec(memory_space=pltpu.SMEM)
    return pl.pallas_call(
        kernel,
        name=name,
        out_shape=[jax.ShapeDtypeStruct(shape, F32) for shape in out_shapes],
        in_specs=[smem if number in scalars else vmem for number in range(len(args))],
        out_specs=[vmem] * len(out_shapes),
        scratch_shapes=[pltpu.VMEM(shape, kind) for shape, kind in scratch],
        compiler_params=pltpu.CompilerParams(vmem_limit_bytes=56 * MIB),
        cost_estimate=pl.CostEstimate(flops=cost, bytes_accessed=4 * MIB, transcendentals=0),
    )(*args)


def from_behind(block, axis, distance):
    devices = range(lax.axis_size(axis))
    route = [(i - distance, i) for i in devices if i - distance in devices]
    return lax.ppermute(block, axis, route)


def summed_over(line, axis, sizes):
    count = lax.axis_size(axis)
    stride = 1
    for size in sizes:
        if stride == count:
            break
        size = min(size, count // stride)
        groups = [
            [block * size * stride + low + stride * k for k in range(size)]
            for block in range(count // (size * stride))
            for low in range(stride)
        ]
        line = lax.all_gather(jnp.sum(line, axis=0), axis, axis_index_groups=groups)
        stride *= size
    return line


def local(
    vol_rhs, trace_in, pml_flag, stretch, cond_op, skel_op, block_coef, recon_op, lift_op,
    elem_face, adjacency, halo_list,
):
    nv, elems = vol_rhs.shape[1], vol_rhs.shape[2]
    faces = trace_in.shape[2]
    halo = halo_list.shape[1]
    blocks = skel_op.shape[0]
    neighbours = adjacency.shape[0]
    slots = faces + DIRS * halo
    flag = pml_flag.reshape(1, elems)
    tilt = stretch.reshape(1, elems)
    table, own_sum, up, mid, down = call(
        prepare_kernel,
        "prepare",
        (vol_rhs, flag, tilt, trace_in, cond_op, elem_face, halo_list),
        [(PAD + faces, LANES), (faces, LANES), (6, ROWS, halo), (4, ROWS, halo), (6, ROWS, halo)],
        [
            ((2 * LANES, elems), F32),
            ((LANES, faces), F32),
            ((4 * LANES, 2 * LANES), F32),
            ((4 * LANES, 2 * LANES), BF16),
            ((4 * LANES, 2 * LANES), BF16),
            ((4, elems, LANES), F32),
        ]
        + [((slots, LANES), F32)] * 4
        + [((DIRS * halo, LANES), F32)],
        (5, 6),
    )
    up = from_behind(up, "gx", 1)
    down = from_behind(down, "gx", -1)
    (base,) = call(
        recon_kernel,
        "recon",
        (vol_rhs, flag, tilt, recon_op),
        [(2, nv, elems)],
        [((2 * LANES, elems), F32), ((2 * LANES, 2 * LANES), F32)],
    )
    right = jnp.stack([down[2], mid[1], up[2], up[3], mid[2], down[3]])
    left = jnp.stack([down[0], mid[0], up[0], up[5], mid[3], down[5]])
    right = from_behind(right, "gy", 1)
    left = from_behind(left, "gy", -1)
    slots_trace, rest_table, res_up, res_mid, res_down = call(
        residual_kernel,
        "residual",
        (table, own_sum, up, down, right, left, skel_op, block_coef, adjacency, halo_list),
        [(PAD + slots, LANES), (PAD + faces, LANES)]
        + [(3, ROWS, halo), (2, ROWS, halo), (3, ROWS, halo)],
        [
            ((neighbours * faces, LANES), F32),
            ((blocks * 2 * ROWS, 2 * LANES), BF16),
            ((DIRS, halo, LANES), F32),
        ]
        + [((PAD + faces, LANES), F32)] * 4,
        (8, 9),
    )
    res_up = from_behind(res_up, "gx", 1)
    res_down = from_behind(res_down, "gx", -1)
    (turned,) = call(turn_kernel, "turn", (rest_table,), [(ROWS, faces)], [])
    res_right = jnp.stack([res_down[2], res_mid[1], res_up[2]])
    res_left = jnp.stack([res_down[0], res_mid[0], res_up[0]])
    res_right = from_behind(res_right, "gy", 1)
    res_left = from_behind(res_left, "gy", -1)
    slots_rest, partial = call(
        image_kernel,
        "image",
        (
            rest_table, turned, res_up, res_down, res_right, res_left, skel_op, block_coef,
            adjacency,
        ),
        [(PAD + slots, LANES), (1, LANES)],
        [
            ((neighbours * faces, LANES), F32),
            ((blocks * 2 * ROWS, 2 * LANES), BF16),
        ],
        (8,),
    )
    gathered = summed_over(partial, "gy", (2, 4, 4))
    gathered = summed_over(gathered, "gx", (4, 4))
    trace_out, volume_out = call(
        finish_kernel,
        "finish",
        (gathered, trace_in, turned, slots_trace, slots_rest, lift_op, base, elem_face),
        [trace_in.shape, vol_rhs.shape],
        [
            ((PAD + slots, LANES), F32),
            ((4 * elems, LANES), F32),
            ((4 * 4 * LANES, 2 * LANES), BF16),
        ],
        (7,),
    )
    return trace_out, volume_out


def solution(mesh):
    split_last = ("gx", "gy")
    in_specs = (
        P(None, None, split_last),
        P(None, None, split_last),
        P(split_last),
        P(split_last),
        P(),
        P(),
        P(None, None, split_last),
        P(),
        P(),
        P(None, split_last),
        P(None, split_last),
        P(None, split_last),
    )
    out_specs = (P(None, None, split_last), P(None, None, split_last))
    return jax.shard_map(
        local, mesh=mesh, in_specs=in_specs, out_specs=out_specs, check_vma=False
    )
```

profile of v0, /device:TPU:8, one launch (start us, length us, event | category | flops | bytes accessed | tf_op | source)
XLA Modules:
  0.0 240.2 jit_solution(10759615720731768300)
XLA Ops:
  0.6 2.3 copy.22.trace
  2.9 1.6 copy.23.cond_op
  4.5 17.8 %prepare.1 = (f32[2056,128]{1,0:T(8,128)}, f32[2048,128]{1,0:T(8,128)}, f32[6,80,256]{2,1,0:T(8,128)}, f32[4,80,256]{2,1,0:T(8,128)}, f32[6,80,256]{2,1,0:T(8,128)}) custom-call(f32[2,120,1024]{2,1,0:T(8,128)} %vol.3, s32[1,1024]{1,0:T(1,128)} %bitcast.8, f32[1,1024]{1,0:T(1,128)} %bitcast.10, f32[2,36,2048]{2,1,0:T(8,128)} %copy.22.trace, ...), custom_call_target="tpu_custom_call" | custom-call | flops 1000000 | bytes 4194304 | tf_op jit(solution)/shard_map/prepare/pallas_call | solution.py:394
  22.3 7.7 %collective-permute-start.1 = (f32[6,80,256]{2,1,0:T(8,128)}, f32[6,80,256]{2,1,0:T(8,128)S(1)}, u32[]{:S(2)}, u32[]{:S(2)}) collective-permute-start(f32[6,80,256]{2,1,0:T(8,128)} %get-tuple-element.17), channel_id=1, source_target_pairs={{32,0},{64,32},{96,64},{128,96},{160,128},{192,160},{224,192},{256... | collective-permute-start | bytes 1474568 | tf_op jit(solution)/shard_map/ppermute | solution.py:409
  30.1 1.9 collective-permute-start
  32.0 5.4 %collective-permute-done.1.down = f32[6,80,256]{2,1,0:T(8,128)S(1)} collective-permute-done((f32[6,80,256]{2,1,0:T(8,128)}, f32[6,80,256]{2,1,0:T(8,128)S(1)}, u32[]{:S(2)}, u32[]{:S(2)}) %collective-permute-start.1) | collective-permute-done | bytes 491552 | tf_op jit(solution)/shard_map/ppermute | solution.py:409
  38.5 2.5 %collective-permute-done.up = f32[6,80,256]{2,1,0:T(8,128)S(1)} collective-permute-done((f32[6,80,256]{2,1,0:T(8,128)}, f32[6,80,256]{2,1,0:T(8,128)S(1)}, u32[]{:S(2)}, u32[]{:S(2)}) %collective-permute-start) | collective-permute-done | bytes 491552 | tf_op jit(solution)/shard_map/ppermute | solution.py:409
  45.5 2.3 collective-permute-done.3.left
  48.6 47.6 %residual.1 = (f32[4104,128]{1,0:T(8,128)}, f32[2056,128]{1,0:T(8,128)}, f32[3,80,256]{2,1,0:T(8,128)}, f32[2,80,256]{2,1,0:T(8,128)}, f32[3,80,256]{2,1,0:T(8,128)}) custom-call(f32[2056,128]{1,0:T(8,128)} %get-tuple-element.14.table, f32[2048,128]{1,0:T(8,128)} %get-tuple-element.15.own_sum, f32[6,80,256]{2,1,0:T(8,128)} %copy-done.1, ...), custom_call_target="tpu_custom_call" | custom-call | flops 1000000 | bytes 4194304 | tf_op jit(solution)/shard_map/residual/pallas_call | solution.py:394
  96.2 1.9 collective-permute-start.5
  98.1 3.9 %collective-permute-start.4 = (f32[3,80,256]{2,1,0:T(8,128)}, f32[3,80,256]{2,1,0:T(8,128)S(1)}, u32[]{:S(2)}, u32[]{:S(2)}) collective-permute-start(f32[3,80,256]{2,1,0:T(8,128)} %get-tuple-element.20), channel_id=1, source_target_pairs={{0,32},{32,64},{64,96},{96,128},{128,160},{160,192},{192,224},{224... | collective-permute-start | bytes 737288 | tf_op jit(solution)/shard_map/ppermute | solution.py:409
  103.0 1.5 collective-permute-done.5.down
  104.5 1.9 collective-permute-done.4.up
  107.8 8.2 %collective-permute-start.6 = (f32[3,80,256]{2,1,0:T(8,128)S(1)}, f32[3,80,256]{2,1,0:T(8,128)S(1)}, u32[]{:S(2)}, u32[]{:S(2)}) collective-permute-start(f32[3,80,256]{2,1,0:T(8,128)S(1)} %pad_maximum_fusion), channel_id=1, source_target_pairs={{0,1},{1,2},{2,3},{3,4},{4,5},{5,6},{6,7},{7,8},{8,9},{9,10},{10,1... | collective-permute-start | bytes 737288 | tf_op jit(solution)/shard_map/ppermute | solution.py:409
  117.0 2.9 %recon.1.base = f32[2,120,1024]{2,1,0:T(8,128)} custom-call(f32[2,120,1024]{2,1,0:T(8,128)} %vol.3, s32[1,1024]{1,0:T(1,128)} %bitcast.9, f32[1,1024]{1,0:T(1,128)} %bitcast.11, f32[2,120,120]{2,1,0:T(8,128)} %recon_op.1), custom_call_target="tpu_custom_call" | custom-call | flops 1000000 | bytes 4194304 | tf_op jit(solution)/shard_map/recon/pallas_call | solution.py:394
  119.9 2.4 turn.1.turned
  123.7 36.5 %image.1 = (f32[4104,128]{1,0:T(8,128)}, f32[1,128]{1,0:T(1,128)}) custom-call(f32[2056,128]{1,0:T(8,128)} %get-tuple-element.19.rest_table, f32[80,2048]{1,0:T(8,128)} %turn.1.turned, f32[3,80,256]{2,1,0:T(8,128)} %copy-done.3, f32[3,80,256]{2,1,0:T(8,128)} %copy-done.2, f32[3,80,256]{2,1,0:T(8,128)} %copy-done.8, f32[3,80,256]{2,1,0:T(8,128)} %copy-done.7, ...), custom_call_target="tpu_custom_call" | custom-call | flops 1000000 | bytes 4194304 | tf_op jit(solution)/shard_map/image/pallas_call | solution.py:394
  160.2 4.0 %all-gather.4 = f32[2,1,128]{2,1,0:T(1,128)S(1)} all-gather(f32[1,1,128]{2,1,0:T(1,128)} %bitcast.17), channel_id=1, replica_groups={{0,1},{2,3},{4,5},{6,7},{8,9},{10,11},{12,13},{14,15},{16,17},{18,19},{..., dimensions={0}, use_global_device_ids=true | all-gather | bytes 1536 | tf_op jit(solution)/shard_map/all_gather | solution.py:424
  164.2 15.7 %all-gather.5 = f32[4,1,128]{2,1,0:T(1,128)S(1)} all-gather(f32[1,1,128]{2,1,0:T(1,128)S(1)} %bitcast.14), channel_id=2, replica_groups={{0,2,4,6},{1,3,5,7},{8,10,12,14},{9,11,13,15},{16,18,20,22},{17,19,21,2..., dimensions={0}, use_global_device_ids=true | all-gather | bytes 2560 | tf_op jit(solution)/shard_map/all_gather | solution.py:424
  180.0 16.2 %all-gather.6 = f32[4,1,128]{2,1,0:T(1,128)S(1)} all-gather(f32[1,1,128]{2,1,0:T(1,128)S(1)} %bitcast.15), channel_id=3, replica_groups={{0,8,16,24},{1,9,17,25},{2,10,18,26},{3,11,19,27},{4,12,20,28},{5,13,21..., dimensions={0}, use_global_device_ids=true | all-gather | bytes 2560 | tf_op jit(solution)/shard_map/all_gather | solution.py:424
  196.2 10.8 %all-gather.7 = f32[4,1,128]{2,1,0:T(1,128)S(1)} all-gather(f32[1,1,128]{2,1,0:T(1,128)S(1)} %bitcast.16), channel_id=4, replica_groups={{0,32,64,96},{128,160,192,224},{256,288,320,352},{384,416,448,480},{1,3..., dimensions={0}, use_global_device_ids=true | all-gather | bytes 2560 | tf_op jit(solution)/shard_map/all_gather | solution.py:424
  207.0 13.3 %all-gather.8 = f32[4,1,128]{2,1,0:T(1,128)} all-gather(f32[1,1,128]{2,1,0:T(1,128)S(1)} %bitcast.13), channel_id=5, replica_groups={{0,128,256,384},{32,160,288,416},{64,192,320,448},{96,224,352,480},{1,1..., dimensions={0}, use_global_device_ids=true | all-gather | bytes 2560 | tf_op jit(solution)/shard_map/all_gather | solution.py:424
  220.3 17.5 %finish.1 = (f32[2,36,2048]{2,1,0:T(8,128)}, f32[2,120,1024]{2,1,0:T(8,128)}) custom-call(f32[4,128]{1,0:T(4,128)} %bitcast.12, f32[2,36,2048]{2,1,0:T(8,128)} %copy.22.trace, f32[80,2048]{1,0:T(8,128)} %turn.1.turned, f32[4104,128]{1,0:T(8,128)} %get-tuple-element.24.slots_trace, f32[4104,128]{1,0:T(8,128)} %get-tuple-element.25.slots_rest, ...), custom_call_target="tpu_custom_call" | custom-call | flops 1000000 | bytes 4194304 | tf_op jit(solution)/shard_map/finish/pallas_call | solution.py:394
  237.8 2.4 copy.28
  (44 shorter events, 11.2 us)
Async XLA Ops:
  2.9 41.9 %copy-start.6 = (f32[7,2,36,36]{3,1,2,0:T(2,128)S(1)}, f32[7,2,36,36]{3,1,2,0:T(2,128)}, u32[]{:S(2)}) copy-start(f32[7,2,36,36]{3,1,2,0:T(2,128)} %param.17) | copy-start | bytes 217732
  22.3 15.1 %collective-permute-start.1 = (f32[6,80,256]{2,1,0:T(8,128)}, f32[6,80,256]{2,1,0:T(8,128)S(1)}, u32[]{:S(2)}, u32[]{:S(2)}) collective-permute-start(f32[6,80,256]{2,1,0:T(8,128)} %get-tuple-element.17), channel_id=1, source_target_pairs={{32,0},{64,32},{96,64},{128,96},{160,128},{192,160},{224,192},{256... | collective-permute-start | bytes 1474568 | tf_op jit(solution)/shard_map/ppermute | solution.py:409
  30.1 10.9 %collective-permute-start = (f32[6,80,256]{2,1,0:T(8,128)}, f32[6,80,256]{2,1,0:T(8,128)S(1)}, u32[]{:S(2)}, u32[]{:S(2)}) collective-permute-start(f32[6,80,256]{2,1,0:T(8,128)} %get-tuple-element.16), channel_id=1, source_target_pairs={{0,32},{32,64},{64,96},{96,128},{128,160},{160,192},{192,224},{224... | collective-permute-start | bytes 1474568 | tf_op jit(solution)/shard_map/ppermute | solution.py:409
  37.4 10.5 %copy-start = (f32[6,80,256]{2,1,0:T(8,128)}, f32[6,80,256]{2,1,0:T(8,128)S(1)}, u32[]{:S(2)}) copy-start(f32[6,80,256]{2,1,0:T(8,128)S(1)} %collective-permute-done.1.down) | copy-start | bytes 1474564
  41.0 6.9 %copy-start.1 = (f32[6,80,256]{2,1,0:T(8,128)}, f32[6,80,256]{2,1,0:T(8,128)S(1)}, u32[]{:S(2)}) copy-start(f32[6,80,256]{2,1,0:T(8,128)S(1)} %collective-permute-done.up) | copy-start | bytes 1474564
  42.1 3.4 %collective-permute-start.2 = (f32[6,80,256]{2,1,0:T(8,128)S(1)}, f32[6,80,256]{2,1,0:T(8,128)S(1)}, u32[]{:S(2)}, u32[]{:S(2)}) collective-permute-start(f32[6,80,256]{2,1,0:T(8,128)S(1)} %get-tuple-element.31), channel_id=1, source_target_pairs={{0,1},{1,2},{2,3},{3,4},{4,5},{5,6},{6,7},{7,8},{8,9},{9,10},{10,1... | collective-permute-start | bytes 1474568 | tf_op jit(solution)/shard_map/ppermute | solution.py:409
  43.5 4.4 %collective-permute-start.3 = (f32[6,80,256]{2,1,0:T(8,128)S(1)}, f32[6,80,256]{2,1,0:T(8,128)S(1)}, u32[]{:S(2)}, u32[]{:S(2)}) collective-permute-start(f32[6,80,256]{2,1,0:T(8,128)S(1)} %get-tuple-element.30), channel_id=1, source_target_pairs={{1,0},{2,1},{3,2},{4,3},{5,4},{6,5},{7,6},{8,7},{9,8},{10,9},{11,1... | collective-permute-start | bytes 1474568 | tf_op jit(solution)/shard_map/ppermute | solution.py:409
  45.5 2.3 copy-start.4
  47.8 0.8 copy-start.5
  48.6 67.4 %copy-start.9 = (f32[4,2,120,36]{2,1,3,0:T(2,128)S(1)}, f32[4,2,120,36]{2,1,3,0:T(2,128)}, u32[]{:S(2)}) copy-start(f32[4,2,120,36]{2,1,3,0:T(2,128)} %param.20) | copy-start | bytes 414724
  96.2 8.3 %collective-permute-start.5 = (f32[3,80,256]{2,1,0:T(8,128)}, f32[3,80,256]{2,1,0:T(8,128)S(1)}, u32[]{:S(2)}, u32[]{:S(2)}) collective-permute-start(f32[3,80,256]{2,1,0:T(8,128)} %get-tuple-element.21), channel_id=1, source_target_pairs={{32,0},{64,32},{96,64},{128,96},{160,128},{192,160},{224,192},{256... | collective-permute-start | bytes 737288 | tf_op jit(solution)/shard_map/ppermute | solution.py:409
  98.1 8.3 %collective-permute-start.4 = (f32[3,80,256]{2,1,0:T(8,128)}, f32[3,80,256]{2,1,0:T(8,128)S(1)}, u32[]{:S(2)}, u32[]{:S(2)}) collective-permute-start(f32[3,80,256]{2,1,0:T(8,128)} %get-tuple-element.20), channel_id=1, source_target_pairs={{0,32},{32,64},{64,96},{96,128},{128,160},{160,192},{192,224},{224... | collective-permute-start | bytes 737288 | tf_op jit(solution)/shard_map/ppermute | solution.py:409
  104.5 15.4 %copy-start.2 = (f32[3,80,256]{2,1,0:T(8,128)}, f32[3,80,256]{2,1,0:T(8,128)S(1)}, u32[]{:S(2)}) copy-start(f32[3,80,256]{2,1,0:T(8,128)S(1)} %collective-permute-done.5.down) | copy-start | bytes 737284
  106.4 15.9 %copy-start.3 = (f32[3,80,256]{2,1,0:T(8,128)}, f32[3,80,256]{2,1,0:T(8,128)S(1)}, u32[]{:S(2)}) copy-start(f32[3,80,256]{2,1,0:T(8,128)S(1)} %collective-permute-done.4.up) | copy-start | bytes 737284
  106.5 15.8 %collective-permute-start.7 = (f32[3,80,256]{2,1,0:T(8,128)S(1)}, f32[3,80,256]{2,1,0:T(8,128)S(1)}, u32[]{:S(2)}, u32[]{:S(2)}) collective-permute-start(f32[3,80,256]{2,1,0:T(8,128)S(1)} %pad_maximum_fusion.1), channel_id=1, source_target_pairs={{1,0},{2,1},{3,2},{4,3},{5,4},{6,5},{7,6},{8,7},{9,8},{10,9},{11,1... | collective-permute-start | bytes 737288 | tf_op jit(solution)/shard_map/ppermute | solution.py:409
  107.8 14.5 %collective-permute-start.6 = (f32[3,80,256]{2,1,0:T(8,128)S(1)}, f32[3,80,256]{2,1,0:T(8,128)S(1)}, u32[]{:S(2)}, u32[]{:S(2)}) collective-permute-start(f32[3,80,256]{2,1,0:T(8,128)S(1)} %pad_maximum_fusion), channel_id=1, source_target_pairs={{0,1},{1,2},{2,3},{3,4},{4,5},{5,6},{6,7},{7,8},{8,9},{9,10},{10,1... | collective-permute-start | bytes 737288 | tf_op jit(solution)/shard_map/ppermute | solution.py:409
  122.3 0.7 copy-start.7
  123.0 0.7 copy-start.8
where the time goes:
time: 241 us; the launch traced here: 240 us
  Pallas kernels  125 us (52%)
  blocking collectives  60 us (25%)
  starting transfers between devices  27.6 us (11%)
  waiting for transfers between devices  13.6 us (6%)
  local copies, waits for them, and re-layouts  13.4 us (6%)
    pallas_call x6, Pallas kernels, call(): pl.pallas_call(kernel, name=name, out_shape=[jax.ShapeDtypeStruct(shape,...  125 us
    all_gather x5, blocking collectives, summed_over(): line = lax.all_gather(jnp.sum(line, axis=0), axis, axis_index_groups=groups)  60 us
    ppermute x8, starting transfers between devices, from_behind(): return lax.ppermute(block, axis, route)  27.6 us
    ppermute x8, waiting for transfers between devices, from_behind(): return lax.ppermute(block, axis, route)  13.6 us
    unnamed x30, local copies, waits for them, and re-layouts  10.1 us
  transfers between devices with their start and end apart: 8, of which 5 were waited for; matrix products, arithmetic and copies ran while one was open for 2% of the time, Pallas kernels for 2%

commit v1 on v0

v1 whole, which is shorter than its diff:
```python
import functools

import jax
import jax.numpy as jnp
from jax import lax
from jax.experimental import pallas as pl
from jax.experimental.pallas import tpu as pltpu
from jax.sharding import PartitionSpec as P

F32 = jnp.float32
BF16 = jnp.bfloat16
HALF = 40
ROWS = 2 * HALF
LANES = 128
PAD = 8
DIRS = 8
UNROLL = 128
MIB = 1 << 20


def split(values):
    high = values.astype(BF16)
    return high, (values - high.astype(F32)).astype(BF16)


def dot(left, right, left_dim=1, right_dim=0):
    return lax.dot_general(
        left, right, (((left_dim,), (right_dim,)), ((), ())), preferred_element_type=F32
    )


def half_rolled(block, height):
    wide = jnp.concatenate(
        [block, jnp.zeros((height, LANES - block.shape[1]), F32)], axis=1
    )
    return wide, pltpu.roll(wide, HALF, 1)


def gather_rows(count, indices, source, target):
    def some(step, carry):
        first = step * UNROLL
        for extra in range(UNROLL):
            row = indices[first + extra]
            target[pl.ds(first + extra, 1), :] = source[pl.ds(row + PAD, 1), :]
        return carry

    lax.fori_loop(0, count // UNROLL, some, 0)


def begin(source, target, semaphore):
    copy = pltpu.make_async_copy(source, target, semaphore)
    copy.start()
    return copy


def parcel_of(rows):
    return rows.T[:ROWS]


def rows_of(parcel):
    halo = parcel.shape[1]
    return jnp.concatenate([parcel, jnp.zeros((LANES - ROWS, halo), F32)], axis=0).T


def scaled_volume(vol, flag, stretch, scaled):
    nv = vol.shape[1]
    tilt = flag[...].astype(F32) * stretch[...]
    real, imag = vol[0], vol[1]
    fill = jnp.zeros((LANES - nv, vol.shape[2]), F32)
    scaled[0:nv, :] = real - tilt * imag
    scaled[nv:LANES, :] = fill
    scaled[LANES : LANES + nv, :] = imag + tilt * real
    scaled[LANES + nv : 2 * LANES, :] = fill


def place_parcels(picked, halo, lower, middle, upper):
    for direction in range(DIRS):
        parcel = parcel_of(picked[direction * halo : (direction + 1) * halo, :])
        if direction < 3:
            lower[direction] = parcel
        elif direction < 5:
            middle[direction - 3] = parcel
        else:
            upper[direction - 5] = parcel


def traces_kernel(
    trace, halo_list, table, up, mid, down, rows, turned, picked, done
):
    nq, faces = trace.shape[1], trace.shape[2]
    halo = up.shape[2]
    turned[...] = jnp.zeros_like(turned)
    turned[0:nq, :] = trace[0]
    turned[HALF : HALF + nq, :] = trace[1]
    rows[0:PAD, :] = jnp.zeros((PAD, LANES), F32)
    for first in range(0, faces, LANES):
        rows[PAD + first : PAD + first + LANES, :] = turned[:, first : first + LANES].T
    table_copy = begin(rows, table, done.at[0])
    gather_rows(DIRS * halo, halo_list, rows, picked)
    place_parcels(picked, halo, down, mid, up)
    table_copy.wait()


def sources_kernel(
    vol, flag, stretch, cond_op, elem_face,
    own_sum, up, mid, down,
    own, scaled, matrix, matrix_hi, matrix_lo, parts, sums0, sums1, sums2, sums3, ghosts, done,
):
    faces = own.shape[0]
    halo = up.shape[2]
    nq = cond_op.shape[2]
    nv, elems = vol.shape[1], vol.shape[2]
    scaled_volume(vol, flag, stretch, scaled)
    matrix[...] = jnp.zeros_like(matrix)
    for corner in range(4):
        low = corner * LANES
        matrix[low : low + nq, 0:nv] = cond_op[corner, 0]
        matrix[low : low + nq, LANES : LANES + nv] = -cond_op[corner, 1]
        matrix[low + HALF : low + HALF + nq, 0:nv] = cond_op[corner, 1]
        matrix[low + HALF : low + HALF + nq, LANES : LANES + nv] = cond_op[corner, 0]
    high, rest = split(matrix[...])
    matrix_hi[...] = high
    matrix_lo[...] = rest
    for first in range(0, elems, LANES):
        stop = first + LANES
        columns = jnp.concatenate(
            [scaled[0:LANES, first:stop].T, scaled[LANES : 2 * LANES, first:stop].T], axis=1
        )
        high, rest = split(columns)
        product = (
            dot(high, matrix_hi[...], 1, 1)
            + dot(rest, matrix_hi[...], 1, 1)
            + dot(high, matrix_lo[...], 1, 1)
        )
        for corner in range(4):
            parts[corner, first:stop, :] = product[:, corner * LANES : (corner + 1) * LANES]
    sums = (sums0, sums1, sums2, sums3)
    for total in sums:
        total[...] = jnp.zeros_like(total)

    def add_some(step, carry):
        for extra in range(4):
            elem = step * 4 + extra
            for corner in range(4):
                slot = elem_face[corner * elems + elem]
                total = sums[corner]
                total[pl.ds(slot, 1), :] = (
                    total[pl.ds(slot, 1), :] + parts[corner, pl.ds(elem, 1), :]
                )
        return carry

    lax.fori_loop(0, elems // 4, add_some, 0)

    def summed(first, size):
        stop = first + size
        return (sums0[first:stop] + sums1[first:stop]) + (sums2[first:stop] + sums3[first:stop])

    own[...] = summed(0, faces)
    own_copy = begin(own, own_sum, done.at[0])
    ghosts[...] = summed(faces, DIRS * halo)
    place_parcels(ghosts, halo, up, mid, down)
    own_copy.wait()


def skeleton_matrix(skel_op, matrix):
    nq = skel_op.shape[2]
    for block in range(skel_op.shape[0]):
        real, real_moved = half_rolled(skel_op[block, 0], nq)
        imag, imag_moved = half_rolled(skel_op[block, 1], nq)
        fill = jnp.zeros((HALF - nq, LANES), F32)
        whole = jnp.concatenate([real - imag_moved, fill, imag + real_moved, fill], axis=0)
        high, rest = split(whole)
        low = block * 2 * ROWS
        matrix[low : low + 2 * ROWS, :] = jnp.concatenate(
            [
                jnp.concatenate([high, high], axis=1),
                jnp.concatenate([rest, jnp.zeros_like(rest)], axis=1),
            ],
            axis=0,
        )


def skeleton_tile(matrix, block_coef, source_of, first, size):
    real_sum = jnp.zeros((HALF, size), F32)
    imag_sum = jnp.zeros((HALF, size), F32)
    for block in range(block_coef.shape[0]):
        high, rest = split(source_of(block, first, size))
        low = block * 2 * ROWS
        product = dot(
            matrix[low : low + 2 * ROWS, :], jnp.concatenate([high, rest], axis=1), 1, 1
        )
        real = product[0:HALF] + product[ROWS : ROWS + HALF]
        imag = product[HALF:ROWS] + product[ROWS + HALF : 2 * ROWS]
        coef_real = block_coef[block, 0:1, pl.ds(first, size)]
        coef_imag = block_coef[block, 1:2, pl.ds(first, size)]
        real_sum = real_sum + (coef_real * real - coef_imag * imag)
        imag_sum = imag_sum + (coef_real * imag + coef_imag * real)
    return real_sum, imag_sum


def join_kernel(up, mid, down, right, left, done):
    moves = [(down, 2, right, 0), (mid, 1, right, 1), (up, 2, right, 2)]
    moves += [(down, 0, left, 0), (mid, 0, left, 1), (up, 0, left, 2)]
    copies = [
        begin(source.at[place], target.at[to], done.at[number])
        for number, (source, place, target, to) in enumerate(moves)
    ]
    for copy in copies:
        copy.wait()


def ghost_places(up, down, right, left):
    return (
        left.at[0], down.at[1], right.at[0], left.at[1],
        right.at[1], left.at[2], up.at[1], right.at[2],
    )


def apply_kernel(
    table, own_sum, up, down, right, left, skel_op, block_coef, adjacency,
    slots_out, rest_out,
    slots, own, rest, arrived, picked, matrix, done,
):
    faces = own.shape[0]
    halo = arrived.shape[2]
    table_copy = begin(table, slots.at[pl.ds(0, PAD + faces)], done.at[0])
    copies = [
        begin(place, arrived.at[direction], done.at[3 + direction])
        for direction, place in enumerate(ghost_places(up, down, right, left))
    ]
    own_copy = begin(own_sum, own, done.at[1])
    skeleton_matrix(skel_op, matrix)
    for direction in range(DIRS):
        copies[direction].wait()
        first = PAD + faces + direction * halo
        slots[first : first + halo, :] = rows_of(arrived[direction])
    table_copy.wait()
    slots_copy = begin(slots, slots_out, done.at[2])
    gather_rows(adjacency.shape[0], adjacency, slots, picked)
    own_copy.wait()
    tile = 256

    def source_of(block, first, size):
        if block == 0:
            return slots[pl.ds(PAD + first, size), :]
        return picked[pl.ds((block - 1) * faces + first, size), :]

    def some(step, carry):
        first = pl.multiple_of(step * tile, tile)
        real, imag = skeleton_tile(matrix, block_coef, source_of, first, tile)
        applied = rows_of(jnp.concatenate([real, imag], axis=0))
        rest[pl.ds(first, tile), :] = own[pl.ds(first, tile), :] - applied
        return carry

    lax.fori_loop(0, faces // tile, some, 0)
    begin(rest, rest_out, done.at[0]).wait()
    slots_copy.wait()


def residual_kernel(
    rest, up, down, right, left, halo_list,
    rest_table, res_up, res_mid, res_down,
    returned, picked, back, sums0, sums1, sums2, sums3, done,
):
    faces = rest.shape[0]
    halo = returned.shape[2]
    rest_copy = begin(rest, sums0.at[pl.ds(PAD, faces)], done.at[0])
    places = (
        left.at[2], up.at[1], right.at[2], left.at[1],
        right.at[1], left.at[0], down.at[1], right.at[0],
    )
    copies = [
        begin(place, returned.at[direction], done.at[1 + direction])
        for direction, place in enumerate(places)
    ]
    sums0[0:PAD, :] = jnp.zeros((PAD, LANES), F32)
    others = (sums1, sums2, sums3)
    for total in others:
        total[...] = jnp.zeros_like(total)
    for direction in range(DIRS):
        copies[direction].wait()
        back[direction] = rows_of(returned[direction])
    rest_copy.wait()
    sums = (sums0,) + others

    def add_some(step, carry):
        for extra in range(2):
            entry = step * 2 + extra
            for direction in range(DIRS):
                face = halo_list[direction * halo + entry] + PAD
                total = sums[direction % 4]
                total[pl.ds(face, 1), :] = (
                    total[pl.ds(face, 1), :] + back[direction, pl.ds(entry, 1), :]
                )
        return carry

    lax.fori_loop(0, halo // 2, add_some, 0)
    rest_table[...] = (sums0[...] + sums1[...]) + (sums2[...] + sums3[...])
    rest_table[0:PAD, :] = jnp.zeros((PAD, LANES), F32)
    gather_rows(DIRS * halo, halo_list, rest_table, picked)
    place_parcels(picked, halo, res_down, res_mid, res_up)


def turn_kernel(rest_table, turned):
    for first in range(0, turned.shape[1], LANES):
        turned[:, first : first + LANES] = parcel_of(
            rest_table[PAD + first : PAD + first + LANES, :]
        )


def lift_matrix(lift_op, matrix):
    nv = lift_op.shape[2]
    for corner in range(4):
        real, real_moved = half_rolled(lift_op[corner, 0], nv)
        imag, imag_moved = half_rolled(lift_op[corner, 1], nv)
        fill = jnp.zeros((LANES - nv, LANES), F32)
        high, rest = split(
            jnp.concatenate([real - imag_moved, fill, imag + real_moved, fill], axis=0)
        )
        low = corner * 4 * LANES
        matrix[low : low + 4 * LANES, :] = jnp.concatenate(
            [
                jnp.concatenate([high, high], axis=1),
                jnp.concatenate([rest, jnp.zeros_like(rest)], axis=1),
            ],
            axis=0,
        )


def lifted_tile(matrix, picked, elems, first, size):
    total = jnp.zeros((2 * LANES, size), F32)
    for corner in range(4):
        low = corner * elems + first
        high, rest = split(picked[low : low + size, :])
        at = corner * 4 * LANES
        product = dot(
            matrix[at : at + 4 * LANES, :], jnp.concatenate([high, rest], axis=1), 1, 1
        )
        total = total + (product[0 : 2 * LANES] + product[2 * LANES : 4 * LANES])
    return total


def base_kernel(
    slots_in, vol, flag, stretch, recon_op, lift_op, elem_face,
    base,
    slots, picked, scaled, recon, matrix, done,
):
    nv, elems = vol.shape[1], vol.shape[2]
    slots_copy = begin(slots_in, slots, done.at[0])
    lift_matrix(lift_op, matrix)
    scaled_volume(vol, flag, stretch, scaled)
    recon[...] = jnp.zeros_like(recon)
    recon[0:nv, 0:nv] = recon_op[0]
    recon[0:nv, LANES : LANES + nv] = -recon_op[1]
    recon[LANES : LANES + nv, 0:nv] = recon_op[1]
    recon[LANES : LANES + nv, LANES : LANES + nv] = recon_op[0]
    recon_high, recon_rest = split(recon[...])
    slots_copy.wait()
    gather_rows(4 * elems, elem_face, slots, picked)
    size = 256
    for first in range(0, elems, size):
        stop = first + size
        wanted, fine = split(scaled[:, first:stop])
        product = dot(recon_high, wanted) + dot(recon_high, fine) + dot(recon_rest, wanted)
        product = product - lifted_tile(matrix, picked, elems, first, size)
        base[0, :, first:stop] = product[0:nv]
        base[1, :, first:stop] = product[LANES : LANES + nv]


def lift_kernel(slots_in, lift_op, elem_face, lifted, slots, picked, matrix, done):
    nv, elems = lifted.shape[1], lifted.shape[2]
    slots_copy = begin(slots_in, slots, done.at[0])
    lift_matrix(lift_op, matrix)
    slots_copy.wait()
    gather_rows(4 * elems, elem_face, slots, picked)
    size = 256
    for first in range(0, elems, size):
        stop = first + size
        product = lifted_tile(matrix, picked, elems, first, size)
        lifted[0, :, first:stop] = product[0:nv]
        lifted[1, :, first:stop] = product[LANES : LANES + nv]


def image_kernel(
    rest_table, turned, up, down, right, left, skel_op, block_coef, adjacency,
    slots_out, partial,
    slots, arrived, picked, matrix, done,
):
    faces = turned.shape[1]
    halo = arrived.shape[2]
    table_copy = begin(rest_table, slots.at[pl.ds(0, PAD + faces)], done.at[0])
    copies = [
        begin(place, arrived.at[direction], done.at[3 + direction])
        for direction, place in enumerate(ghost_places(up, down, right, left))
    ]
    skeleton_matrix(skel_op, matrix)
    for direction in range(DIRS):
        copies[direction].wait()
        first = PAD + faces + direction * halo
        slots[first : first + halo, :] = rows_of(arrived[direction])
    table_copy.wait()
    slots_copy = begin(slots, slots_out, done.at[2])
    gather_rows(adjacency.shape[0], adjacency, slots, picked)
    tile = 256

    def source_of(block, first, size):
        if block == 0:
            return slots[pl.ds(PAD + first, size), :]
        return picked[pl.ds((block - 1) * faces + first, size), :]

    def some(step, carry):
        first = pl.multiple_of(step * tile, tile)
        real, imag = skeleton_tile(matrix, block_coef, source_of, first, tile)
        rest_real = turned[0:HALF, pl.ds(first, tile)]
        rest_imag = turned[HALF:ROWS, pl.ds(first, tile)]
        return (
            carry[0] + (real * rest_real + imag * rest_imag),
            carry[1] + (real * rest_imag - imag * rest_real),
            carry[2] + (real * real + imag * imag),
        )

    zero = jnp.zeros((HALF, tile), F32)
    totals = lax.fori_loop(0, faces // tile, some, (zero, zero, zero))
    lane = lax.broadcasted_iota(jnp.int32, (1, LANES), 1)
    line = jnp.zeros((1, LANES), F32)
    for place in range(3):
        line = line + jnp.where(lane == place, jnp.sum(totals[place]), 0.0)
    partial[...] = jnp.broadcast_to(line, partial.shape)
    slots_copy.wait()


def finish_kernel(gathered, trace, turned, base, lifted, trace_out, volume_out):
    nq = trace.shape[1]
    line = jnp.sum(gathered[...], axis=0, keepdims=True)
    lane = lax.broadcasted_iota(jnp.int32, (1, LANES), 1)
    entry = [
        jnp.sum(jnp.where(lane == place, line, 0.0), axis=1, keepdims=True)
        for place in range(3)
    ]
    step_real = entry[0] / entry[2]
    step_imag = entry[1] / entry[2]
    volume_out[0] = base[0] - (step_real * lifted[0] - step_imag * lifted[1])
    volume_out[1] = base[1] - (step_real * lifted[1] + step_imag * lifted[0])
    rest_real = turned[0:nq, :]
    rest_imag = turned[HALF : HALF + nq, :]
    trace_out[0] = trace[0] + (step_real * rest_real - step_imag * rest_imag)
    trace_out[1] = trace[1] + (step_real * rest_imag + step_imag * rest_real)


SPACES = {
    "v": pltpu.MemorySpace.VMEM,
    "s": pltpu.MemorySpace.SMEM,
    "a": pl.ANY,
    "h": pltpu.HBM,
    "V": pltpu.MemorySpace.VMEM,
}


def call(kernel, name, args, out_shapes, spaces, scratch, limit, semaphores=0, time=1):
    specs = [pl.BlockSpec(memory_space=SPACES[letter]) for letter in spaces]
    shapes = [pltpu.VMEM(shape, kind) for shape, kind in scratch]
    if semaphores:
        shapes.append(pltpu.SemaphoreType.DMA((semaphores,)))
    args = [
        pltpu.with_memory_space_constraint(arg, pltpu.HBM) if letter in "hV" else arg
        for arg, letter in zip(args, spaces)
    ]
    return pl.pallas_call(
        kernel,
        name=name,
        out_shape=[
            pltpu.HBM(shape, F32) if letter in "hV" else jax.ShapeDtypeStruct(shape, F32)
            for shape, letter in zip(out_shapes, spaces[len(args) :])
        ],
        in_specs=specs[: len(args)],
        out_specs=specs[len(args) :],
        scratch_shapes=shapes,
        compiler_params=pltpu.CompilerParams(vmem_limit_bytes=limit * MIB),
        cost_estimate=pl.CostEstimate(
            flops=0, bytes_accessed=3300000 * time, transcendentals=0
        ),
    )(*args)


def from_behind(block, axis, distance):
    devices = range(lax.axis_size(axis))
    route = [(i - distance, i) for i in devices if i - distance in devices]
    return lax.ppermute(block, axis, route)


def everywhere(lines, axis):
    return lax.all_to_all(lines, axis, 0, 0)


def local(
    vol_rhs, trace_in, pml_flag, stretch, cond_op, skel_op, block_coef, recon_op, lift_op,
    elem_face, adjacency, halo_list,
):
    nv, elems = vol_rhs.shape[1], vol_rhs.shape[2]
    faces = trace_in.shape[2]
    halo = halo_list.shape[1]
    blocks = skel_op.shape[0]
    neighbours = adjacency.shape[0]
    slots = faces + DIRS * halo
    elem_face = elem_face.reshape(-1)
    adjacency = adjacency.reshape(-1)
    halo_list = halo_list.reshape(-1)
    flag = pml_flag.reshape(1, elems)
    tilt = stretch.reshape(1, elems)
    parcels = [(3, ROWS, halo), (2, ROWS, halo), (3, ROWS, halo)]

    def exchange(up, mid, down, sign, beside=None):
        up = from_behind(up, "gx", 1)
        down = from_behind(down, "gx", -1)
        if beside is not None:
            up, down, beside = lax.optimization_barrier((up, down, beside))
        right, left = call(
            join_kernel, "join", (up, mid, down), [up.shape, up.shape], "aaa" + "vv", [], 2, 6
        )
        right = from_behind(right, "gy", sign)
        left = from_behind(left, "gy", -sign)
        return (up, down, right, left) if beside is None else (up, down, right, left, beside)

    table, *outgoing = call(
        traces_kernel,
        "traces",
        (trace_in, halo_list),
        [(PAD + faces, LANES)] + parcels,
        "vs" + "hvvv",
        [((PAD + faces, LANES), F32), ((LANES, faces), F32), ((DIRS * halo, LANES), F32)],
        8,
        1,
        4,
    )
    arrived = exchange(*outgoing, 1)
    own_sum, *outgoing = call(
        sources_kernel,
        "sources",
        (vol_rhs, flag, tilt, cond_op, elem_face),
        [(faces, LANES)] + parcels,
        "VVVVs" + "hvvv",
        [
            ((faces, LANES), F32),
            ((2 * LANES, elems), F32),
            ((4 * LANES, 2 * LANES), F32),
            ((4 * LANES, 2 * LANES), BF16),
            ((4 * LANES, 2 * LANES), BF16),
            ((4, elems, LANES), F32),
        ]
        + [((slots, LANES), F32)] * 4
        + [((DIRS * halo, LANES), F32)],
        22,
        1,
        9,
    )
    returned = exchange(*outgoing, -1)
    slots_trace, rest = call(
        apply_kernel,
        "apply",
        (table, own_sum, *arrived, skel_op, block_coef, adjacency),
        [(PAD + slots, LANES), (faces, LANES)],
        "hhaaaaVVs" + "hh",
        [
            ((PAD + slots, LANES), F32),
            ((faces, LANES), F32),
            ((faces, LANES), F32),
            ((DIRS, ROWS, halo), F32),
            ((neighbours * faces, LANES), F32),
            ((blocks * 2 * ROWS, 2 * LANES), BF16),
        ],
        20,
        3 + DIRS,
        18,
    )
    rest_table, *outgoing = call(
        residual_kernel,
        "residual",
        (rest, *returned, halo_list),
        [(PAD + faces, LANES)] + parcels,
        "haaaas" + "Vvvv",
        [
            ((DIRS, ROWS, halo), F32),
            ((DIRS * halo, LANES), F32),
            ((DIRS, halo, LANES), F32),
        ]
        + [((PAD + faces, LANES), F32)] * 4,
        12,
        1 + DIRS,
        8,
    )
    (base,) = call(
        base_kernel,
        "base",
        (slots_trace, vol_rhs, flag, tilt, recon_op, lift_op, elem_face),
        [vol_rhs.shape],
        "hVVVVVs" + "V",
        [
            ((PAD + slots, LANES), F32),
            ((4 * elems, LANES), F32),
            ((2 * LANES, elems), F32),
            ((2 * LANES, 2 * LANES), F32),
            ((4 * 4 * LANES, 2 * LANES), BF16),
        ],
        14,
        1,
        8,
    )
    *arrived, base = exchange(*outgoing, 1, base)
    (turned,) = call(
        turn_kernel, "turn", (rest_table,), [(ROWS, faces)], "VV", [], 4
    )
    across, along = lax.axis_size("gx"), lax.axis_size("gy")
    slots_rest, partial = call(
        image_kernel,
        "image",
        (rest_table, turned, *arrived, skel_op, block_coef, adjacency),
        [(PAD + slots, LANES), (along, LANES)],
        "hVaaaaVVs" + "hv",
        [
            ((PAD + slots, LANES), F32),
            ((DIRS, ROWS, halo), F32),
            ((neighbours * faces, LANES), F32),
            ((blocks * 2 * ROWS, 2 * LANES), BF16),
        ],
        20,
        3 + DIRS,
        18,
    )
    (lifted,) = call(
        lift_kernel,
        "lift",
        (slots_rest, lift_op, elem_face),
        [vol_rhs.shape],
        "hVs" + "V",
        [
            ((PAD + slots, LANES), F32),
            ((4 * elems, LANES), F32),
            ((4 * 4 * LANES, 2 * LANES), BF16),
        ],
        12,
        1,
        7,
    )
    lines, lifted = lax.optimization_barrier((everywhere(partial, "gy"), lifted))
    lines = jnp.sum(lines, axis=0, keepdims=True)
    gathered = everywhere(jnp.broadcast_to(lines, (across, LANES)), "gx")
    trace_out, volume_out = call(
        finish_kernel,
        "finish",
        (gathered, trace_in, turned, base, lifted),
        [trace_in.shape, vol_rhs.shape],
        "vVVVV" + "vV",
        [],
        8,
    )
    return trace_out, volume_out


def solution(mesh):
    split_last = ("gx", "gy")
    in_specs = (
        P(None, None, split_last),
        P(None, None, split_last),
        P(split_last),
        P(split_last),
        P(),
        P(),
        P(None, None, split_last),
        P(),
        P(),
        P(None, split_last),
        P(None, split_last),
        P(None, split_last),
    )
    out_specs = (P(None, None, split_last), P(None, None, split_last))
    return jax.shard_map(
        local, mesh=mesh, in_specs=in_specs, out_specs=out_specs, check_vma=False
    )
```

time: 241 us -> 170 us (0.71)
  the two profiles are of different devices: /device:TPU:8 before, /device:TPU:1 now
where the time goes in v1:
time: 170 us; the launch traced here: 169 us
  Pallas kernels  86.4 us (51%)
  starting transfers between devices  49.8 us (29%)
  blocking collectives  17.6 us (10%)
  local copies, waits for them, and re-layouts  7.62 us (4%)
  waiting for transfers between devices  6.44 us (4%)
    pallas_call x12, Pallas kernels, call(): pl.pallas_call(kernel, name=name, out_shape=[pltpu.HBM(shape, F32) if let...  86.4 us
    ppermute x12, starting transfers between devices, from_behind(): return lax.ppermute(block, axis, route)  33.8 us
    all_to_all x1, blocking collectives, everywhere(): return lax.all_to_all(lines, axis, 0, 0)  17.6 us
    all_to_all x1, starting transfers between devices, everywhere(): return lax.all_to_all(lines, axis, 0, 0)  16 us
    unnamed x14, local copies, waits for them, and re-layouts  6.33 us
    all_to_all x1, waiting for transfers between devices, everywhere(): return lax.all_to_all(lines, axis, 0, 0)  3.47 us
  transfers between devices with their start and end apart: 13, of which 2 were waited for; matrix products, arithmetic and copies ran while one was open for 2% of the time, Pallas kernels for 31%

profile of v1, /device:TPU:1, one launch (start us, length us, event | category | flops | bytes accessed | tf_op | source)
XLA Modules:
  0.0 168.8 jit_solution(4669319491851307266)
XLA Ops:
  0.6 1.4 copy.22.trace
  2.9 3.0 %traces.1 = (f32[2056,128]{1,0:T(8,128)}, f32[3,80,256]{2,1,0:T(8,128)S(1)}, f32[2,80,256]{2,1,0:T(8,128)S(1)}, f32[3,80,256]{2,1,0:T(8,128)S(1)}) custom-call(f32[2,36,2048]{2,1,0:T(8,128)S(1)} %copy.22.trace, s32[2048]{0:T(1024)S(1)} %bitcast.16), custom_call_target="tpu_custom_call" | custom-call | bytes 13200000 | tf_op jit(solution)/shard_map/traces/pallas_call | solution.py:468
  6.0 4.0 %collective-permute-start = (f32[3,80,256]{2,1,0:T(8,128)S(1)}, f32[3,80,256]{2,1,0:T(8,128)S(1)}, u32[]{:S(2)}, u32[]{:S(2)}) collective-permute-start(f32[3,80,256]{2,1,0:T(8,128)S(1)} %get-tuple-element.31), channel_id=1, source_target_pairs={{0,32},{32,64},{64,96},{96,128},{128,160},{160,192},{192,224},{224... | collective-permute-start | bytes 737288 | tf_op jit(solution)/shard_map/ppermute | solution.py:488
  12.0 1.6 copy.23.cond_op
  13.6 11.7 %sources.1 = (f32[2048,128]{1,0:T(8,128)}, f32[3,80,256]{2,1,0:T(8,128)S(1)}, f32[2,80,256]{2,1,0:T(8,128)S(1)}, f32[3,80,256]{2,1,0:T(8,128)S(1)}) custom-call(f32[2,120,1024]{2,1,0:T(8,128)} %vol.3, s32[1,1024]{1,0:T(1,128)} %bitcast.21, f32[1,1024]{1,0:T(1,128)} %bitcast.23, f32[4,2,36,120]{3,2,1,0:T(8,128)} %copy.23.cond_op, s32[4096]{0:T(1024)S(1)} %bitcast.13), custom_call_target="tpu_custom_call" | custom-call | bytes 29700000 | tf_op jit(solution)/shard_map/sources/pallas_call | solution.py:468
  25.3 4.0 %collective-permute-start.4 = (f32[3,80,256]{2,1,0:T(8,128)S(1)}, f32[3,80,256]{2,1,0:T(8,128)S(1)}, u32[]{:S(2)}, u32[]{:S(2)}) collective-permute-start(f32[3,80,256]{2,1,0:T(8,128)S(1)} %get-tuple-element.37), channel_id=1, source_target_pairs={{0,32},{32,64},{64,96},{96,128},{128,160},{160,192},{192,224},{224... | collective-permute-start | bytes 737288 | tf_op jit(solution)/shard_map/ppermute | solution.py:488
  31.3 4.9 %collective-permute-start.2 = (f32[3,80,256]{2,1,0:T(8,128)S(1)}, f32[3,80,256]{2,1,0:T(8,128)S(1)}, u32[]{:S(2)}, u32[]{:S(2)}) collective-permute-start(f32[3,80,256]{2,1,0:T(8,128)S(1)} %get-tuple-element.34), channel_id=1, source_target_pairs={{0,1},{1,2},{2,3},{3,4},{4,5},{5,6},{6,7},{7,8},{8,9},{9,10},{10,1... | collective-permute-start | bytes 737288 | tf_op jit(solution)/shard_map/ppermute | solution.py:488
  36.3 3.0 %collective-permute-start.3 = (f32[3,80,256]{2,1,0:T(8,128)S(1)}, f32[3,80,256]{2,1,0:T(8,128)S(1)}, u32[]{:S(2)}, u32[]{:S(2)}) collective-permute-start(f32[3,80,256]{2,1,0:T(8,128)S(1)} %get-tuple-element.35), channel_id=1, source_target_pairs={{1,0},{2,1},{3,2},{4,3},{5,4},{6,5},{7,6},{8,7},{9,8},{10,9},{11,1... | collective-permute-start | bytes 737288 | tf_op jit(solution)/shard_map/ppermute | solution.py:488
  40.7 4.7 %collective-permute-start.6 = (f32[3,80,256]{2,1,0:T(8,128)}, f32[3,80,256]{2,1,0:T(8,128)S(1)}, u32[]{:S(2)}, u32[]{:S(2)}) collective-permute-start(f32[3,80,256]{2,1,0:T(8,128)} %get-tuple-element.40), channel_id=1, source_target_pairs={{1,0},{2,1},{3,2},{4,3},{5,4},{6,5},{7,6},{8,7},{9,8},{10,9},{11,1... | collective-permute-start | bytes 737288 | tf_op jit(solution)/shard_map/ppermute | solution.py:488
  45.4 1.9 %collective-permute-start.7 = (f32[3,80,256]{2,1,0:T(8,128)S(1)}, f32[3,80,256]{2,1,0:T(8,128)S(1)}, u32[]{:S(2)}, u32[]{:S(2)}) collective-permute-start(f32[3,80,256]{2,1,0:T(8,128)S(1)} %get-tuple-element.41), channel_id=1, source_target_pairs={{0,1},{1,2},{2,3},{3,4},{4,5},{5,6},{6,7},{7,8},{8,9},{9,10},{10,1... | collective-permute-start | bytes 737288 | tf_op jit(solution)/shard_map/ppermute | solution.py:488
  48.1 19.0 %apply.1 = (f32[4104,128]{1,0:T(8,128)}, f32[2048,128]{1,0:T(8,128)}) custom-call(f32[2056,128]{1,0:T(8,128)} %get-tuple-element.29.table, f32[2048,128]{1,0:T(8,128)} %get-tuple-element.30.own_sum, f32[3,80,256]{2,1,0:T(8,128)S(1)} %collective-permute-done.up, f32[3,80,256]{2,1,0:T(8,128)S(1)} %collective-permute-done.1.down, ...), custom_call_target="tpu_custom_call" | custom-call | bytes 59400000 | tf_op jit(solution)/shard_map/apply/pallas_call | solution.py:468
  67.1 8.8 %residual.1 = (f32[2056,128]{1,0:T(8,128)}, f32[3,80,256]{2,1,0:T(8,128)S(1)}, f32[2,80,256]{2,1,0:T(8,128)S(1)}, f32[3,80,256]{2,1,0:T(8,128)S(1)}) custom-call(f32[2048,128]{1,0:T(8,128)} %get-tuple-element.36.rest, f32[3,80,256]{2,1,0:T(8,128)S(1)} %collective-permute-done.4.up, f32[3,80,256]{2,1,0:T(8,128)S(1)} %collective-permute-done.5.down, ...), custom_call_target="tpu_custom_call" | custom-call | bytes 26400000 | tf_op jit(solution)/shard_map/residual/pallas_call | solution.py:468
  75.9 3.1 %collective-permute-start.8 = (f32[3,80,256]{2,1,0:T(8,128)S(1)}, f32[3,80,256]{2,1,0:T(8,128)S(1)}, u32[]{:S(2)}, u32[]{:S(2)}) collective-permute-start(f32[3,80,256]{2,1,0:T(8,128)S(1)} %get-tuple-element.43), channel_id=1, source_target_pairs={{0,32},{32,64},{64,96},{96,128},{128,160},{160,192},{192,224},{224... | collective-permute-start | bytes 737288 | tf_op jit(solution)/shard_map/ppermute | solution.py:488
  81.3 9.0 %base.1 = f32[2,120,1024]{2,1,0:T(8,128)} custom-call(f32[4104,128]{1,0:T(8,128)} %get-tuple-element.45.slots_in, f32[2,120,1024]{2,1,0:T(8,128)} %vol.3, s32[1,1024]{1,0:T(1,128)} %bitcast.22, f32[1,1024]{1,0:T(1,128)} %bitcast.24, f32[2,120,120]{2,1,0:T(8,128)} %recon_op.1, f32[4,2,120,36]{3,2,1,0:T(8,128)} %copy.25.lift_op, s32[4096]{0:T(1024)S(1)} %bitcast.14), custom_call_target="tpu_custom_call" | custom-call | bytes 26400000 | tf_op jit(solution)/shard_map/base/pallas_call | solution.py:468
  91.1 2.2 %collective-permute-start.10 = (f32[3,80,256]{2,1,0:T(8,128)S(1)}, f32[3,80,256]{2,1,0:T(8,128)S(1)}, u32[]{:S(2)}, u32[]{:S(2)}) collective-permute-start(f32[3,80,256]{2,1,0:T(8,128)S(1)} %get-tuple-element.49), channel_id=1, source_target_pairs={{0,1},{1,2},{2,3},{3,4},{4,5},{5,6},{6,7},{7,8},{8,9},{9,10},{10,1... | collective-permute-start | bytes 737288 | tf_op jit(solution)/shard_map/ppermute | solution.py:488
  93.3 2.1 %collective-permute-start.11 = (f32[3,80,256]{2,1,0:T(8,128)S(1)}, f32[3,80,256]{2,1,0:T(8,128)S(1)}, u32[]{:S(2)}, u32[]{:S(2)}) collective-permute-start(f32[3,80,256]{2,1,0:T(8,128)S(1)} %get-tuple-element.50), channel_id=1, source_target_pairs={{1,0},{2,1},{3,2},{4,3},{5,4},{6,5},{7,6},{8,7},{9,8},{10,9},{11,1... | collective-permute-start | bytes 737288 | tf_op jit(solution)/shard_map/ppermute | solution.py:488
  95.5 2.4 %turn.1.turned = f32[80,2048]{1,0:T(8,128)} custom-call(f32[2056,128]{1,0:T(8,128)} %get-tuple-element.42.rest_table), custom_call_target="tpu_custom_call" | custom-call | bytes 3300000 | tf_op jit(solution)/shard_map/turn/pallas_call | solution.py:468
  97.9 2.9 %collective-permute-done.11.left = f32[3,80,256]{2,1,0:T(8,128)S(1)} collective-permute-done((f32[3,80,256]{2,1,0:T(8,128)S(1)}, f32[3,80,256]{2,1,0:T(8,128)S(1)}, u32[]{:S(2)}, u32[]{:S(2)}) %collective-permute-start.11) | collective-permute-done | bytes 245792 | tf_op jit(solution)/shard_map/ppermute | solution.py:488
  100.8 18.2 %image.1 = (f32[4104,128]{1,0:T(8,128)}, f32[32,128]{1,0:T(8,128)}) custom-call(f32[2056,128]{1,0:T(8,128)} %get-tuple-element.42.rest_table, f32[80,2048]{1,0:T(8,128)} %turn.1.turned, f32[3,80,256]{2,1,0:T(8,128)S(1)} %collective-permute-done.8.up, f32[3,80,256]{2,1,0:T(8,128)S(1)} %collective-permute-done.9.down, ...), custom_call_target="tpu_custom_call" | custom-call | bytes 59400000 | tf_op jit(solution)/shard_map/image/pallas_call | solution.py:468
  119.0 16.0 %all-to-all-start = ((f32[32,1,128]{2,1,0:T(1,128)}), f32[32,1,128]{2,1,0:T(1,128)S(1)}, u32[]{:S(2)}, u32[]{:S(2)}) async-start(f32[32,1,128]{2,1,0:T(1,128)} %bitcast.3), calls=%async_computation | async-start | bytes 32768 | tf_op jit(solution)/shard_map/all_to_all | solution.py:492
  135.0 8.3 %lift.1.lifted = f32[2,120,1024]{2,1,0:T(8,128)} custom-call(f32[4104,128]{1,0:T(8,128)} %get-tuple-element.52.slots_in, f32[4,2,120,36]{3,2,1,0:T(8,128)} %copy.25.lift_op, s32[4096]{0:T(1024)S(1)} %bitcast.15), custom_call_target="tpu_custom_call" | custom-call | bytes 23100000 | tf_op jit(solution)/shard_map/lift/pallas_call | solution.py:468
  143.3 3.5 %all-to-all-done = f32[32,1,128]{2,1,0:T(1,128)S(1)} async-done(((f32[32,1,128]{2,1,0:T(1,128)}), f32[32,1,128]{2,1,0:T(1,128)S(1)}, u32[]{:S(2)}, u32[]{:S(2)}) %all-to-all-start) | async-done | bytes 16416 | tf_op jit(solution)/shard_map/all_to_all | solution.py:492
  146.8 17.6 %all_to_all.20 = f32[16,1,128]{2,1,0:T(1,128)S(1)} all-to-all(f32[16,1,128]{2,1,0:T(1,128)S(1)} %broadcast_in_dim.2), channel_id=1, replica_groups=mesh['gx'=16,'gy'=32] {'gx'}, dimensions={0} | all-to-all | bytes 16384 | tf_op jit(solution)/shard_map/all_to_all | solution.py:492
  164.4 3.2 %finish.1 = (f32[2,36,2048]{2,1,0:T(8,128)S(1)}, f32[2,120,1024]{2,1,0:T(8,128)}) custom-call(f32[16,128]{1,0:T(8,128)S(1)} %bitcast.18, f32[2,36,2048]{2,1,0:T(8,128)} %copy-done, f32[80,2048]{1,0:T(8,128)} %turn.1.turned, f32[2,120,1024]{2,1,0:T(8,128)} %base.1, f32[2,120,1024]{2,1,0:T(8,128)} %lift.1.lifted), custom_call_target="tpu_custom_call" | custom-call | bytes 3300000 | tf_op jit(solution)/shard_map/finish/pallas_call | solution.py:468
  (33 shorter events, 11.3 us)
Async XLA Ops:
  0.6 46.7 %copy-start.1 = (f32[7,2,36,36]{3,1,2,0:T(2,128)S(1)}, f32[7,2,36,36]{3,1,2,0:T(2,128)}, u32[]{:S(2)}) copy-start(f32[7,2,36,36]{3,1,2,0:T(2,128)} %param.17) | copy-start | bytes 217732
  2.1 65.0 %copy-start = (f32[2,36,2048]{2,1,0:T(8,128)}, f32[2,36,2048]{2,1,0:T(8,128)S(1)}, u32[]{:S(2)}) copy-start(f32[2,36,2048]{2,1,0:T(8,128)S(1)} %copy.22.trace) | copy-start | bytes 1769476
  2.1 45.9 %copy-start.3 = (s32[6,2048]{1,0:T(8,128)S(1)}, s32[6,2048]{1,0:T(8,128)}, u32[]{:S(2)}) copy-start(s32[6,2048]{1,0:T(8,128)} %param.22) | copy-start | bytes 147460
  6.0 24.6 %collective-permute-start = (f32[3,80,256]{2,1,0:T(8,128)S(1)}, f32[3,80,256]{2,1,0:T(8,128)S(1)}, u32[]{:S(2)}, u32[]{:S(2)}) collective-permute-start(f32[3,80,256]{2,1,0:T(8,128)S(1)} %get-tuple-element.31), channel_id=1, source_target_pairs={{0,32},{32,64},{64,96},{96,128},{128,160},{160,192},{192,224},{224... | collective-permute-start | bytes 737288 | tf_op jit(solution)/shard_map/ppermute | solution.py:488
  10.0 20.6 %collective-permute-start.1 = (f32[3,80,256]{2,1,0:T(8,128)S(1)}, f32[3,80,256]{2,1,0:T(8,128)S(1)}, u32[]{:S(2)}, u32[]{:S(2)}) collective-permute-start(f32[3,80,256]{2,1,0:T(8,128)S(1)} %get-tuple-element.32), channel_id=1, source_target_pairs={{32,0},{64,32},{96,64},{128,96},{160,128},{192,160},{224,192},{256... | collective-permute-start | bytes 737288 | tf_op jit(solution)/shard_map/ppermute | solution.py:488
  25.3 14.0 %collective-permute-start.4 = (f32[3,80,256]{2,1,0:T(8,128)S(1)}, f32[3,80,256]{2,1,0:T(8,128)S(1)}, u32[]{:S(2)}, u32[]{:S(2)}) collective-permute-start(f32[3,80,256]{2,1,0:T(8,128)S(1)} %get-tuple-element.37), channel_id=1, source_target_pairs={{0,32},{32,64},{64,96},{96,128},{128,160},{160,192},{192,224},{224... | collective-permute-start | bytes 737288 | tf_op jit(solution)/shard_map/ppermute | solution.py:488
  29.3 10.0 %collective-permute-start.5 = (f32[3,80,256]{2,1,0:T(8,128)S(1)}, f32[3,80,256]{2,1,0:T(8,128)S(1)}, u32[]{:S(2)}, u32[]{:S(2)}) collective-permute-start(f32[3,80,256]{2,1,0:T(8,128)S(1)} %get-tuple-element.38), channel_id=1, source_target_pairs={{32,0},{64,32},{96,64},{128,96},{160,128},{192,160},{224,192},{256... | collective-permute-start | bytes 737288 | tf_op jit(solution)/shard_map/ppermute | solution.py:488
  31.3 16.7 %collective-permute-start.2 = (f32[3,80,256]{2,1,0:T(8,128)S(1)}, f32[3,80,256]{2,1,0:T(8,128)S(1)}, u32[]{:S(2)}, u32[]{:S(2)}) collective-permute-start(f32[3,80,256]{2,1,0:T(8,128)S(1)} %get-tuple-element.34), channel_id=1, source_target_pairs={{0,1},{1,2},{2,3},{3,4},{4,5},{5,6},{6,7},{7,8},{8,9},{9,10},{10,1... | collective-permute-start | bytes 737288 | tf_op jit(solution)/shard_map/ppermute | solution.py:488
  36.3 11.8 %collective-permute-start.3 = (f32[3,80,256]{2,1,0:T(8,128)S(1)}, f32[3,80,256]{2,1,0:T(8,128)S(1)}, u32[]{:S(2)}, u32[]{:S(2)}) collective-permute-start(f32[3,80,256]{2,1,0:T(8,128)S(1)} %get-tuple-element.35), channel_id=1, source_target_pairs={{1,0},{2,1},{3,2},{4,3},{5,4},{6,5},{7,6},{8,7},{9,8},{10,9},{11,1... | collective-permute-start | bytes 737288 | tf_op jit(solution)/shard_map/ppermute | solution.py:488
  40.7 26.4 %collective-permute-start.6 = (f32[3,80,256]{2,1,0:T(8,128)}, f32[3,80,256]{2,1,0:T(8,128)S(1)}, u32[]{:S(2)}, u32[]{:S(2)}) collective-permute-start(f32[3,80,256]{2,1,0:T(8,128)} %get-tuple-element.40), channel_id=1, source_target_pairs={{1,0},{2,1},{3,2},{4,3},{5,4},{6,5},{7,6},{8,7},{9,8},{10,9},{11,1... | collective-permute-start | bytes 737288 | tf_op jit(solution)/shard_map/ppermute | solution.py:488
  45.4 21.7 %collective-permute-start.7 = (f32[3,80,256]{2,1,0:T(8,128)S(1)}, f32[3,80,256]{2,1,0:T(8,128)S(1)}, u32[]{:S(2)}, u32[]{:S(2)}) collective-permute-start(f32[3,80,256]{2,1,0:T(8,128)S(1)} %get-tuple-element.41), channel_id=1, source_target_pairs={{0,1},{1,2},{2,3},{3,4},{4,5},{5,6},{6,7},{7,8},{8,9},{9,10},{10,1... | collective-permute-start | bytes 737288 | tf_op jit(solution)/shard_map/ppermute | solution.py:488
  48.1 32.2 %copy-start.2 = (f32[4,2,120,36]{2,1,3,0:T(2,128)S(1)}, f32[4,2,120,36]{2,1,3,0:T(2,128)}, u32[]{:S(2)}) copy-start(f32[4,2,120,36]{2,1,3,0:T(2,128)} %param.20) | copy-start | bytes 414724
  75.9 14.4 %collective-permute-start.8 = (f32[3,80,256]{2,1,0:T(8,128)S(1)}, f32[3,80,256]{2,1,0:T(8,128)S(1)}, u32[]{:S(2)}, u32[]{:S(2)}) collective-permute-start(f32[3,80,256]{2,1,0:T(8,128)S(1)} %get-tuple-element.43), channel_id=1, source_target_pairs={{0,32},{32,64},{64,96},{96,128},{128,160},{160,192},{192,224},{224... | collective-permute-start | bytes 737288 | tf_op jit(solution)/shard_map/ppermute | solution.py:488
  79.0 11.4 %collective-permute-start.9 = (f32[3,80,256]{2,1,0:T(8,128)S(1)}, f32[3,80,256]{2,1,0:T(8,128)S(1)}, u32[]{:S(2)}, u32[]{:S(2)}) collective-permute-start(f32[3,80,256]{2,1,0:T(8,128)S(1)} %get-tuple-element.44), channel_id=1, source_target_pairs={{32,0},{64,32},{96,64},{128,96},{160,128},{192,160},{224,192},{256... | collective-permute-start | bytes 737288 | tf_op jit(solution)/shard_map/ppermute | solution.py:488
  91.1 6.8 %collective-permute-start.10 = (f32[3,80,256]{2,1,0:T(8,128)S(1)}, f32[3,80,256]{2,1,0:T(8,128)S(1)}, u32[]{:S(2)}, u32[]{:S(2)}) collective-permute-start(f32[3,80,256]{2,1,0:T(8,128)S(1)} %get-tuple-element.49), channel_id=1, source_target_pairs={{0,1},{1,2},{2,3},{3,4},{4,5},{5,6},{6,7},{7,8},{8,9},{9,10},{10,1... | collective-permute-start | bytes 737288 | tf_op jit(solution)/shard_map/ppermute | solution.py:488
  93.3 7.5 %collective-permute-start.11 = (f32[3,80,256]{2,1,0:T(8,128)S(1)}, f32[3,80,256]{2,1,0:T(8,128)S(1)}, u32[]{:S(2)}, u32[]{:S(2)}) collective-permute-start(f32[3,80,256]{2,1,0:T(8,128)S(1)} %get-tuple-element.50), channel_id=1, source_target_pairs={{1,0},{2,1},{3,2},{4,3},{5,4},{6,5},{7,6},{8,7},{9,8},{10,9},{11,1... | collective-permute-start | bytes 737288 | tf_op jit(solution)/shard_map/ppermute | solution.py:488
  119.0 27.7 %all-to-all-start = ((f32[32,1,128]{2,1,0:T(1,128)}), f32[32,1,128]{2,1,0:T(1,128)S(1)}, u32[]{:S(2)}, u32[]{:S(2)}) async-start(f32[32,1,128]{2,1,0:T(1,128)} %bitcast.3), calls=%async_computation | async-start | bytes 32768 | tf_op jit(solution)/shard_map/all_to_all | solution.py:492

commit v2 on v1

v2 whole, which is shorter than its diff:
```python
import functools

import jax
import jax.numpy as jnp
from jax import lax
from jax.experimental import pallas as pl
from jax.experimental.pallas import tpu as pltpu
from jax.sharding import PartitionSpec as P

F32 = jnp.float32
BF16 = jnp.bfloat16
HALF = 40
ROWS = 2 * HALF
LANES = 128
PAD = 8
DIRS = 8
UNROLL = 128
TILE = 256
LIFT = 256
MIB = 1 << 20


def split(values):
    high = values.astype(BF16)
    return high, (values - high.astype(F32)).astype(BF16)


def dot(left, right, left_dim=1, right_dim=0):
    return lax.dot_general(
        left, right, (((left_dim,), (right_dim,)), ((), ())), preferred_element_type=F32
    )


def half_rolled(block, height):
    wide = jnp.concatenate(
        [block, jnp.zeros((height, LANES - block.shape[1]), F32)], axis=1
    )
    return wide, pltpu.roll(wide, HALF, 1)


def gather_rows(count, indices, source, target, start=0, base=0):
    def some(step, carry):
        first = step * UNROLL
        for extra in range(UNROLL):
            row = indices[start + first + extra]
            target[pl.ds(base + first + extra, 1), :] = source[pl.ds(row + PAD, 1), :]
        return carry

    lax.fori_loop(0, count // UNROLL, some, 0)


def begin(source, target, semaphore):
    copy = pltpu.make_async_copy(source, target, semaphore)
    copy.start()
    return copy


def parcel_of(rows):
    return rows.T[:ROWS]


def rows_of(parcel):
    halo = parcel.shape[1]
    return jnp.concatenate([parcel, jnp.zeros((LANES - ROWS, halo), F32)], axis=0).T


def scaled_volume(vol, flag, stretch, scaled):
    nv = vol.shape[1]
    tilt = flag[...].astype(F32) * stretch[...]
    real, imag = vol[0], vol[1]
    fill = jnp.zeros((LANES - nv, vol.shape[2]), F32)
    scaled[0:nv, :] = real - tilt * imag
    scaled[nv:LANES, :] = fill
    scaled[LANES : LANES + nv, :] = imag + tilt * real
    scaled[LANES + nv : 2 * LANES, :] = fill


def place_parcels(picked, halo, lower, middle, upper):
    for direction in range(DIRS):
        parcel = parcel_of(picked[direction * halo : (direction + 1) * halo, :])
        if direction < 3:
            lower[direction] = parcel
        elif direction < 5:
            middle[direction - 3] = parcel
        else:
            upper[direction - 5] = parcel


def traces_kernel(
    trace, halo_list, table, up, mid, down, rows, turned, picked, done
):
    nq, faces = trace.shape[0], trace.shape[2]
    halo = up.shape[2]
    turned[...] = jnp.zeros_like(turned)
    turned[0:nq, :] = trace[:, 0, :]
    turned[HALF : HALF + nq, :] = trace[:, 1, :]
    rows[0:PAD, :] = jnp.zeros((PAD, LANES), F32)
    for first in range(0, faces, LANES):
        rows[PAD + first : PAD + first + LANES, :] = turned[:, first : first + LANES].T
    table_copy = begin(rows, table, done.at[0])
    gather_rows(DIRS * halo, halo_list, rows, picked)
    place_parcels(picked, halo, down, mid, up)
    table_copy.wait()


def sources_kernel(
    parts_in, elem_face,
    own_sum, up, mid, down,
    own, parts, sums0, sums1, sums2, sums3, sums4, sums5, sums6, sums7, ghosts, done,
):
    faces = own.shape[0]
    halo = up.shape[2]
    elems = parts.shape[1]
    parts_copy = begin(parts_in, parts, done.at[1])
    sums = (sums0, sums1, sums2, sums3, sums4, sums5, sums6, sums7)
    for total in sums:
        total[...] = jnp.zeros_like(total)
    parts_copy.wait()
    near = elems // 2

    def add_some(step, carry):
        for extra in range(4):
            elem = step * 4 + extra
            places = [
                (corner, elem + part * near) for corner in range(4) for part in range(2)
            ]
            slots = [elem_face[corner * elems + at] for corner, at in places]
            before = [total[pl.ds(slot, 1), :] for total, slot in zip(sums, slots)]
            values = [parts[corner, pl.ds(at, 1), :] for corner, at in places]
            for number, total in enumerate(sums):
                total[pl.ds(slots[number], 1), :] = before[number] + values[number]
        return carry

    lax.fori_loop(0, near // 4, add_some, 0)

    def summed(first, size):
        rows = [total[first : first + size, :] for total in sums]
        while len(rows) > 1:
            rows = [rows[k] + rows[k + 1] for k in range(0, len(rows), 2)]
        return rows[0]

    own[...] = summed(0, faces)
    own_copy = begin(own, own_sum, done.at[0])
    ghosts[...] = summed(faces, DIRS * halo)
    place_parcels(ghosts, halo, up, mid, down)
    own_copy.wait()


def halves(real, real_moved, imag, imag_moved, fill):
    high, rest = split(
        jnp.concatenate([real - imag_moved, fill, imag + real_moved, fill], axis=0)
    )
    return jnp.concatenate(
        [
            jnp.concatenate([high, high], axis=1),
            jnp.concatenate([rest, jnp.zeros_like(rest)], axis=1),
        ],
        axis=0,
    )


def operators_kernel(
    vol, flag, stretch, recon_op, cond_op, skel_op, lift_op,
    recon0, recon1, parts_out, skeleton, lifting,
    scaled, recon, cond, parts, done,
):
    nv, elems = vol.shape[1], vol.shape[2]
    nq = skel_op.shape[1]
    cond[...] = jnp.zeros_like(cond)
    for corner in range(4):
        real, imag = cond_op[corner, :, 0, :], cond_op[corner, :, 1, :]
        low = corner * LANES
        cond[low : low + nq, 0:nv] = real
        cond[low : low + nq, LANES : LANES + nv] = -imag
        cond[low + HALF : low + HALF + nq, 0:nv] = imag
        cond[low + HALF : low + HALF + nq, LANES : LANES + nv] = real
    scaled_volume(vol, flag, stretch, scaled)
    cond_high, cond_rest = split(cond[...])
    sent = []
    for first in range(0, elems, LANES):
        stop = first + LANES
        columns = jnp.concatenate(
            [scaled[0:LANES, first:stop].T, scaled[LANES : 2 * LANES, first:stop].T], axis=1
        )
        high, rest = split(columns)
        product = dot(high, cond_high, 1, 1) + dot(rest, cond_high, 1, 1) + dot(high, cond_rest, 1, 1)
        for corner in range(4):
            parts[corner, first:stop, :] = product[:, corner * LANES : (corner + 1) * LANES]
        sent.append(
            begin(
                parts.at[:, pl.ds(first, LANES), :],
                parts_out.at[:, pl.ds(first, LANES), :],
                done.at[first // LANES],
            )
        )
    for block in range(skel_op.shape[0]):
        low = block * 2 * ROWS
        skeleton[low : low + 2 * ROWS, :] = halves(
            *half_rolled(skel_op[block, :, 0, :], nq),
            *half_rolled(skel_op[block, :, 1, :], nq),
            jnp.zeros((HALF - nq, LANES), F32),
        )
    for corner in range(4):
        low = corner * 4 * LANES
        wide = []
        for part in range(2):
            block = jnp.concatenate(
                [lift_op[corner, :, part, :], jnp.zeros((nq, LANES - nv), F32)], axis=1
            )
            block = jnp.concatenate([block, jnp.zeros((LANES - nq, LANES), F32)], axis=0).T
            wide += [block, pltpu.roll(block, HALF, 1)]
        high, rest = split(jnp.concatenate([wide[0] - wide[3], wide[2] + wide[1]], axis=0))
        lifting[low : low + 2 * LANES, 0:LANES] = high
        lifting[low : low + 2 * LANES, LANES : 2 * LANES] = high
        lifting[low + 2 * LANES : low + 4 * LANES, 0:LANES] = rest
        lifting[low + 2 * LANES : low + 4 * LANES, LANES : 2 * LANES] = jnp.zeros_like(rest)
    recon[...] = jnp.zeros_like(recon)
    recon[0:nv, 0:nv] = recon_op[0]
    recon[0:nv, LANES : LANES + nv] = -recon_op[1]
    recon[LANES : LANES + nv, 0:nv] = recon_op[1]
    recon[LANES : LANES + nv, LANES : LANES + nv] = recon_op[0]
    high, rest = split(recon[...])
    size = 256
    part = recon0.shape[2]
    for first in range(0, elems, size):
        wanted, fine = split(scaled[:, first : first + size])
        product = dot(high, wanted) + dot(high, fine) + dot(rest, wanted)
        target = recon0 if first < part else recon1
        at = first % part
        target[0, :, at : at + size] = product[0:nv]
        target[1, :, at : at + size] = product[LANES : LANES + nv]
    for copy in sent:
        copy.wait()


def skeleton_tile(matrix, block_coef, slots, picked, first, size):
    real_sum = jnp.zeros((HALF, size), F32)
    imag_sum = jnp.zeros((HALF, size), F32)
    for block in range(block_coef.shape[0]):
        if block == 0:
            rows = slots[pl.ds(PAD + first, size), :]
        else:
            rows = picked[(block - 1) * size : block * size, :]
        high, rest = split(rows)
        low = block * 2 * ROWS
        product = dot(
            matrix[low : low + 2 * ROWS, :], jnp.concatenate([high, rest], axis=1), 1, 1
        )
        real = product[0:HALF] + product[ROWS : ROWS + HALF]
        imag = product[HALF:ROWS] + product[ROWS + HALF : 2 * ROWS]
        coef_real = block_coef[block, 0:1, pl.ds(first, size)]
        coef_imag = block_coef[block, 1:2, pl.ds(first, size)]
        real_sum = real_sum + (coef_real * real - coef_imag * imag)
        imag_sum = imag_sum + (coef_real * imag + coef_imag * real)
    return real_sum, imag_sum


def skeleton_loop(matrix, block_coef, adjacency, slots, picked, use, carry):
    tile = TILE
    faces = block_coef.shape[2]
    neighbours = block_coef.shape[0] - 1
    steps = faces // tile

    def fetch(step, target):
        for neighbour in range(neighbours):
            first = neighbour * faces + step * tile
            for extra in range(tile):
                row = adjacency[first + extra]
                at = neighbour * tile + extra
                target[at : at + 1, :] = slots[pl.ds(row + PAD, 1), :]

    def compute(step, source, carry):
        first = pl.multiple_of(step * tile, tile)
        real, imag = skeleton_tile(matrix, block_coef, slots, source, first, tile)
        return use(carry, first, real, imag)

    for neighbour in range(neighbours):
        gather_rows(tile, adjacency, slots, picked[0], neighbour * faces, neighbour * tile)

    def pair(number, carry):
        step = 2 * number
        fetch(step + 1, picked[1])
        carry = compute(step, picked[0], carry)
        fetch(step + 2, picked[0])
        return compute(step + 1, picked[1], carry)

    carry = lax.fori_loop(0, steps // 2 - 1, pair, carry)
    fetch(steps - 1, picked[1])
    carry = compute(steps - 2, picked[0], carry)
    return compute(steps - 1, picked[1], carry)


def join_kernel(up, mid, down, right, left, done):
    moves = [(down, 2, right, 0), (mid, 1, right, 1), (up, 2, right, 2)]
    moves += [(down, 0, left, 0), (mid, 0, left, 1), (up, 0, left, 2)]
    copies = [
        begin(source.at[place], target.at[to], done.at[number])
        for number, (source, place, target, to) in enumerate(moves)
    ]
    for copy in copies:
        copy.wait()


def ghost_places(up, down, right, left):
    return (
        left.at[0], down.at[1], right.at[0], left.at[1],
        right.at[1], left.at[2], up.at[1], right.at[2],
    )


def apply_kernel(
    table, own_sum, up, down, right, left, matrix, block_coef, adjacency,
    slots_out, rest_out,
    slots, own, rest, arrived, picked0, picked1, done,
):
    faces = own.shape[0]
    halo = arrived.shape[2]
    table_copy = begin(table, slots.at[pl.ds(0, PAD + faces)], done.at[0])
    copies = [
        begin(place, arrived.at[direction], done.at[3 + direction])
        for direction, place in enumerate(ghost_places(up, down, right, left))
    ]
    own_copy = begin(own_sum, own, done.at[1])
    for direction in range(DIRS):
        copies[direction].wait()
        first = PAD + faces + direction * halo
        slots[first : first + halo, :] = rows_of(arrived[direction])
    table_copy.wait()
    slots_copy = begin(slots, slots_out, done.at[2])
    own_copy.wait()

    def use(carry, first, real, imag):
        applied = rows_of(jnp.concatenate([real, imag], axis=0))
        rest[pl.ds(first, TILE), :] = own[pl.ds(first, TILE), :] - applied
        return carry

    skeleton_loop(matrix, block_coef, adjacency, slots, (picked0, picked1), use, 0)
    begin(rest, rest_out, done.at[0]).wait()
    slots_copy.wait()


def residual_kernel(
    rest, up, down, right, left, halo_list,
    rest_table, res_up, res_mid, res_down,
    returned, picked, back, sums0, sums1, sums2, sums3, sums4, sums5, sums6, sums7, done,
):
    faces = rest.shape[0]
    halo = returned.shape[2]
    rest_copy = begin(rest, sums0.at[pl.ds(PAD, faces)], done.at[0])
    places = (
        left.at[2], up.at[1], right.at[2], left.at[1],
        right.at[1], left.at[0], down.at[1], right.at[0],
    )
    copies = [
        begin(place, returned.at[direction], done.at[1 + direction])
        for direction, place in enumerate(places)
    ]
    sums0[0:PAD, :] = jnp.zeros((PAD, LANES), F32)
    others = (sums1, sums2, sums3, sums4, sums5, sums6, sums7)
    for total in others:
        total[...] = jnp.zeros_like(total)
    for direction in range(DIRS):
        copies[direction].wait()
        back[direction] = rows_of(returned[direction])
    rest_copy.wait()
    sums = (sums0,) + others

    def add_some(step, carry):
        for extra in range(4):
            entry = step * 4 + extra
            places = [halo_list[direction * halo + entry] + PAD for direction in range(DIRS)]
            before = [total[pl.ds(place, 1), :] for total, place in zip(sums, places)]
            values = [back[direction, pl.ds(entry, 1), :] for direction in range(DIRS)]
            for number, total in enumerate(sums):
                total[pl.ds(places[number], 1), :] = before[number] + values[number]
        return carry

    lax.fori_loop(0, halo // 4, add_some, 0)
    rest_table[...] = ((sums0[...] + sums1[...]) + (sums2[...] + sums3[...])) + (
        (sums4[...] + sums5[...]) + (sums6[...] + sums7[...])
    )
    rest_table[0:PAD, :] = jnp.zeros((PAD, LANES), F32)
    gather_rows(DIRS * halo, halo_list, rest_table, picked)
    place_parcels(picked, halo, res_down, res_mid, res_up)


def turn_kernel(rest_table, turned):
    for first in range(0, turned.shape[1], LANES):
        turned[:, first : first + LANES] = parcel_of(
            rest_table[PAD + first : PAD + first + LANES, :]
        )


def lifted_loop(matrix, elem_face, start, count, elems, slots, picked, use):
    size = LIFT

    def fetch(step, target):
        for corner in range(4):
            first = corner * count + start + step * size
            for extra in range(size):
                row = elem_face[first + extra]
                at = corner * size + extra
                target[at : at + 1, :] = slots[pl.ds(row + PAD, 1), :]

    def compute(step, rows):
        total = jnp.zeros((2 * LANES, size), F32)
        for corner in range(4):
            high, rest = split(rows[corner * size : (corner + 1) * size, :])
            at = corner * 4 * LANES
            product = dot(
                matrix[at : at + 4 * LANES, :], jnp.concatenate([high, rest], axis=1), 1, 1
            )
            total = total + (product[0 : 2 * LANES] + product[2 * LANES : 4 * LANES])
        use(step * size, total)

    steps = elems // size
    fetch(0, picked[0])
    for step in range(steps):
        if step + 1 < steps:
            fetch(step + 1, picked[(step + 1) % 2])
        compute(step, picked[step % 2])


def base_kernel(
    start, count, slots_in, recon, matrix, elem_face, base, slots, picked0, picked1, done
):
    nv, elems = base.shape[1], base.shape[2]
    begin(slots_in, slots, done.at[0]).wait()

    def use(first, product):
        stop = first + LIFT
        base[0, :, first:stop] = recon[0, :, first:stop] - product[0:nv]
        base[1, :, first:stop] = recon[1, :, first:stop] - product[LANES : LANES + nv]

    lifted_loop(matrix, elem_face, start, count, elems, slots, (picked0, picked1), use)


def lift_kernel(slots_in, matrix, elem_face, lifted, slots, picked0, picked1, done):
    nv, elems = lifted.shape[1], lifted.shape[2]
    begin(slots_in, slots, done.at[0]).wait()

    def use(first, product):
        stop = first + LIFT
        lifted[0, :, first:stop] = product[0:nv]
        lifted[1, :, first:stop] = product[LANES : LANES + nv]

    lifted_loop(matrix, elem_face, 0, elems, elems, slots, (picked0, picked1), use)


def image_kernel(
    rest_table, turned, up, down, right, left, matrix, block_coef, adjacency,
    slots_out, partial,
    slots, arrived, picked0, picked1, done,
):
    faces = turned.shape[1]
    halo = arrived.shape[2]
    table_copy = begin(rest_table, slots.at[pl.ds(0, PAD + faces)], done.at[0])
    copies = [
        begin(place, arrived.at[direction], done.at[3 + direction])
        for direction, place in enumerate(ghost_places(up, down, right, left))
    ]
    for direction in range(DIRS):
        copies[direction].wait()
        first = PAD + faces + direction * halo
        slots[first : first + halo, :] = rows_of(arrived[direction])
    table_copy.wait()
    slots_copy = begin(slots, slots_out, done.at[2])

    def use(carry, first, real, imag):
        rest_real = turned[0:HALF, pl.ds(first, TILE)]
        rest_imag = turned[HALF:ROWS, pl.ds(first, TILE)]
        return (
            carry[0] + (real * rest_real + imag * rest_imag),
            carry[1] + (real * rest_imag - imag * rest_real),
            carry[2] + (real * real + imag * imag),
        )

    zero = jnp.zeros((HALF, TILE), F32)
    totals = skeleton_loop(
        matrix, block_coef, adjacency, slots, (picked0, picked1), use, (zero, zero, zero)
    )
    lane = lax.broadcasted_iota(jnp.int32, (1, LANES), 1)
    line = jnp.zeros((1, LANES), F32)
    for place in range(3):
        line = line + jnp.where(lane == place, jnp.sum(totals[place]), 0.0)
    partial[...] = jnp.broadcast_to(line, partial.shape)
    slots_copy.wait()


def finish_kernel(gathered, trace, turned, base0, base1, lifted, trace_out, volume_out):
    nq = trace.shape[0]
    line = jnp.sum(gathered[...], axis=0, keepdims=True)
    lane = lax.broadcasted_iota(jnp.int32, (1, LANES), 1)
    entry = [
        jnp.sum(jnp.where(lane == place, line, 0.0), axis=1, keepdims=True)
        for place in range(3)
    ]
    step_real = entry[0] / entry[2]
    step_imag = entry[1] / entry[2]
    first = 0
    for base in (base0, base1):
        stop = first + base.shape[2]
        real, imag = lifted[0, :, first:stop], lifted[1, :, first:stop]
        volume_out[0, :, first:stop] = base[0] - (step_real * real - step_imag * imag)
        volume_out[1, :, first:stop] = base[1] - (step_real * imag + step_imag * real)
        first = stop
    rest_real = turned[0:nq, :]
    rest_imag = turned[HALF : HALF + nq, :]
    trace_out[:, 0, :] = trace[:, 0, :] + (step_real * rest_real - step_imag * rest_imag)
    trace_out[:, 1, :] = trace[:, 1, :] + (step_real * rest_imag + step_imag * rest_real)


SPACES = {
    "v": pltpu.MemorySpace.VMEM,
    "s": pltpu.MemorySpace.SMEM,
    "a": pl.ANY,
    "h": pltpu.HBM,
    "V": pltpu.MemorySpace.VMEM,
    "B": pltpu.MemorySpace.VMEM,
}


def call(kernel, name, args, out_shapes, spaces, scratch, limit, semaphores=0, time=1):
    specs = [pl.BlockSpec(memory_space=SPACES[letter]) for letter in spaces]
    shapes = [pltpu.VMEM(shape, kind) for shape, kind in scratch]
    if semaphores:
        shapes.append(pltpu.SemaphoreType.DMA((semaphores,)))
    args = [
        pltpu.with_memory_space_constraint(arg, pltpu.HBM) if letter in "hVB" else arg
        for arg, letter in zip(args, spaces)
    ]
    return pl.pallas_call(
        kernel,
        name=name,
        out_shape=[
            pltpu.HBM(shape, BF16 if letter == "B" else F32)
            if letter in "hVB"
            else jax.ShapeDtypeStruct(shape, F32)
            for shape, letter in zip(out_shapes, spaces[len(args) :])
        ],
        in_specs=specs[: len(args)],
        out_specs=specs[len(args) :],
        scratch_shapes=shapes,
        compiler_params=pltpu.CompilerParams(vmem_limit_bytes=limit * MIB),
        cost_estimate=pl.CostEstimate(
            flops=0, bytes_accessed=3300000 * time, transcendentals=0
        ),
    )(*args)


def from_behind(block, axis, distance):
    devices = range(lax.axis_size(axis))
    route = [(i - distance, i) for i in devices if i - distance in devices]
    return lax.ppermute(block, axis, route)


def everywhere(lines, axis):
    return lax.all_to_all(lines, axis, 0, 0)


def local(
    vol_rhs, trace_in, pml_flag, stretch, cond_op, skel_op, block_coef, recon_op, lift_op,
    elem_face, adjacency, halo_list,
):
    nv, elems = vol_rhs.shape[1], vol_rhs.shape[2]
    faces = trace_in.shape[2]
    halo = halo_list.shape[1]
    blocks = skel_op.shape[0]
    neighbours = adjacency.shape[0]
    slots = faces + DIRS * halo
    elem_face = elem_face.reshape(-1)
    adjacency = adjacency.reshape(-1)
    halo_list = halo_list.reshape(-1)
    flag = pml_flag.reshape(1, elems)
    tilt = stretch.reshape(1, elems)
    parcels = [(3, ROWS, halo), (2, ROWS, halo), (3, ROWS, halo)]

    def exchange(up, mid, down, sign, beside):
        up = from_behind(up, "gx", 1)
        down = from_behind(down, "gx", -1)
        up, down, beside = lax.optimization_barrier((up, down, beside))
        right, left = call(
            join_kernel, "join", (up, mid, down), [up.shape, up.shape], "aaa" + "vv", [], 2, 6
        )
        right = from_behind(right, "gy", sign)
        left = from_behind(left, "gy", -sign)
        return (up, down, right, left), beside

    trace_pairs = jnp.transpose(trace_in, (1, 0, 2))
    table, *outgoing = call(
        traces_kernel,
        "traces",
        (trace_pairs, halo_list),
        [(PAD + faces, LANES)] + parcels,
        "Vs" + "hvvv",
        [((PAD + faces, LANES), F32), ((LANES, faces), F32), ((DIRS * halo, LANES), F32)],
        8,
        1,
        4,
    )
    near = elems // 2
    operators = call(
        operators_kernel,
        "operators",
        (
            vol_rhs, flag, tilt, recon_op, jnp.transpose(cond_op, (0, 2, 1, 3)),
            jnp.transpose(skel_op, (0, 2, 1, 3)), jnp.transpose(lift_op, (0, 3, 1, 2)),
        ),
        [(2, nv, near), (2, nv, elems - near)]
        + [(4, elems, LANES)]
        + [(blocks * 2 * ROWS, 2 * LANES), (4 * 4 * LANES, 2 * LANES)],
        "VVVVVVV" + "VVhBB",
        [
            ((2 * LANES, elems), F32),
            ((2 * LANES, 2 * LANES), F32),
            ((4 * LANES, 2 * LANES), F32),
            ((4, elems, LANES), F32),
        ],
        18,
        elems // LANES,
        8,
    )
    arrived, operators = exchange(*outgoing, 1, operators)
    recon0, recon1, parts, skeleton, lifting = operators
    own_sum, *outgoing = call(
        sources_kernel,
        "sources",
        (parts, elem_face),
        [(faces, LANES)] + parcels,
        "hs" + "hvvv",
        [
            ((faces, LANES), F32),
            ((4, elems, LANES), F32),
        ]
        + [((slots, LANES), F32)] * 8
        + [((DIRS * halo, LANES), F32)],
        30,
        2,
        7,
    )
    slots_trace, rest = call(
        apply_kernel,
        "apply",
        (table, own_sum, *arrived, skeleton, block_coef, adjacency),
        [(PAD + slots, LANES), (faces, LANES)],
        "hhaaaaBVs" + "hh",
        [
            ((PAD + slots, LANES), F32),
            ((faces, LANES), F32),
            ((faces, LANES), F32),
            ((DIRS, ROWS, halo), F32),
            ((neighbours * TILE, LANES), F32),
            ((neighbours * TILE, LANES), F32),
        ],
        16,
        3 + DIRS,
        16,
    )
    returned, (slots_trace, rest) = exchange(*outgoing, -1, (slots_trace, rest))

    def base_part(start, recon):
        return call(
            functools.partial(base_kernel, start, elems),
            "base",
            (slots_trace, recon, lifting, elem_face),
            [recon.shape],
            "hVBs" + "V",
            [((PAD + slots, LANES), F32)] + [((4 * LIFT, LANES), F32)] * 2,
            10,
            1,
            5,
        )[0]

    base0 = base_part(0, recon0)
    *returned, base0 = lax.optimization_barrier((*returned, base0))
    rest_table, *outgoing = call(
        residual_kernel,
        "residual",
        (rest, *returned, halo_list),
        [(PAD + faces, LANES)] + parcels,
        "haaaas" + "Vvvv",
        [
            ((DIRS, ROWS, halo), F32),
            ((DIRS * halo, LANES), F32),
            ((DIRS, halo, LANES), F32),
        ]
        + [((PAD + faces, LANES), F32)] * 8,
        16,
        1 + DIRS,
        8,
    )
    base1 = base_part(near, recon1)
    arrived, base1 = exchange(*outgoing, 1, base1)
    (turned,) = call(turn_kernel, "turn", (rest_table,), [(ROWS, faces)], "VV", [], 4)
    across, along = lax.axis_size("gx"), lax.axis_size("gy")
    slots_rest, partial = call(
        image_kernel,
        "image",
        (rest_table, turned, *arrived, skeleton, block_coef, adjacency),
        [(PAD + slots, LANES), (along, LANES)],
        "hVaaaaBVs" + "hv",
        [
            ((PAD + slots, LANES), F32),
            ((DIRS, ROWS, halo), F32),
            ((neighbours * TILE, LANES), F32),
            ((neighbours * TILE, LANES), F32),
        ],
        16,
        3 + DIRS,
        16,
    )
    (lifted,) = call(
        lift_kernel,
        "lift",
        (slots_rest, lifting, elem_face),
        [vol_rhs.shape],
        "hBs" + "V",
        [((PAD + slots, LANES), F32)] + [((4 * LIFT, LANES), F32)] * 2,
        12,
        1,
        7,
    )
    lines, lifted = lax.optimization_barrier((everywhere(partial, "gy"), lifted))
    lines = jnp.sum(lines, axis=0, keepdims=True)
    gathered = everywhere(jnp.broadcast_to(lines, (across, LANES)), "gx")
    trace_pairs, volume_out = call(
        finish_kernel,
        "finish",
        (gathered, trace_pairs, turned, base0, base1, lifted),
        [trace_pairs.shape, vol_rhs.shape],
        "vvvvvv" + "VV",
        [],
        8,
    )
    trace_out = jnp.transpose(trace_pairs, (1, 0, 2))
    return trace_out, volume_out


def solution(mesh):
    split_last = ("gx", "gy")
    in_specs = (
        P(None, None, split_last),
        P(None, None, split_last),
        P(split_last),
        P(split_last),
        P(),
        P(),
        P(None, None, split_last),
        P(),
        P(),
        P(None, split_last),
        P(None, split_last),
        P(None, split_last),
    )
    out_specs = (P(None, None, split_last), P(None, None, split_last))
    return jax.shard_map(
        local, mesh=mesh, in_specs=in_specs, out_specs=out_specs, check_vma=False
    )
```

time: 170 us -> 166 us (0.976)
  local copies, waits for them, and re-layouts: 7.62 us -> 2.67 us
  Pallas kernels: 86.4 us -> 82.9 us
  waiting for transfers between devices: 6.44 us -> 9.81 us
    unnamed x14, local copies, waits for them, and re-layouts: 6.33 us -> 2.64 us
    pallas_call x12 -> x14, Pallas kernels: 86.4 us -> 82.9 us  [call(): pl.pallas_call(kernel, name=name, out_shape=[pltpu.HBM(shape, BF16 if let...]
    ppermute x12, waiting for transfers between devices: 2.97 us -> 5.42 us  [from_behind(): return lax.ppermute(block, axis, route)]
  transfers between devices with their start and end apart: 13 -> 13, of which waited for: 2 -> 3; matrix products, arithmetic and copies ran while one was open for 2% -> 0% of each run, Pallas kernels for 31% -> 32%
where the time goes in v2:
time: 166 us; the launch traced here: 165 us
  Pallas kernels  82.9 us (50%)
  starting transfers between devices  50.9 us (31%)
  blocking collectives  17.7 us (11%)
  waiting for transfers between devices  9.81 us (6%)
  local copies, waits for them, and re-layouts  2.67 us (2%)
    pallas_call x14, Pallas kernels, call(): pl.pallas_call(kernel, name=name, out_shape=[pltpu.HBM(shape, BF16 if let...  82.9 us
    ppermute x12, starting transfers between devices, from_behind(): return lax.ppermute(block, axis, route)  34.9 us
    all_to_all x1, blocking collectives, everywhere(): return lax.all_to_all(lines, axis, 0, 0)  17.7 us
    all_to_all x1, starting transfers between devices, everywhere(): return lax.all_to_all(lines, axis, 0, 0)  16.1 us
    ppermute x12, waiting for transfers between devices, from_behind(): return lax.ppermute(block, axis, route)  5.42 us
    all_to_all x1, waiting for transfers between devices, everywhere(): return lax.all_to_all(lines, axis, 0, 0)  4.39 us
  transfers between devices with their start and end apart: 13, of which 3 were waited for; matrix products, arithmetic and copies ran while one was open for 0% of the time, Pallas kernels for 32%

profile of v2, /device:TPU:1, one launch (start us, length us, event | category | flops | bytes accessed | tf_op | source)
XLA Modules:
  0.0 165.0 jit_solution(18446522637746557751)
XLA Ops:
  1.3 3.5 %traces.1 = (f32[2056,128]{1,0:T(8,128)}, f32[3,80,256]{2,1,0:T(8,128)S(1)}, f32[2,80,256]{2,1,0:T(8,128)S(1)}, f32[3,80,256]{2,1,0:T(8,128)S(1)}) custom-call(f32[36,2,2048]{2,1,0:T(2,128)} %bitcast.18, s32[2048]{0:T(1024)S(1)} %bitcast.24), custom_call_target="tpu_custom_call" | custom-call | bytes 13200000 | tf_op jit(solution)/shard_map/traces/pallas_call | solution.py:532
  4.8 4.0 %collective-permute-start = (f32[3,80,256]{2,1,0:T(8,128)S(1)}, f32[3,80,256]{2,1,0:T(8,128)S(1)}, u32[]{:S(2)}, u32[]{:S(2)}) collective-permute-start(f32[3,80,256]{2,1,0:T(8,128)S(1)} %get-tuple-element.52), channel_id=1, source_target_pairs={{0,32},{32,64},{64,96},{96,128},{128,160},{160,192},{192,224},{224... | collective-permute-start | bytes 737288 | tf_op jit(solution)/shard_map/ppermute | solution.py:554
  10.9 6.2 %operators.1 = (f32[2,120,512]{2,1,0:T(8,128)}, f32[2,120,512]{2,1,0:T(8,128)}, f32[4,1024,128]{2,1,0:T(8,128)}, bf16[1120,256]{1,0:T(8,128)(2,1)}, bf16[2048,256]{1,0:T(8,128)(2,1)}) custom-call(f32[2,120,1024]{2,1,0:T(8,128)} %vol.1, s32[1,1024]{1,0:T(1,128)} %bitcast.33, f32[1,1024]{1,0:T(1,128)} %bitcast.34, f32[2,120,120]{2,1,0:T(8,128)} %recon_op.1, ...), custom_call_target="tpu_custom_call" | custom-call | bytes 26400000 | tf_op jit(solution)/shard_map/operators/pallas_call | solution.py:532
  17.8 5.4 %collective-permute-start.4 = (f32[3,80,256]{2,1,0:T(8,128)S(1)}, f32[3,80,256]{2,1,0:T(8,128)S(1)}, u32[]{:S(2)}, u32[]{:S(2)}) collective-permute-start(f32[3,80,256]{2,1,0:T(8,128)S(1)} %get-tuple-element.67), channel_id=1, source_target_pairs={{0,1},{1,2},{2,3},{3,4},{4,5},{5,6},{6,7},{7,8},{8,9},{9,10},{10,1... | collective-permute-start | bytes 737288 | tf_op jit(solution)/shard_map/ppermute | solution.py:554
  23.2 2.0 %collective-permute-start.5 = (f32[3,80,256]{2,1,0:T(8,128)S(1)}, f32[3,80,256]{2,1,0:T(8,128)S(1)}, u32[]{:S(2)}, u32[]{:S(2)}) collective-permute-start(f32[3,80,256]{2,1,0:T(8,128)S(1)} %get-tuple-element.68), channel_id=1, source_target_pairs={{1,0},{2,1},{3,2},{4,3},{5,4},{6,5},{7,6},{8,7},{9,8},{10,9},{11,1... | collective-permute-start | bytes 737288 | tf_op jit(solution)/shard_map/ppermute | solution.py:554
  25.2 8.4 %sources.1 = (f32[2048,128]{1,0:T(8,128)}, f32[3,80,256]{2,1,0:T(8,128)S(1)}, f32[2,80,256]{2,1,0:T(8,128)S(1)}, f32[3,80,256]{2,1,0:T(8,128)S(1)}) custom-call(f32[4,1024,128]{2,1,0:T(8,128)} %get-tuple-element.59.parts_in, s32[4096]{0:T(1024)S(1)} %bitcast.20), custom_call_target="tpu_custom_call" | custom-call | bytes 23100000 | tf_op jit(solution)/shard_map/sources/pallas_call | solution.py:532
  33.6 4.3 %collective-permute-start.2 = (f32[3,80,256]{2,1,0:T(8,128)S(1)}, f32[3,80,256]{2,1,0:T(8,128)S(1)}, u32[]{:S(2)}, u32[]{:S(2)}) collective-permute-start(f32[3,80,256]{2,1,0:T(8,128)S(1)} %get-tuple-element.60), channel_id=1, source_target_pairs={{0,32},{32,64},{64,96},{96,128},{128,160},{160,192},{192,224},{224... | collective-permute-start | bytes 737288 | tf_op jit(solution)/shard_map/ppermute | solution.py:554
  39.3 16.7 %apply.1 = (f32[4104,128]{1,0:T(8,128)}, f32[2048,128]{1,0:T(8,128)}) custom-call(f32[2056,128]{1,0:T(8,128)} %get-tuple-element.62.table, f32[2048,128]{1,0:T(8,128)} %get-tuple-element.63.own_sum, f32[3,80,256]{2,1,0:T(8,128)S(1)} %collective-permute-done.up, f32[3,80,256]{2,1,0:T(8,128)S(1)} %collective-permute-done.1.down, ...), custom_call_target="tpu_custom_call" | custom-call | bytes 52800000 | tf_op jit(solution)/shard_map/apply/pallas_call | solution.py:532
  56.8 1.9 %collective-permute-start.6 = (f32[3,80,256]{2,1,0:T(8,128)S(1)}, f32[3,80,256]{2,1,0:T(8,128)S(1)}, u32[]{:S(2)}, u32[]{:S(2)}) collective-permute-start(f32[3,80,256]{2,1,0:T(8,128)S(1)} %get-tuple-element.76), channel_id=1, source_target_pairs={{1,0},{2,1},{3,2},{4,3},{5,4},{6,5},{7,6},{8,7},{9,8},{10,9},{11,1... | collective-permute-start | bytes 737288 | tf_op jit(solution)/shard_map/ppermute | solution.py:554
  58.7 3.8 %collective-permute-start.7 = (f32[3,80,256]{2,1,0:T(8,128)S(1)}, f32[3,80,256]{2,1,0:T(8,128)S(1)}, u32[]{:S(2)}, u32[]{:S(2)}) collective-permute-start(f32[3,80,256]{2,1,0:T(8,128)S(1)} %get-tuple-element.77), channel_id=1, source_target_pairs={{0,1},{1,2},{2,3},{3,4},{4,5},{5,6},{6,7},{7,8},{8,9},{9,10},{10,1... | collective-permute-start | bytes 737288 | tf_op jit(solution)/shard_map/ppermute | solution.py:554
  62.5 5.6 %base.2.base0 = f32[2,120,512]{2,1,0:T(8,128)} custom-call(f32[4104,128]{1,0:T(8,128)} %get-tuple-element.78.slots_in, f32[2,120,512]{2,1,0:T(8,128)} %get-tuple-element.79.recon, bf16[2048,256]{1,0:T(8,128)(2,1)} %get-tuple-element.80.matrix, s32[4096]{0:T(1024)S(1)} %bitcast.21), custom_call_target="tpu_custom_call" | custom-call | bytes 16500000 | tf_op jit(solution)/shard_map/base/pallas_call | solution.py:532
  68.1 7.9 %residual.1 = (f32[2056,128]{1,0:T(8,128)}, f32[3,80,256]{2,1,0:T(8,128)S(1)}, f32[2,80,256]{2,1,0:T(8,128)S(1)}, f32[3,80,256]{2,1,0:T(8,128)S(1)}) custom-call(f32[2048,128]{1,0:T(8,128)} %get-tuple-element.72.rest, f32[3,80,256]{2,1,0:T(8,128)S(1)} %collective-permute-done.2.up, f32[3,80,256]{2,1,0:T(8,128)S(1)} %collective-permute-done.3.down, ...), custom_call_target="tpu_custom_call" | custom-call | bytes 26400000 | tf_op jit(solution)/shard_map/residual/pallas_call | solution.py:532
  76.1 4.0 %collective-permute-start.8 = (f32[3,80,256]{2,1,0:T(8,128)S(1)}, f32[3,80,256]{2,1,0:T(8,128)S(1)}, u32[]{:S(2)}, u32[]{:S(2)}) collective-permute-start(f32[3,80,256]{2,1,0:T(8,128)S(1)} %get-tuple-element.86), channel_id=1, source_target_pairs={{0,32},{32,64},{64,96},{96,128},{128,160},{160,192},{192,224},{224... | collective-permute-start | bytes 737288 | tf_op jit(solution)/shard_map/ppermute | solution.py:554
  81.4 5.6 %base.3.base1 = f32[2,120,512]{2,1,0:T(8,128)} custom-call(f32[4104,128]{1,0:T(8,128)} %get-tuple-element.78.slots_in, f32[2,120,512]{2,1,0:T(8,128)} %get-tuple-element.88.recon, bf16[2048,256]{1,0:T(8,128)(2,1)} %get-tuple-element.80.matrix, s32[4096]{0:T(1024)S(1)} %bitcast.22), custom_call_target="tpu_custom_call" | custom-call | bytes 16500000 | tf_op jit(solution)/shard_map/base/pallas_call | solution.py:532
  87.0 2.2 %collective-permute-done.9.down = f32[3,80,256]{2,1,0:T(8,128)S(1)} collective-permute-done((f32[3,80,256]{2,1,0:T(8,128)S(1)}, f32[3,80,256]{2,1,0:T(8,128)S(1)}, u32[]{:S(2)}, u32[]{:S(2)}) %collective-permute-start.9) | collective-permute-done | bytes 245792 | tf_op jit(solution)/shard_map/ppermute | solution.py:554
  89.9 3.7 %collective-permute-start.10 = (f32[3,80,256]{2,1,0:T(8,128)S(1)}, f32[3,80,256]{2,1,0:T(8,128)S(1)}, u32[]{:S(2)}, u32[]{:S(2)}) collective-permute-start(f32[3,80,256]{2,1,0:T(8,128)S(1)} %get-tuple-element.92), channel_id=1, source_target_pairs={{0,1},{1,2},{2,3},{3,4},{4,5},{5,6},{6,7},{7,8},{8,9},{9,10},{10,1... | collective-permute-start | bytes 737288 | tf_op jit(solution)/shard_map/ppermute | solution.py:554
  93.6 1.9 %collective-permute-start.11 = (f32[3,80,256]{2,1,0:T(8,128)S(1)}, f32[3,80,256]{2,1,0:T(8,128)S(1)}, u32[]{:S(2)}, u32[]{:S(2)}) collective-permute-start(f32[3,80,256]{2,1,0:T(8,128)S(1)} %get-tuple-element.93), channel_id=1, source_target_pairs={{1,0},{2,1},{3,2},{4,3},{5,4},{6,5},{7,6},{8,7},{9,8},{10,9},{11,1... | collective-permute-start | bytes 737288 | tf_op jit(solution)/shard_map/ppermute | solution.py:554
  95.5 2.4 %turn.1.turned = f32[80,2048]{1,0:T(8,128)} custom-call(f32[2056,128]{1,0:T(8,128)} %get-tuple-element.85.rest_table), custom_call_target="tpu_custom_call" | custom-call | bytes 3300000 | tf_op jit(solution)/shard_map/turn/pallas_call | solution.py:532
  97.9 3.2 %collective-permute-done.11.left = f32[3,80,256]{2,1,0:T(8,128)S(1)} collective-permute-done((f32[3,80,256]{2,1,0:T(8,128)S(1)}, f32[3,80,256]{2,1,0:T(8,128)S(1)}, u32[]{:S(2)}, u32[]{:S(2)}) %collective-permute-start.11) | collective-permute-done | bytes 245792 | tf_op jit(solution)/shard_map/ppermute | solution.py:554
  101.1 15.6 %image.1 = (f32[4104,128]{1,0:T(8,128)}, f32[32,128]{1,0:T(8,128)}) custom-call(f32[2056,128]{1,0:T(8,128)} %get-tuple-element.85.rest_table, f32[80,2048]{1,0:T(8,128)} %turn.1.turned, f32[3,80,256]{2,1,0:T(8,128)S(1)} %collective-permute-done.8.up, f32[3,80,256]{2,1,0:T(8,128)S(1)} %collective-permute-done.9.down, ...), custom_call_target="tpu_custom_call" | custom-call | bytes 52800000 | tf_op jit(solution)/shard_map/image/pallas_call | solution.py:532
  116.7 16.1 %all-to-all-start = ((f32[32,1,128]{2,1,0:T(1,128)}), f32[32,1,128]{2,1,0:T(1,128)S(1)}, u32[]{:S(2)}, u32[]{:S(2)}) async-start(f32[32,1,128]{2,1,0:T(1,128)} %bitcast.7), calls=%async_computation | async-start | bytes 32768 | tf_op jit(solution)/shard_map/all_to_all | solution.py:558
  132.8 7.3 %lift.1.lifted = f32[2,120,1024]{2,1,0:T(8,128)} custom-call(f32[4104,128]{1,0:T(8,128)} %get-tuple-element.95.slots_in, bf16[2048,256]{1,0:T(8,128)(2,1)} %get-tuple-element.80.matrix, s32[4096]{0:T(1024)S(1)} %bitcast.23), custom_call_target="tpu_custom_call" | custom-call | bytes 23100000 | tf_op jit(solution)/shard_map/lift/pallas_call | solution.py:532
  140.1 4.4 %all-to-all-done = f32[32,1,128]{2,1,0:T(1,128)S(1)} async-done(((f32[32,1,128]{2,1,0:T(1,128)}), f32[32,1,128]{2,1,0:T(1,128)S(1)}, u32[]{:S(2)}, u32[]{:S(2)}) %all-to-all-start) | async-done | bytes 16416 | tf_op jit(solution)/shard_map/all_to_all | solution.py:558
  144.6 17.7 %all_to_all.20 = f32[16,1,128]{2,1,0:T(1,128)S(1)} all-to-all(f32[16,1,128]{2,1,0:T(1,128)S(1)} %broadcast_in_dim.2), channel_id=1, replica_groups=mesh['gx'=16,'gy'=32] {'gx'}, dimensions={0} | all-to-all | bytes 16384 | tf_op jit(solution)/shard_map/all_to_all | solution.py:558
  (34 shorter events, 10.2 us)
Async XLA Ops:
  4.8 12.3 %collective-permute-start = (f32[3,80,256]{2,1,0:T(8,128)S(1)}, f32[3,80,256]{2,1,0:T(8,128)S(1)}, u32[]{:S(2)}, u32[]{:S(2)}) collective-permute-start(f32[3,80,256]{2,1,0:T(8,128)S(1)} %get-tuple-element.52), channel_id=1, source_target_pairs={{0,32},{32,64},{64,96},{96,128},{128,160},{160,192},{192,224},{224... | collective-permute-start | bytes 737288 | tf_op jit(solution)/shard_map/ppermute | solution.py:554
  8.8 8.3 %collective-permute-start.1 = (f32[3,80,256]{2,1,0:T(8,128)S(1)}, f32[3,80,256]{2,1,0:T(8,128)S(1)}, u32[]{:S(2)}, u32[]{:S(2)}) collective-permute-start(f32[3,80,256]{2,1,0:T(8,128)S(1)} %get-tuple-element.53), channel_id=1, source_target_pairs={{32,0},{64,32},{96,64},{128,96},{160,128},{192,160},{224,192},{256... | collective-permute-start | bytes 737288 | tf_op jit(solution)/shard_map/ppermute | solution.py:554
  10.9 28.4 %copy-start.5 = (s32[6,2048]{1,0:T(8,128)S(1)}, s32[6,2048]{1,0:T(8,128)}, u32[]{:S(2)}) copy-start(s32[6,2048]{1,0:T(8,128)} %param.22) | copy-start | bytes 147460
  17.8 21.4 %collective-permute-start.4 = (f32[3,80,256]{2,1,0:T(8,128)S(1)}, f32[3,80,256]{2,1,0:T(8,128)S(1)}, u32[]{:S(2)}, u32[]{:S(2)}) collective-permute-start(f32[3,80,256]{2,1,0:T(8,128)S(1)} %get-tuple-element.67), channel_id=1, source_target_pairs={{0,1},{1,2},{2,3},{3,4},{4,5},{5,6},{6,7},{7,8},{8,9},{9,10},{10,1... | collective-permute-start | bytes 737288 | tf_op jit(solution)/shard_map/ppermute | solution.py:554
  23.2 16.0 %collective-permute-start.5 = (f32[3,80,256]{2,1,0:T(8,128)S(1)}, f32[3,80,256]{2,1,0:T(8,128)S(1)}, u32[]{:S(2)}, u32[]{:S(2)}) collective-permute-start(f32[3,80,256]{2,1,0:T(8,128)S(1)} %get-tuple-element.68), channel_id=1, source_target_pairs={{1,0},{2,1},{3,2},{4,3},{5,4},{6,5},{7,6},{8,7},{9,8},{10,9},{11,1... | collective-permute-start | bytes 737288 | tf_op jit(solution)/shard_map/ppermute | solution.py:554
  33.6 22.4 %collective-permute-start.2 = (f32[3,80,256]{2,1,0:T(8,128)S(1)}, f32[3,80,256]{2,1,0:T(8,128)S(1)}, u32[]{:S(2)}, u32[]{:S(2)}) collective-permute-start(f32[3,80,256]{2,1,0:T(8,128)S(1)} %get-tuple-element.60), channel_id=1, source_target_pairs={{0,32},{32,64},{64,96},{96,128},{128,160},{160,192},{192,224},{224... | collective-permute-start | bytes 737288 | tf_op jit(solution)/shard_map/ppermute | solution.py:554
  37.9 18.1 %collective-permute-start.3 = (f32[3,80,256]{2,1,0:T(8,128)S(1)}, f32[3,80,256]{2,1,0:T(8,128)S(1)}, u32[]{:S(2)}, u32[]{:S(2)}) collective-permute-start(f32[3,80,256]{2,1,0:T(8,128)S(1)} %get-tuple-element.61), channel_id=1, source_target_pairs={{32,0},{64,32},{96,64},{128,96},{160,128},{192,160},{224,192},{256... | collective-permute-start | bytes 737288 | tf_op jit(solution)/shard_map/ppermute | solution.py:554
  56.8 11.4 %collective-permute-start.6 = (f32[3,80,256]{2,1,0:T(8,128)S(1)}, f32[3,80,256]{2,1,0:T(8,128)S(1)}, u32[]{:S(2)}, u32[]{:S(2)}) collective-permute-start(f32[3,80,256]{2,1,0:T(8,128)S(1)} %get-tuple-element.76), channel_id=1, source_target_pairs={{1,0},{2,1},{3,2},{4,3},{5,4},{6,5},{7,6},{8,7},{9,8},{10,9},{11,1... | collective-permute-start | bytes 737288 | tf_op jit(solution)/shard_map/ppermute | solution.py:554
  58.7 9.5 %collective-permute-start.7 = (f32[3,80,256]{2,1,0:T(8,128)S(1)}, f32[3,80,256]{2,1,0:T(8,128)S(1)}, u32[]{:S(2)}, u32[]{:S(2)}) collective-permute-start(f32[3,80,256]{2,1,0:T(8,128)S(1)} %get-tuple-element.77), channel_id=1, source_target_pairs={{0,1},{1,2},{2,3},{3,4},{4,5},{5,6},{6,7},{7,8},{8,9},{9,10},{10,1... | collective-permute-start | bytes 737288 | tf_op jit(solution)/shard_map/ppermute | solution.py:554
  76.1 10.9 %collective-permute-start.8 = (f32[3,80,256]{2,1,0:T(8,128)S(1)}, f32[3,80,256]{2,1,0:T(8,128)S(1)}, u32[]{:S(2)}, u32[]{:S(2)}) collective-permute-start(f32[3,80,256]{2,1,0:T(8,128)S(1)} %get-tuple-element.86), channel_id=1, source_target_pairs={{0,32},{32,64},{64,96},{96,128},{128,160},{160,192},{192,224},{224... | collective-permute-start | bytes 737288 | tf_op jit(solution)/shard_map/ppermute | solution.py:554
  80.1 9.1 %collective-permute-start.9 = (f32[3,80,256]{2,1,0:T(8,128)S(1)}, f32[3,80,256]{2,1,0:T(8,128)S(1)}, u32[]{:S(2)}, u32[]{:S(2)}) collective-permute-start(f32[3,80,256]{2,1,0:T(8,128)S(1)} %get-tuple-element.87), channel_id=1, source_target_pairs={{32,0},{64,32},{96,64},{128,96},{160,128},{192,160},{224,192},{256... | collective-permute-start | bytes 737288 | tf_op jit(solution)/shard_map/ppermute | solution.py:554
  89.9 8.0 %collective-permute-start.10 = (f32[3,80,256]{2,1,0:T(8,128)S(1)}, f32[3,80,256]{2,1,0:T(8,128)S(1)}, u32[]{:S(2)}, u32[]{:S(2)}) collective-permute-start(f32[3,80,256]{2,1,0:T(8,128)S(1)} %get-tuple-element.92), channel_id=1, source_target_pairs={{0,1},{1,2},{2,3},{3,4},{4,5},{5,6},{6,7},{7,8},{8,9},{9,10},{10,1... | collective-permute-start | bytes 737288 | tf_op jit(solution)/shard_map/ppermute | solution.py:554
  93.6 7.5 %collective-permute-start.11 = (f32[3,80,256]{2,1,0:T(8,128)S(1)}, f32[3,80,256]{2,1,0:T(8,128)S(1)}, u32[]{:S(2)}, u32[]{:S(2)}) collective-permute-start(f32[3,80,256]{2,1,0:T(8,128)S(1)} %get-tuple-element.93), channel_id=1, source_target_pairs={{1,0},{2,1},{3,2},{4,3},{5,4},{6,5},{7,6},{8,7},{9,8},{10,9},{11,1... | collective-permute-start | bytes 737288 | tf_op jit(solution)/shard_map/ppermute | solution.py:554
  116.7 27.8 %all-to-all-start = ((f32[32,1,128]{2,1,0:T(1,128)}), f32[32,1,128]{2,1,0:T(1,128)S(1)}, u32[]{:S(2)}, u32[]{:S(2)}) async-start(f32[32,1,128]{2,1,0:T(1,128)} %bitcast.7), calls=%async_computation | async-start | bytes 32768 | tf_op jit(solution)/shard_map/all_to_all | solution.py:558
  132.8 29.5 %copy-start = (f32[80,2048]{1,0:T(8,128)S(1)}, f32[80,2048]{1,0:T(8,128)}, u32[]{:S(2)}) copy-start(f32[80,2048]{1,0:T(8,128)} %turn.1.turned) | copy-start | bytes 1966084
  132.8 29.5 %copy-start.2 = (f32[2,36,2048]{2,0,1:T(2,128)S(1)}, f32[2,36,2048]{2,0,1:T(2,128)}, u32[]{:S(2)}) copy-start(f32[2,36,2048]{2,0,1:T(2,128)} %param.13) | copy-start | bytes 1769476
  132.8 29.4 %copy-start.3 = (f32[2,120,512]{2,1,0:T(8,128)S(1)}, f32[2,120,512]{2,1,0:T(8,128)}, u32[]{:S(2)}) copy-start(f32[2,120,512]{2,1,0:T(8,128)} %base.2.base0) | copy-start | bytes 1474564
  132.8 29.4 %copy-start.4 = (f32[2,120,512]{2,1,0:T(8,128)S(1)}, f32[2,120,512]{2,1,0:T(8,128)}, u32[]{:S(2)}) copy-start(f32[2,120,512]{2,1,0:T(8,128)} %base.3.base1) | copy-start | bytes 1474564
  162.2 1.2 copy-start.1

commit v3 on v2

--- a/solution.py
+++ b/solution.py
@@ -86,10 +86,14 @@
             upper[direction - 5] = parcel
 
 
-def traces_kernel(
-    trace, halo_list, table, up, mid, down, rows, turned, picked, done
+def prepare_kernel(
+    trace, vol, flag, stretch, cond_op, halo_list, elem_face,
+    table, own_sum, up, mid, down,
+    rows, turned, picked, own, scaled, cond, parts,
+    sums0, sums1, sums2, sums3, sums4, sums5, sums6, sums7, done,
 ):
     nq, faces = trace.shape[0], trace.shape[2]
+    nv, elems = vol.shape[1], vol.shape[2]
     halo = up.shape[2]
     turned[...] = jnp.zeros_like(turned)
     turned[0:nq, :] = trace[:, 0, :]
@@ -98,24 +102,28 @@
     for first in range(0, faces, LANES):
         rows[PAD + first : PAD + first + LANES, :] = turned[:, first : first + LANES].T
     table_copy = begin(rows, table, done.at[0])
-    gather_rows(DIRS * halo, halo_list, rows, picked)
-    place_parcels(picked, halo, down, mid, up)
-    table_copy.wait()
-
-
-def sources_kernel(
-    parts_in, elem_face,
-    own_sum, up, mid, down,
-    own, parts, sums0, sums1, sums2, sums3, sums4, sums5, sums6, sums7, ghosts, done,
-):
-    faces = own.shape[0]
-    halo = up.shape[2]
-    elems = parts.shape[1]
-    parts_copy = begin(parts_in, parts, done.at[1])
+    cond[...] = jnp.zeros_like(cond)
+    for corner in range(4):
+        real, imag = cond_op[corner, :, 0, :], cond_op[corner, :, 1, :]
+        low = corner * LANES
+        cond[low : low + nq, 0:nv] = real
+        cond[low : low + nq, LANES : LANES + nv] = -imag
+        cond[low + HALF : low + HALF + nq, 0:nv] = imag
+        cond[low + HALF : low + HALF + nq, LANES : LANES + nv] = real
+    scaled_volume(vol, flag, stretch, scaled)
+    cond_high, cond_rest = split(cond[...])
+    for first in range(0, elems, LANES):
+        stop = first + LANES
+        columns = jnp.concatenate(
+            [scaled[0:LANES, first:stop].T, scaled[LANES : 2 * LANES, first:stop].T], axis=1
+        )
+        high, rest = split(columns)
+        product = dot(high, cond_high, 1, 1) + dot(rest, cond_high, 1, 1) + dot(high, cond_rest, 1, 1)
+        for corner in range(4):
+            parts[corner, first:stop, :] = product[:, corner * LANES : (corner + 1) * LANES]
     sums = (sums0, sums1, sums2, sums3, sums4, sums5, sums6, sums7)
     for total in sums:
         total[...] = jnp.zeros_like(total)
-    parts_copy.wait()
     near = elems // 2
 
     def add_some(step, carry):
@@ -134,15 +142,27 @@
     lax.fori_loop(0, near // 4, add_some, 0)
 
     def summed(first, size):
-        rows = [total[first : first + size, :] for total in sums]
-        while len(rows) > 1:
-            rows = [rows[k] + rows[k + 1] for k in range(0, len(rows), 2)]
-        return rows[0]
+        lines = [total[first : first + size, :] for total in sums]
+        while len(lines) > 1:
+            lines = [lines[k] + lines[k + 1] for k in range(0, len(lines), 2)]
+        return lines[0]
 
     own[...] = summed(0, faces)
-    own_copy = begin(own, own_sum, done.at[0])
-    ghosts[...] = summed(faces, DIRS * halo)
-    place_parcels(ghosts, halo, up, mid, down)
+    own_copy = begin(own, own_sum, done.at[1])
+    gather_rows(DIRS * halo, halo_list, rows, picked)
+    for direction in range(DIRS):
+        parcel = parcel_of(picked[direction * halo : (direction + 1) * halo, :])
+        back = parcel_of(summed(faces + direction * halo, halo))
+        if direction < 3:
+            down[direction] = parcel
+            up[3 + direction] = back
+        elif direction < 5:
+            mid[direction - 3] = parcel
+            mid[direction - 1] = back
+        else:
+            up[direction - 5] = parcel
+            down[direction - 2] = back
+    table_copy.wait()
     own_copy.wait()
 
 
@@ -160,39 +180,11 @@
 
 
 def operators_kernel(
-    vol, flag, stretch, recon_op, cond_op, skel_op, lift_op,
-    recon0, recon1, parts_out, skeleton, lifting,
-    scaled, recon, cond, parts, done,
+    vol, flag, stretch, recon_op, skel_op, lift_op, recon_out, skeleton, lifting, scaled, recon
 ):
     nv, elems = vol.shape[1], vol.shape[2]
     nq = skel_op.shape[1]
-    cond[...] = jnp.zeros_like(cond)
-    for corner in range(4):
-        real, imag = cond_op[corner, :, 0, :], cond_op[corner, :, 1, :]
-        low = corner * LANES
-        cond[low : low + nq, 0:nv] = real
-        cond[low : low + nq, LANES : LANES + nv] = -imag
-        cond[low + HALF : low + HALF + nq, 0:nv] = imag
-        cond[low + HALF : low + HALF + nq, LANES : LANES + nv] = real
     scaled_volume(vol, flag, stretch, scaled)
-    cond_high, cond_rest = split(cond[...])
-    sent = []
-    for first in range(0, elems, LANES):
-        stop = first + LANES
-        columns = jnp.concatenate(
-            [scaled[0:LANES, first:stop].T, scaled[LANES : 2 * LANES, first:stop].T], axis=1
-        )
-        high, rest = split(columns)
-        product = dot(high, cond_high, 1, 1) + dot(rest, cond_high, 1, 1) + dot(high, cond_rest, 1, 1)
-        for corner in range(4):
-            parts[corner, first:stop, :] = product[:, corner * LANES : (corner + 1) * LANES]
-        sent.append(
-            begin(
-                parts.at[:, pl.ds(first, LANES), :],
-                parts_out.at[:, pl.ds(first, LANES), :],
-                done.at[first // LANES],
-            )
-        )
     for block in range(skel_op.shape[0]):
         low = block * 2 * ROWS
         skeleton[low : low + 2 * ROWS, :] = halves(
@@ -221,16 +213,12 @@
     recon[LANES : LANES + nv, LANES : LANES + nv] = recon_op[0]
     high, rest = split(recon[...])
     size = 256
-    part = recon0.shape[2]
     for first in range(0, elems, size):
-        wanted, fine = split(scaled[:, first : first + size])
+        stop = first + size
+        wanted, fine = split(scaled[:, first:stop])
         product = dot(high, wanted) + dot(high, fine) + dot(rest, wanted)
-        target = recon0 if first < part else recon1
-        at = first % part
-        target[0, :, at : at + size] = product[0:nv]
-        target[1, :, at : at + size] = product[LANES : LANES + nv]
-    for copy in sent:
-        copy.wait()
+        recon_out[0, :, first:stop] = product[0:nv]
+        recon_out[1, :, first:stop] = product[LANES : LANES + nv]
 
 
 def skeleton_tile(matrix, block_coef, slots, picked, first, size):
@@ -293,6 +281,9 @@
 def join_kernel(up, mid, down, right, left, done):
     moves = [(down, 2, right, 0), (mid, 1, right, 1), (up, 2, right, 2)]
     moves += [(down, 0, left, 0), (mid, 0, left, 1), (up, 0, left, 2)]
+    if up.shape[0] == 6:
+        moves += [(up, 3, right, 3), (mid, 2, right, 4), (down, 3, right, 5)]
+        moves += [(up, 5, left, 3), (mid, 3, left, 4), (down, 5, left, 5)]
     copies = [
         begin(source.at[place], target.at[to], done.at[number])
         for number, (source, place, target, to) in enumerate(moves)
@@ -348,8 +339,8 @@
     halo = returned.shape[2]
     rest_copy = begin(rest, sums0.at[pl.ds(PAD, faces)], done.at[0])
     places = (
-        left.at[2], up.at[1], right.at[2], left.at[1],
-        right.at[1], left.at[0], down.at[1], right.at[0],
+        right.at[3], up.at[4], left.at[3], right.at[4],
+        left.at[4], right.at[5], down.at[4], left.at[5],
     )
     copies = [
         begin(place, returned.at[direction], done.at[1 + direction])
@@ -391,12 +382,12 @@
         )
 
 
-def lifted_loop(matrix, elem_face, start, count, elems, slots, picked, use):
+def lifted_loop(matrix, elem_face, elems, slots, picked, use):
     size = LIFT
 
     def fetch(step, target):
         for corner in range(4):
-            first = corner * count + start + step * size
+            first = corner * elems + step * size
             for extra in range(size):
                 row = elem_face[first + extra]
                 at = corner * size + extra
@@ -422,7 +413,7 @@
 
 
 def base_kernel(
-    start, count, slots_in, recon, matrix, elem_face, base, slots, picked0, picked1, done
+    slots_in, recon, matrix, elem_face, base, slots, picked0, picked1, done
 ):
     nv, elems = base.shape[1], base.shape[2]
     begin(slots_in, slots, done.at[0]).wait()
@@ -432,7 +423,7 @@
         base[0, :, first:stop] = recon[0, :, first:stop] - product[0:nv]
         base[1, :, first:stop] = recon[1, :, first:stop] - product[LANES : LANES + nv]
 
-    lifted_loop(matrix, elem_face, start, count, elems, slots, (picked0, picked1), use)
+    lifted_loop(matrix, elem_face, elems, slots, (picked0, picked1), use)
 
 
 def lift_kernel(slots_in, matrix, elem_face, lifted, slots, picked0, picked1, done):
@@ -444,7 +435,7 @@
         lifted[0, :, first:stop] = product[0:nv]
         lifted[1, :, first:stop] = product[LANES : LANES + nv]
 
-    lifted_loop(matrix, elem_face, 0, elems, elems, slots, (picked0, picked1), use)
+    lifted_loop(matrix, elem_face, elems, slots, (picked0, picked1), use)
 
 
 def image_kernel(
@@ -487,7 +478,7 @@
     slots_copy.wait()
 
 
-def finish_kernel(gathered, trace, turned, base0, base1, lifted, trace_out, volume_out):
+def finish_kernel(gathered, trace, turned, base, lifted, trace_out, volume_out):
     nq = trace.shape[0]
     line = jnp.sum(gathered[...], axis=0, keepdims=True)
     lane = lax.broadcasted_iota(jnp.int32, (1, LANES), 1)
@@ -497,13 +488,8 @@
     ]
     step_real = entry[0] / entry[2]
     step_imag = entry[1] / entry[2]
-    first = 0
-    for base in (base0, base1):
-        stop = first + base.shape[2]
-        real, imag = lifted[0, :, first:stop], lifted[1, :, first:stop]
-        volume_out[0, :, first:stop] = base[0] - (step_real * real - step_imag * imag)
-        volume_out[1, :, first:stop] = base[1] - (step_real * imag + step_imag * real)
-        first = stop
+    volume_out[0] = base[0] - (step_real * lifted[0] - step_imag * lifted[1])
+    volume_out[1] = base[1] - (step_real * lifted[1] + step_imag * lifted[0])
     rest_real = turned[0:nq, :]
     rest_imag = turned[HALF : HALF + nq, :]
     trace_out[:, 0, :] = trace[:, 0, :] + (step_real * rest_real - step_imag * rest_imag)
@@ -580,64 +566,54 @@
         down = from_behind(down, "gx", -1)
         up, down, beside = lax.optimization_barrier((up, down, beside))
         right, left = call(
-            join_kernel, "join", (up, mid, down), [up.shape, up.shape], "aaa" + "vv", [], 2, 6
+            join_kernel, "join", (up, mid, down), [up.shape, up.shape], "aaa" + "vv", [], 2,
+            2 * up.shape[0],
         )
         right = from_behind(right, "gy", sign)
         left = from_behind(left, "gy", -sign)
         return (up, down, right, left), beside
 
     trace_pairs = jnp.transpose(trace_in, (1, 0, 2))
-    table, *outgoing = call(
-        traces_kernel,
-        "traces",
-        (trace_pairs, halo_list),
-        [(PAD + faces, LANES)] + parcels,
-        "Vs" + "hvvv",
-        [((PAD + faces, LANES), F32), ((LANES, faces), F32), ((DIRS * halo, LANES), F32)],
-        8,
-        1,
-        4,
-    )
-    near = elems // 2
+    table, own_sum, *outgoing = call(
+        prepare_kernel,
+        "prepare",
+        (
+            trace_pairs, vol_rhs, flag, tilt, jnp.transpose(cond_op, (0, 2, 1, 3)),
+            halo_list, elem_face,
+        ),
+        [(PAD + faces, LANES), (faces, LANES)]
+        + [(6, ROWS, halo), (4, ROWS, halo), (6, ROWS, halo)],
+        "VVVVVss" + "hhvvv",
+        [
+            ((PAD + faces, LANES), F32),
+            ((LANES, faces), F32),
+            ((DIRS * halo, LANES), F32),
+            ((faces, LANES), F32),
+            ((2 * LANES, elems), F32),
+            ((4 * LANES, 2 * LANES), F32),
+            ((4, elems, LANES), F32),
+        ]
+        + [((slots, LANES), F32)] * 8,
+        36,
+        2,
+        15,
+    )
     operators = call(
         operators_kernel,
         "operators",
         (
-            vol_rhs, flag, tilt, recon_op, jnp.transpose(cond_op, (0, 2, 1, 3)),
+            vol_rhs, flag, tilt, recon_op,
             jnp.transpose(skel_op, (0, 2, 1, 3)), jnp.transpose(lift_op, (0, 3, 1, 2)),
         ),
-        [(2, nv, near), (2, nv, elems - near)]
-        + [(4, elems, LANES)]
-        + [(blocks * 2 * ROWS, 2 * LANES), (4 * 4 * LANES, 2 * LANES)],
-        "VVVVVVV" + "VVhBB",
-        [
-            ((2 * LANES, elems), F32),
-            ((2 * LANES, 2 * LANES), F32),
-            ((4 * LANES, 2 * LANES), F32),
-            ((4, elems, LANES), F32),
-        ],
-        18,
-        elems // LANES,
-        8,
+        [vol_rhs.shape, (blocks * 2 * ROWS, 2 * LANES), (4 * 4 * LANES, 2 * LANES)],
+        "VVVVVV" + "VBB",
+        [((2 * LANES, elems), F32), ((2 * LANES, 2 * LANES), F32)],
+        14,
+        0,
+        5,
     )
     arrived, operators = exchange(*outgoing, 1, operators)
-    recon0, recon1, parts, skeleton, lifting = operators
-    own_sum, *outgoing = call(
-        sources_kernel,
-        "sources",
-        (parts, elem_face),
-        [(faces, LANES)] + parcels,
-        "hs" + "hvvv",
-        [
-            ((faces, LANES), F32),
-            ((4, elems, LANES), F32),
-        ]
-        + [((slots, LANES), F32)] * 8
-        + [((DIRS * halo, LANES), F32)],
-        30,
-        2,
-        7,
-    )
+    recon, skeleton, lifting = operators
     slots_trace, rest = call(
         apply_kernel,
         "apply",
@@ -656,27 +632,10 @@
         3 + DIRS,
         16,
     )
-    returned, (slots_trace, rest) = exchange(*outgoing, -1, (slots_trace, rest))
-
-    def base_part(start, recon):
-        return call(
-            functools.partial(base_kernel, start, elems),
-            "base",
-            (slots_trace, recon, lifting, elem_face),
-            [recon.shape],
-            "hVBs" + "V",
-            [((PAD + slots, LANES), F32)] + [((4 * LIFT, LANES), F32)] * 2,
-            10,
-            1,
-            5,
-        )[0]
-
-    base0 = base_part(0, recon0)
-    *returned, base0 = lax.optimization_barrier((*returned, base0))
     rest_table, *outgoing = call(
         residual_kernel,
         "residual",
-        (rest, *returned, halo_list),
+        (rest, *arrived, halo_list),
         [(PAD + faces, LANES)] + parcels,
         "haaaas" + "Vvvv",
         [
@@ -689,8 +648,18 @@
         1 + DIRS,
         8,
     )
-    base1 = base_part(near, recon1)
-    arrived, base1 = exchange(*outgoing, 1, base1)
+    (base,) = call(
+        base_kernel,
+        "base",
+        (slots_trace, recon, lifting, elem_face),
+        [vol_rhs.shape],
+        "hVBs" + "V",
+        [((PAD + slots, LANES), F32)] + [((4 * LIFT, LANES), F32)] * 2,
+        14,
+        1,
+        8,
+    )
+    arrived, base = exchange(*outgoing, 1, base)
     (turned,) = call(turn_kernel, "turn", (rest_table,), [(ROWS, faces)], "VV", [], 4)
     across, along = lax.axis_size("gx"), lax.axis_size("gy")
     slots_rest, partial = call(
@@ -726,9 +695,9 @@
     trace_pairs, volume_out = call(
         finish_kernel,
         "finish",
-        (gathered, trace_pairs, turned, base0, base1, lifted),
+        (gathered, trace_pairs, turned, base, lifted),
         [trace_pairs.shape, vol_rhs.shape],
-        "vvvvvv" + "VV",
+        "vvvvv" + "VV",
         [],
         8,
     )

time: 166 us -> 158 us (0.952)
  waiting for transfers between devices: 9.81 us -> 21.1 us
  starting transfers between devices: 50.9 us -> 41.7 us
  Pallas kernels: 82.9 us -> 76.1 us
  blocking collectives: 17.7 us -> 15 us
    ppermute x12 -> x8, waiting for transfers between devices: 5.42 us -> 16.7 us  [from_behind(): return lax.ppermute(block, axis, route)]
    ppermute x12 -> x8, starting transfers between devices: 34.9 us -> 25.5 us  [from_behind(): return lax.ppermute(block, axis, route)]
    pallas_call x14 -> x11, Pallas kernels: 82.9 us -> 76.1 us  [call(): pl.pallas_call(kernel, name=name, out_shape=[pltpu.HBM(shape, BF16 if let...]
    all_to_all x1, blocking collectives: 17.7 us -> 15 us  [everywhere(): return lax.all_to_all(lines, axis, 0, 0)]
  transfers between devices with their start and end apart: 13 -> 9, of which waited for: 3 -> 6; matrix products, arithmetic and copies ran while one was open for 0% -> 0% of each run, Pallas kernels for 32% -> 13%
where the time goes in v3:
time: 158 us; the launch traced here: 157 us
  Pallas kernels  76.1 us (48%)
  starting transfers between devices  41.7 us (26%)
  waiting for transfers between devices  21.1 us (13%)
  blocking collectives  15 us (9%)
  local copies, waits for them, and re-layouts  2.66 us (2%)
    pallas_call x11, Pallas kernels, call(): pl.pallas_call(kernel, name=name, out_shape=[pltpu.HBM(shape, BF16 if let...  76.1 us
    ppermute x8, starting transfers between devices, from_behind(): return lax.ppermute(block, axis, route)  25.5 us
    ppermute x8, waiting for transfers between devices, from_behind(): return lax.ppermute(block, axis, route)  16.7 us
    all_to_all x1, starting transfers between devices, everywhere(): return lax.all_to_all(lines, axis, 0, 0)  16.2 us
    all_to_all x1, blocking collectives, everywhere(): return lax.all_to_all(lines, axis, 0, 0)  15 us
    all_to_all x1, waiting for transfers between devices, everywhere(): return lax.all_to_all(lines, axis, 0, 0)  4.38 us
  transfers between devices with their start and end apart: 9, of which 6 were waited for; matrix products, arithmetic and copies ran while one was open for 0% of the time, Pallas kernels for 13%

profile of v3, /device:TPU:1, one launch (start us, length us, event | category | flops | bytes accessed | tf_op | source)
XLA Modules:
  0.0 157.4 jit_solution(12413510822793859377)
XLA Ops:
  2.1 11.5 %prepare.1 = (f32[2056,128]{1,0:T(8,128)}, f32[2048,128]{1,0:T(8,128)}, f32[6,80,256]{2,1,0:T(8,128)S(1)}, f32[4,80,256]{2,1,0:T(8,128)S(1)}, f32[6,80,256]{2,1,0:T(8,128)S(1)}) custom-call(f32[36,2,2048]{2,1,0:T(2,128)} %bitcast.18, f32[2,120,1024]{2,1,0:T(8,128)} %vol.3, s32[1,1024]{1,0:T(1,128)} %bitcast.30, f32[1,1024]{1,0:T(1,128)} %bitcast.32, ...), custom_call_target="tpu_custom_call" | custom-call | bytes 49500000 | tf_op jit(solution)/shard_map/prepare/pallas_call | solution.py:518
  13.6 4.1 %collective-permute-start = (f32[6,80,256]{2,1,0:T(8,128)S(1)}, f32[6,80,256]{2,1,0:T(8,128)S(1)}, u32[]{:S(2)}, u32[]{:S(2)}) collective-permute-start(f32[6,80,256]{2,1,0:T(8,128)S(1)} %get-tuple-element.36), channel_id=1, source_target_pairs={{0,32},{32,64},{64,96},{96,128},{128,160},{160,192},{192,224},{224... | collective-permute-start | bytes 1474568 | tf_op jit(solution)/shard_map/ppermute | solution.py:540
  19.0 3.4 %operators.1 = (f32[2,120,1024]{2,1,0:T(8,128)}, bf16[1120,256]{1,0:T(8,128)(2,1)}, bf16[2048,256]{1,0:T(8,128)(2,1)}) custom-call(f32[2,120,1024]{2,1,0:T(8,128)} %vol.3, s32[1,1024]{1,0:T(1,128)} %bitcast.31, f32[1,1024]{1,0:T(1,128)} %bitcast.33, f32[2,120,120]{2,1,0:T(8,128)} %recon_op.1, f32[7,36,2,36]{3,2,1,0:T(2,128)} %bitcast.26, ...), custom_call_target="tpu_custom_call" | custom-call | bytes 16500000 | tf_op jit(solution)/shard_map/operators/pallas_call | solution.py:518
  22.4 1.9 %collective-permute-done.up = f32[6,80,256]{2,1,0:T(8,128)S(1)} collective-permute-done((f32[6,80,256]{2,1,0:T(8,128)S(1)}, f32[6,80,256]{2,1,0:T(8,128)S(1)}, u32[]{:S(2)}, u32[]{:S(2)}) %collective-permute-start) | collective-permute-done | bytes 491552 | tf_op jit(solution)/shard_map/ppermute | solution.py:540
  24.3 3.9 %collective-permute-done.1.down = f32[6,80,256]{2,1,0:T(8,128)S(1)} collective-permute-done((f32[6,80,256]{2,1,0:T(8,128)S(1)}, f32[6,80,256]{2,1,0:T(8,128)S(1)}, u32[]{:S(2)}, u32[]{:S(2)}) %collective-permute-start.1) | collective-permute-done | bytes 491552 | tf_op jit(solution)/shard_map/ppermute | solution.py:540
  28.1 1.4 join.2
  29.5 8.5 %collective-permute-start.2 = (f32[6,80,256]{2,1,0:T(8,128)S(1)}, f32[6,80,256]{2,1,0:T(8,128)S(1)}, u32[]{:S(2)}, u32[]{:S(2)}) collective-permute-start(f32[6,80,256]{2,1,0:T(8,128)S(1)} %get-tuple-element.44), channel_id=1, source_target_pairs={{0,1},{1,2},{2,3},{3,4},{4,5},{5,6},{6,7},{7,8},{8,9},{9,10},{10,1... | collective-permute-start | bytes 1474568 | tf_op jit(solution)/shard_map/ppermute | solution.py:540
  38.0 2.1 %collective-permute-start.3 = (f32[6,80,256]{2,1,0:T(8,128)S(1)}, f32[6,80,256]{2,1,0:T(8,128)S(1)}, u32[]{:S(2)}, u32[]{:S(2)}) collective-permute-start(f32[6,80,256]{2,1,0:T(8,128)S(1)} %get-tuple-element.45), channel_id=1, source_target_pairs={{1,0},{2,1},{3,2},{4,3},{5,4},{6,5},{7,6},{8,7},{9,8},{10,9},{11,1... | collective-permute-start | bytes 1474568 | tf_op jit(solution)/shard_map/ppermute | solution.py:540
  40.1 3.6 %collective-permute-done.2.right = f32[6,80,256]{2,1,0:T(8,128)S(1)} collective-permute-done((f32[6,80,256]{2,1,0:T(8,128)S(1)}, f32[6,80,256]{2,1,0:T(8,128)S(1)}, u32[]{:S(2)}, u32[]{:S(2)}) %collective-permute-start.2) | collective-permute-done | bytes 491552 | tf_op jit(solution)/shard_map/ppermute | solution.py:540
  43.7 4.4 %collective-permute-done.3.left = f32[6,80,256]{2,1,0:T(8,128)S(1)} collective-permute-done((f32[6,80,256]{2,1,0:T(8,128)S(1)}, f32[6,80,256]{2,1,0:T(8,128)S(1)}, u32[]{:S(2)}, u32[]{:S(2)}) %collective-permute-start.3) | collective-permute-done | bytes 491552 | tf_op jit(solution)/shard_map/ppermute | solution.py:540
  48.1 16.7 %apply.1 = (f32[4104,128]{1,0:T(8,128)}, f32[2048,128]{1,0:T(8,128)}) custom-call(f32[2056,128]{1,0:T(8,128)} %get-tuple-element.34.table, f32[2048,128]{1,0:T(8,128)} %get-tuple-element.35.own_sum, f32[6,80,256]{2,1,0:T(8,128)S(1)} %collective-permute-done.up, f32[6,80,256]{2,1,0:T(8,128)S(1)} %collective-permute-done.1.down, ...), custom_call_target="tpu_custom_call" | custom-call | bytes 52800000 | tf_op jit(solution)/shard_map/apply/pallas_call | solution.py:518
  64.9 7.9 %residual.1 = (f32[2056,128]{1,0:T(8,128)}, f32[3,80,256]{2,1,0:T(8,128)S(1)}, f32[2,80,256]{2,1,0:T(8,128)S(1)}, f32[3,80,256]{2,1,0:T(8,128)S(1)}) custom-call(f32[2048,128]{1,0:T(8,128)} %get-tuple-element.47.rest, f32[6,80,256]{2,1,0:T(8,128)S(1)} %collective-permute-done.up, f32[6,80,256]{2,1,0:T(8,128)S(1)} %collective-permute-done.1.down, ...), custom_call_target="tpu_custom_call" | custom-call | bytes 26400000 | tf_op jit(solution)/shard_map/residual/pallas_call | solution.py:518
  72.8 3.2 %collective-permute-start.4 = (f32[3,80,256]{2,1,0:T(8,128)S(1)}, f32[3,80,256]{2,1,0:T(8,128)S(1)}, u32[]{:S(2)}, u32[]{:S(2)}) collective-permute-start(f32[3,80,256]{2,1,0:T(8,128)S(1)} %get-tuple-element.49), channel_id=1, source_target_pairs={{0,32},{32,64},{64,96},{96,128},{128,160},{160,192},{192,224},{224... | collective-permute-start | bytes 737288 | tf_op jit(solution)/shard_map/ppermute | solution.py:540
  77.3 7.5 %base.1 = f32[2,120,1024]{2,1,0:T(8,128)} custom-call(f32[4104,128]{1,0:T(8,128)} %get-tuple-element.51.slots_in, f32[2,120,1024]{2,1,0:T(8,128)} %get-tuple-element.52.recon, bf16[2048,256]{1,0:T(8,128)(2,1)} %get-tuple-element.53.matrix, s32[4096]{0:T(1024)S(1)} %bitcast.21), custom_call_target="tpu_custom_call" | custom-call | bytes 26400000 | tf_op jit(solution)/shard_map/base/pallas_call | solution.py:518
  85.6 2.9 %collective-permute-start.6 = (f32[3,80,256]{2,1,0:T(8,128)S(1)}, f32[3,80,256]{2,1,0:T(8,128)S(1)}, u32[]{:S(2)}, u32[]{:S(2)}) collective-permute-start(f32[3,80,256]{2,1,0:T(8,128)S(1)} %get-tuple-element.57), channel_id=1, source_target_pairs={{0,1},{1,2},{2,3},{3,4},{4,5},{5,6},{6,7},{7,8},{8,9},{9,10},{10,1... | collective-permute-start | bytes 737288 | tf_op jit(solution)/shard_map/ppermute | solution.py:540
  88.5 2.1 %collective-permute-start.7 = (f32[3,80,256]{2,1,0:T(8,128)S(1)}, f32[3,80,256]{2,1,0:T(8,128)S(1)}, u32[]{:S(2)}, u32[]{:S(2)}) collective-permute-start(f32[3,80,256]{2,1,0:T(8,128)S(1)} %get-tuple-element.58), channel_id=1, source_target_pairs={{1,0},{2,1},{3,2},{4,3},{5,4},{6,5},{7,6},{8,7},{9,8},{10,9},{11,1... | collective-permute-start | bytes 737288 | tf_op jit(solution)/shard_map/ppermute | solution.py:540
  90.6 2.4 %turn.1.turned = f32[80,2048]{1,0:T(8,128)} custom-call(f32[2056,128]{1,0:T(8,128)} %get-tuple-element.48.rest_table), custom_call_target="tpu_custom_call" | custom-call | bytes 3300000 | tf_op jit(solution)/shard_map/turn/pallas_call | solution.py:518
  93.1 2.9 %collective-permute-done.7.left = f32[3,80,256]{2,1,0:T(8,128)S(1)} collective-permute-done((f32[3,80,256]{2,1,0:T(8,128)S(1)}, f32[3,80,256]{2,1,0:T(8,128)S(1)}, u32[]{:S(2)}, u32[]{:S(2)}) %collective-permute-start.7) | collective-permute-done | bytes 245792 | tf_op jit(solution)/shard_map/ppermute | solution.py:540
  96.0 15.6 %image.1 = (f32[4104,128]{1,0:T(8,128)}, f32[32,128]{1,0:T(8,128)}) custom-call(f32[2056,128]{1,0:T(8,128)} %get-tuple-element.48.rest_table, f32[80,2048]{1,0:T(8,128)} %turn.1.turned, f32[3,80,256]{2,1,0:T(8,128)S(1)} %collective-permute-done.4.up, f32[3,80,256]{2,1,0:T(8,128)S(1)} %collective-permute-done.5.down, ...), custom_call_target="tpu_custom_call" | custom-call | bytes 52800000 | tf_op jit(solution)/shard_map/image/pallas_call | solution.py:518
  111.6 16.2 %all-to-all-start = ((f32[32,1,128]{2,1,0:T(1,128)}), f32[32,1,128]{2,1,0:T(1,128)S(1)}, u32[]{:S(2)}, u32[]{:S(2)}) async-start(f32[32,1,128]{2,1,0:T(1,128)} %bitcast.7), calls=%async_computation | async-start | bytes 32768 | tf_op jit(solution)/shard_map/all_to_all | solution.py:544
  127.9 7.3 %lift.1.lifted = f32[2,120,1024]{2,1,0:T(8,128)} custom-call(f32[4104,128]{1,0:T(8,128)} %get-tuple-element.60.slots_in, bf16[2048,256]{1,0:T(8,128)(2,1)} %get-tuple-element.53.matrix, s32[4096]{0:T(1024)S(1)} %bitcast.22), custom_call_target="tpu_custom_call" | custom-call | bytes 23100000 | tf_op jit(solution)/shard_map/lift/pallas_call | solution.py:518
  135.2 4.4 %all-to-all-done = f32[32,1,128]{2,1,0:T(1,128)S(1)} async-done(((f32[32,1,128]{2,1,0:T(1,128)}), f32[32,1,128]{2,1,0:T(1,128)S(1)}, u32[]{:S(2)}, u32[]{:S(2)}) %all-to-all-start) | async-done | bytes 16416 | tf_op jit(solution)/shard_map/all_to_all | solution.py:544
  139.6 15.0 %all_to_all.20 = f32[16,1,128]{2,1,0:T(1,128)S(1)} all-to-all(f32[16,1,128]{2,1,0:T(1,128)S(1)} %broadcast_in_dim.2), channel_id=1, replica_groups=mesh['gx'=16,'gy'=32] {'gx'}, dimensions={0} | all-to-all | bytes 16384 | tf_op jit(solution)/shard_map/all_to_all | solution.py:544
  155.8 1.5 finish.1
  (21 shorter events, 6.0 us)
Async XLA Ops:
  2.1 38.1 %copy-start.4 = (s32[6,2048]{1,0:T(8,128)S(1)}, s32[6,2048]{1,0:T(8,128)}, u32[]{:S(2)}) copy-start(s32[6,2048]{1,0:T(8,128)} %param.22) | copy-start | bytes 147460
  13.6 10.7 %collective-permute-start = (f32[6,80,256]{2,1,0:T(8,128)S(1)}, f32[6,80,256]{2,1,0:T(8,128)S(1)}, u32[]{:S(2)}, u32[]{:S(2)}) collective-permute-start(f32[6,80,256]{2,1,0:T(8,128)S(1)} %get-tuple-element.36), channel_id=1, source_target_pairs={{0,32},{32,64},{64,96},{96,128},{128,160},{160,192},{192,224},{224... | collective-permute-start | bytes 1474568 | tf_op jit(solution)/shard_map/ppermute | solution.py:540
  17.7 10.5 %collective-permute-start.1 = (f32[6,80,256]{2,1,0:T(8,128)S(1)}, f32[6,80,256]{2,1,0:T(8,128)S(1)}, u32[]{:S(2)}, u32[]{:S(2)}) collective-permute-start(f32[6,80,256]{2,1,0:T(8,128)S(1)} %get-tuple-element.37), channel_id=1, source_target_pairs={{32,0},{64,32},{96,64},{128,96},{160,128},{192,160},{224,192},{256... | collective-permute-start | bytes 1474568 | tf_op jit(solution)/shard_map/ppermute | solution.py:540
  29.5 14.2 %collective-permute-start.2 = (f32[6,80,256]{2,1,0:T(8,128)S(1)}, f32[6,80,256]{2,1,0:T(8,128)S(1)}, u32[]{:S(2)}, u32[]{:S(2)}) collective-permute-start(f32[6,80,256]{2,1,0:T(8,128)S(1)} %get-tuple-element.44), channel_id=1, source_target_pairs={{0,1},{1,2},{2,3},{3,4},{4,5},{5,6},{6,7},{7,8},{8,9},{9,10},{10,1... | collective-permute-start | bytes 1474568 | tf_op jit(solution)/shard_map/ppermute | solution.py:540
  38.0 10.1 %collective-permute-start.3 = (f32[6,80,256]{2,1,0:T(8,128)S(1)}, f32[6,80,256]{2,1,0:T(8,128)S(1)}, u32[]{:S(2)}, u32[]{:S(2)}) collective-permute-start(f32[6,80,256]{2,1,0:T(8,128)S(1)} %get-tuple-element.45), channel_id=1, source_target_pairs={{1,0},{2,1},{3,2},{4,3},{5,4},{6,5},{7,6},{8,7},{9,8},{10,9},{11,1... | collective-permute-start | bytes 1474568 | tf_op jit(solution)/shard_map/ppermute | solution.py:540
  72.8 12.0 %collective-permute-start.4 = (f32[3,80,256]{2,1,0:T(8,128)S(1)}, f32[3,80,256]{2,1,0:T(8,128)S(1)}, u32[]{:S(2)}, u32[]{:S(2)}) collective-permute-start(f32[3,80,256]{2,1,0:T(8,128)S(1)} %get-tuple-element.49), channel_id=1, source_target_pairs={{0,32},{32,64},{64,96},{96,128},{128,160},{160,192},{192,224},{224... | collective-permute-start | bytes 737288 | tf_op jit(solution)/shard_map/ppermute | solution.py:540
  76.0 8.8 %collective-permute-start.5 = (f32[3,80,256]{2,1,0:T(8,128)S(1)}, f32[3,80,256]{2,1,0:T(8,128)S(1)}, u32[]{:S(2)}, u32[]{:S(2)}) collective-permute-start(f32[3,80,256]{2,1,0:T(8,128)S(1)} %get-tuple-element.50), channel_id=1, source_target_pairs={{32,0},{64,32},{96,64},{128,96},{160,128},{192,160},{224,192},{256... | collective-permute-start | bytes 737288 | tf_op jit(solution)/shard_map/ppermute | solution.py:540
  85.6 7.5 %collective-permute-start.6 = (f32[3,80,256]{2,1,0:T(8,128)S(1)}, f32[3,80,256]{2,1,0:T(8,128)S(1)}, u32[]{:S(2)}, u32[]{:S(2)}) collective-permute-start(f32[3,80,256]{2,1,0:T(8,128)S(1)} %get-tuple-element.57), channel_id=1, source_target_pairs={{0,1},{1,2},{2,3},{3,4},{4,5},{5,6},{6,7},{7,8},{8,9},{9,10},{10,1... | collective-permute-start | bytes 737288 | tf_op jit(solution)/shard_map/ppermute | solution.py:540
  88.5 7.5 %collective-permute-start.7 = (f32[3,80,256]{2,1,0:T(8,128)S(1)}, f32[3,80,256]{2,1,0:T(8,128)S(1)}, u32[]{:S(2)}, u32[]{:S(2)}) collective-permute-start(f32[3,80,256]{2,1,0:T(8,128)S(1)} %get-tuple-element.58), channel_id=1, source_target_pairs={{1,0},{2,1},{3,2},{4,3},{5,4},{6,5},{7,6},{8,7},{9,8},{10,9},{11,1... | collective-permute-start | bytes 737288 | tf_op jit(solution)/shard_map/ppermute | solution.py:540
  111.6 28.0 %all-to-all-start = ((f32[32,1,128]{2,1,0:T(1,128)}), f32[32,1,128]{2,1,0:T(1,128)S(1)}, u32[]{:S(2)}, u32[]{:S(2)}) async-start(f32[32,1,128]{2,1,0:T(1,128)} %bitcast.7), calls=%async_computation | async-start | bytes 32768 | tf_op jit(solution)/shard_map/all_to_all | solution.py:544
  127.8 26.8 %copy-start = (f32[80,2048]{1,0:T(8,128)S(1)}, f32[80,2048]{1,0:T(8,128)}, u32[]{:S(2)}) copy-start(f32[80,2048]{1,0:T(8,128)} %turn.1.turned) | copy-start | bytes 1966084
  127.9 26.8 %copy-start.1 = (f32[2,120,1024]{2,1,0:T(8,128)S(1)}, f32[2,120,1024]{2,1,0:T(8,128)}, u32[]{:S(2)}) copy-start(f32[2,120,1024]{2,1,0:T(8,128)} %base.1) | copy-start | bytes 2949124
  127.9 26.8 %copy-start.3 = (f32[2,36,2048]{2,0,1:T(2,128)S(1)}, f32[2,36,2048]{2,0,1:T(2,128)}, u32[]{:S(2)}) copy-start(f32[2,36,2048]{2,0,1:T(2,128)} %param.13) | copy-start | bytes 1769476
  154.6 1.2 copy-start.2

commit v4 on v3

--- a/solution.py
+++ b/solution.py
@@ -49,6 +49,15 @@
     lax.fori_loop(0, count // UNROLL, some, 0)
 
 
+def as_stored(table):
+    lines, count = table.shape
+    return jnp.transpose(table.reshape(lines, count // LANES, LANES), (1, 0, 2)).reshape(-1)
+
+
+def stored_at(lines, line, entry):
+    return (entry // LANES) * (lines * LANES) + line * LANES + entry % LANES
+
+
 def begin(source, target, semaphore):
     copy = pltpu.make_async_copy(source, target, semaphore)
     copy.start()
@@ -57,6 +66,11 @@
 
 def parcel_of(rows):
     return rows.T[:ROWS]
+
+
+def picked_parcel(picked, direction, halo):
+    starts = [stored_at(DIRS, direction, first) for first in range(0, halo, LANES)]
+    return jnp.concatenate([parcel_of(picked[at : at + LANES, :]) for at in starts], axis=1)
 
 
 def rows_of(parcel):
@@ -77,7 +91,7 @@
 
 def place_parcels(picked, halo, lower, middle, upper):
     for direction in range(DIRS):
-        parcel = parcel_of(picked[direction * halo : (direction + 1) * halo, :])
+        parcel = picked_parcel(picked, direction, halo)
         if direction < 3:
             lower[direction] = parcel
         elif direction < 5:
@@ -126,20 +140,26 @@
         total[...] = jnp.zeros_like(total)
     near = elems // 2
 
-    def add_some(step, carry):
+    def add_some(chunk, step, carry):
+        first = chunk * 4 * LANES + step * 4
         for extra in range(4):
-            elem = step * 4 + extra
+            elem = chunk * LANES + step * 4 + extra
             places = [
                 (corner, elem + part * near) for corner in range(4) for part in range(2)
             ]
-            slots = [elem_face[corner * elems + at] for corner, at in places]
+            slots = [
+                elem_face[first + extra + stored_at(4, corner, part * near)]
+                for corner in range(4)
+                for part in range(2)
+            ]
             before = [total[pl.ds(slot, 1), :] for total, slot in zip(sums, slots)]
             values = [parts[corner, pl.ds(at, 1), :] for corner, at in places]
             for number, total in enumerate(sums):
                 total[pl.ds(slots[number], 1), :] = before[number] + values[number]
         return carry
 
-    lax.fori_loop(0, near // 4, add_some, 0)
+    for chunk in range(near // LANES):
+        lax.fori_loop(0, LANES // 4, functools.partial(add_some, chunk), 0)
 
     def summed(first, size):
         lines = [total[first : first + size, :] for total in sums]
@@ -151,7 +171,7 @@
     own_copy = begin(own, own_sum, done.at[1])
     gather_rows(DIRS * halo, halo_list, rows, picked)
     for direction in range(DIRS):
-        parcel = parcel_of(picked[direction * halo : (direction + 1) * halo, :])
+        parcel = picked_parcel(picked, direction, halo)
         back = parcel_of(summed(faces + direction * halo, halo))
         if direction < 3:
             down[direction] = parcel
@@ -356,17 +376,21 @@
     rest_copy.wait()
     sums = (sums0,) + others
 
-    def add_some(step, carry):
+    def add_some(chunk, step, carry):
+        first = chunk * DIRS * LANES + step * 4
         for extra in range(4):
-            entry = step * 4 + extra
-            places = [halo_list[direction * halo + entry] + PAD for direction in range(DIRS)]
+            entry = chunk * LANES + step * 4 + extra
+            places = [
+                halo_list[first + extra + direction * LANES] + PAD for direction in range(DIRS)
+            ]
             before = [total[pl.ds(place, 1), :] for total, place in zip(sums, places)]
             values = [back[direction, pl.ds(entry, 1), :] for direction in range(DIRS)]
             for number, total in enumerate(sums):
                 total[pl.ds(places[number], 1), :] = before[number] + values[number]
         return carry
 
-    lax.fori_loop(0, halo // 4, add_some, 0)
+    for chunk in range(halo // LANES):
+        lax.fori_loop(0, LANES // 4, functools.partial(add_some, chunk), 0)
     rest_table[...] = ((sums0[...] + sums1[...]) + (sums2[...] + sums3[...])) + (
         (sums4[...] + sums5[...]) + (sums6[...] + sums7[...])
     )
@@ -387,9 +411,8 @@
 
     def fetch(step, target):
         for corner in range(4):
-            first = corner * elems + step * size
             for extra in range(size):
-                row = elem_face[first + extra]
+                row = elem_face[stored_at(4, corner, step * size + extra)]
                 at = corner * size + extra
                 target[at : at + 1, :] = slots[pl.ds(row + PAD, 1), :]
 
@@ -503,6 +526,7 @@
     "h": pltpu.HBM,
     "V": pltpu.MemorySpace.VMEM,
     "B": pltpu.MemorySpace.VMEM,
+    "S": pltpu.MemorySpace.SMEM,
 }
 
 
@@ -512,7 +536,7 @@
     if semaphores:
         shapes.append(pltpu.SemaphoreType.DMA((semaphores,)))
     args = [
-        pltpu.with_memory_space_constraint(arg, pltpu.HBM) if letter in "hVB" else arg
+        pltpu.with_memory_space_constraint(arg, pltpu.HBM) if letter in "hVBS" else arg
         for arg, letter in zip(args, spaces)
     ]
     return pl.pallas_call(
@@ -554,9 +578,9 @@
     blocks = skel_op.shape[0]
     neighbours = adjacency.shape[0]
     slots = faces + DIRS * halo
-    elem_face = elem_face.reshape(-1)
+    elem_face = as_stored(elem_face)
     adjacency = adjacency.reshape(-1)
-    halo_list = halo_list.reshape(-1)
+    halo_list = as_stored(halo_list)
     flag = pml_flag.reshape(1, elems)
     tilt = stretch.reshape(1, elems)
     parcels = [(3, ROWS, halo), (2, ROWS, halo), (3, ROWS, halo)]
@@ -583,7 +607,7 @@
         ),
         [(PAD + faces, LANES), (faces, LANES)]
         + [(6, ROWS, halo), (4, ROWS, halo), (6, ROWS, halo)],
-        "VVVVVss" + "hhvvv",
+        "VVVVVSS" + "hhvvv",
         [
             ((PAD + faces, LANES), F32),
             ((LANES, faces), F32),

time: 158 us -> 157 us (level)
  no operation moved by 1% of the time
where the time goes in v4:
time: 157 us; the launch traced here: 156 us
  Pallas kernels  76.1 us (48%)
  starting transfers between devices  41.7 us (27%)
  waiting for transfers between devices  21 us (13%)
  blocking collectives  15 us (10%)
    pallas_call x11, Pallas kernels, call(): pl.pallas_call(kernel, name=name, out_shape=[pltpu.HBM(shape, BF16 if let...  76.1 us
    ppermute x8, starting transfers between devices, from_behind(): return lax.ppermute(block, axis, route)  25.5 us
    ppermute x8, waiting for transfers between devices, from_behind(): return lax.ppermute(block, axis, route)  16.7 us
    all_to_all x1, starting transfers between devices, everywhere(): return lax.all_to_all(lines, axis, 0, 0)  16.2 us
    all_to_all x1, blocking collectives, everywhere(): return lax.all_to_all(lines, axis, 0, 0)  15 us
    all_to_all x1, waiting for transfers between devices, everywhere(): return lax.all_to_all(lines, axis, 0, 0)  4.36 us
  transfers between devices with their start and end apart: 9, of which 6 were waited for; matrix products, arithmetic and copies ran while one was open for 0% of the time, Pallas kernels for 13%

profile of v4, /device:TPU:1, one launch (start us, length us, event | category | flops | bytes accessed | tf_op | source)
XLA Modules:
  0.0 156.0 jit_solution(13983501160780883992)
XLA Ops:
  0.6 11.5 %prepare.1 = (f32[2056,128]{1,0:T(8,128)}, f32[2048,128]{1,0:T(8,128)}, f32[6,80,256]{2,1,0:T(8,128)S(1)}, f32[4,80,256]{2,1,0:T(8,128)S(1)}, f32[6,80,256]{2,1,0:T(8,128)S(1)}) custom-call(f32[36,2,2048]{2,1,0:T(2,128)} %bitcast.22, f32[2,120,1024]{2,1,0:T(8,128)} %vol.3, s32[1,1024]{1,0:T(1,128)} %bitcast.34, f32[1,1024]{1,0:T(1,128)} %bitcast.36, ...), custom_call_target="tpu_custom_call" | custom-call | bytes 49500000 | tf_op jit(solution)/shard_map/prepare/pallas_call | solution.py:542
  12.2 4.1 %collective-permute-start = (f32[6,80,256]{2,1,0:T(8,128)S(1)}, f32[6,80,256]{2,1,0:T(8,128)S(1)}, u32[]{:S(2)}, u32[]{:S(2)}) collective-permute-start(f32[6,80,256]{2,1,0:T(8,128)S(1)} %get-tuple-element.36), channel_id=1, source_target_pairs={{0,32},{32,64},{64,96},{96,128},{128,160},{160,192},{192,224},{224... | collective-permute-start | bytes 1474568 | tf_op jit(solution)/shard_map/ppermute | solution.py:564
  17.6 3.4 %operators.1 = (f32[2,120,1024]{2,1,0:T(8,128)}, bf16[1120,256]{1,0:T(8,128)(2,1)}, bf16[2048,256]{1,0:T(8,128)(2,1)}) custom-call(f32[2,120,1024]{2,1,0:T(8,128)} %vol.3, s32[1,1024]{1,0:T(1,128)} %bitcast.35, f32[1,1024]{1,0:T(1,128)} %bitcast.37, f32[2,120,120]{2,1,0:T(8,128)} %recon_op.1, f32[7,36,2,36]{3,2,1,0:T(2,128)} %bitcast.30, ...), custom_call_target="tpu_custom_call" | custom-call | bytes 16500000 | tf_op jit(solution)/shard_map/operators/pallas_call | solution.py:542
  21.0 1.9 %collective-permute-done.up = f32[6,80,256]{2,1,0:T(8,128)S(1)} collective-permute-done((f32[6,80,256]{2,1,0:T(8,128)S(1)}, f32[6,80,256]{2,1,0:T(8,128)S(1)}, u32[]{:S(2)}, u32[]{:S(2)}) %collective-permute-start) | collective-permute-done | bytes 491552 | tf_op jit(solution)/shard_map/ppermute | solution.py:564
  22.9 3.9 %collective-permute-done.1.down = f32[6,80,256]{2,1,0:T(8,128)S(1)} collective-permute-done((f32[6,80,256]{2,1,0:T(8,128)S(1)}, f32[6,80,256]{2,1,0:T(8,128)S(1)}, u32[]{:S(2)}, u32[]{:S(2)}) %collective-permute-start.1) | collective-permute-done | bytes 491552 | tf_op jit(solution)/shard_map/ppermute | solution.py:564
  26.7 1.4 join.2
  28.1 8.5 %collective-permute-start.2 = (f32[6,80,256]{2,1,0:T(8,128)S(1)}, f32[6,80,256]{2,1,0:T(8,128)S(1)}, u32[]{:S(2)}, u32[]{:S(2)}) collective-permute-start(f32[6,80,256]{2,1,0:T(8,128)S(1)} %get-tuple-element.44), channel_id=1, source_target_pairs={{0,1},{1,2},{2,3},{3,4},{4,5},{5,6},{6,7},{7,8},{8,9},{9,10},{10,1... | collective-permute-start | bytes 1474568 | tf_op jit(solution)/shard_map/ppermute | solution.py:564
  36.6 2.1 %collective-permute-start.3 = (f32[6,80,256]{2,1,0:T(8,128)S(1)}, f32[6,80,256]{2,1,0:T(8,128)S(1)}, u32[]{:S(2)}, u32[]{:S(2)}) collective-permute-start(f32[6,80,256]{2,1,0:T(8,128)S(1)} %get-tuple-element.45), channel_id=1, source_target_pairs={{1,0},{2,1},{3,2},{4,3},{5,4},{6,5},{7,6},{8,7},{9,8},{10,9},{11,1... | collective-permute-start | bytes 1474568 | tf_op jit(solution)/shard_map/ppermute | solution.py:564
  38.7 3.6 %collective-permute-done.2.right = f32[6,80,256]{2,1,0:T(8,128)S(1)} collective-permute-done((f32[6,80,256]{2,1,0:T(8,128)S(1)}, f32[6,80,256]{2,1,0:T(8,128)S(1)}, u32[]{:S(2)}, u32[]{:S(2)}) %collective-permute-start.2) | collective-permute-done | bytes 491552 | tf_op jit(solution)/shard_map/ppermute | solution.py:564
  42.4 4.4 %collective-permute-done.3.left = f32[6,80,256]{2,1,0:T(8,128)S(1)} collective-permute-done((f32[6,80,256]{2,1,0:T(8,128)S(1)}, f32[6,80,256]{2,1,0:T(8,128)S(1)}, u32[]{:S(2)}, u32[]{:S(2)}) %collective-permute-start.3) | collective-permute-done | bytes 491552 | tf_op jit(solution)/shard_map/ppermute | solution.py:564
  46.8 16.7 %apply.1 = (f32[4104,128]{1,0:T(8,128)}, f32[2048,128]{1,0:T(8,128)}) custom-call(f32[2056,128]{1,0:T(8,128)} %get-tuple-element.34.table, f32[2048,128]{1,0:T(8,128)} %get-tuple-element.35.own_sum, f32[6,80,256]{2,1,0:T(8,128)S(1)} %collective-permute-done.up, f32[6,80,256]{2,1,0:T(8,128)S(1)} %collective-permute-done.1.down, ...), custom_call_target="tpu_custom_call" | custom-call | bytes 52800000 | tf_op jit(solution)/shard_map/apply/pallas_call | solution.py:542
  63.5 8.0 %residual.1 = (f32[2056,128]{1,0:T(8,128)}, f32[3,80,256]{2,1,0:T(8,128)S(1)}, f32[2,80,256]{2,1,0:T(8,128)S(1)}, f32[3,80,256]{2,1,0:T(8,128)S(1)}) custom-call(f32[2048,128]{1,0:T(8,128)} %get-tuple-element.47.rest, f32[6,80,256]{2,1,0:T(8,128)S(1)} %collective-permute-done.up, f32[6,80,256]{2,1,0:T(8,128)S(1)} %collective-permute-done.1.down, ...), custom_call_target="tpu_custom_call" | custom-call | bytes 26400000 | tf_op jit(solution)/shard_map/residual/pallas_call | solution.py:542
  71.5 3.2 %collective-permute-start.4 = (f32[3,80,256]{2,1,0:T(8,128)S(1)}, f32[3,80,256]{2,1,0:T(8,128)S(1)}, u32[]{:S(2)}, u32[]{:S(2)}) collective-permute-start(f32[3,80,256]{2,1,0:T(8,128)S(1)} %get-tuple-element.49), channel_id=1, source_target_pairs={{0,32},{32,64},{64,96},{96,128},{128,160},{160,192},{192,224},{224... | collective-permute-start | bytes 737288 | tf_op jit(solution)/shard_map/ppermute | solution.py:564
  76.0 7.5 %base.1 = f32[2,120,1024]{2,1,0:T(8,128)} custom-call(f32[4104,128]{1,0:T(8,128)} %get-tuple-element.51.slots_in, f32[2,120,1024]{2,1,0:T(8,128)} %get-tuple-element.52.recon, bf16[2048,256]{1,0:T(8,128)(2,1)} %get-tuple-element.53.matrix, s32[4096]{0:T(1024)S(1)} %bitcast.25), custom_call_target="tpu_custom_call" | custom-call | bytes 26400000 | tf_op jit(solution)/shard_map/base/pallas_call | solution.py:542
  84.2 2.9 %collective-permute-start.6 = (f32[3,80,256]{2,1,0:T(8,128)S(1)}, f32[3,80,256]{2,1,0:T(8,128)S(1)}, u32[]{:S(2)}, u32[]{:S(2)}) collective-permute-start(f32[3,80,256]{2,1,0:T(8,128)S(1)} %get-tuple-element.57), channel_id=1, source_target_pairs={{0,1},{1,2},{2,3},{3,4},{4,5},{5,6},{6,7},{7,8},{8,9},{9,10},{10,1... | collective-permute-start | bytes 737288 | tf_op jit(solution)/shard_map/ppermute | solution.py:564
  87.2 2.1 %collective-permute-start.7 = (f32[3,80,256]{2,1,0:T(8,128)S(1)}, f32[3,80,256]{2,1,0:T(8,128)S(1)}, u32[]{:S(2)}, u32[]{:S(2)}) collective-permute-start(f32[3,80,256]{2,1,0:T(8,128)S(1)} %get-tuple-element.58), channel_id=1, source_target_pairs={{1,0},{2,1},{3,2},{4,3},{5,4},{6,5},{7,6},{8,7},{9,8},{10,9},{11,1... | collective-permute-start | bytes 737288 | tf_op jit(solution)/shard_map/ppermute | solution.py:564
  89.3 2.4 %turn.1.turned = f32[80,2048]{1,0:T(8,128)} custom-call(f32[2056,128]{1,0:T(8,128)} %get-tuple-element.48.rest_table), custom_call_target="tpu_custom_call" | custom-call | bytes 3300000 | tf_op jit(solution)/shard_map/turn/pallas_call | solution.py:542
  91.7 2.9 %collective-permute-done.7.left = f32[3,80,256]{2,1,0:T(8,128)S(1)} collective-permute-done((f32[3,80,256]{2,1,0:T(8,128)S(1)}, f32[3,80,256]{2,1,0:T(8,128)S(1)}, u32[]{:S(2)}, u32[]{:S(2)}) %collective-permute-start.7) | collective-permute-done | bytes 245792 | tf_op jit(solution)/shard_map/ppermute | solution.py:564
  94.7 15.6 %image.1 = (f32[4104,128]{1,0:T(8,128)}, f32[32,128]{1,0:T(8,128)}) custom-call(f32[2056,128]{1,0:T(8,128)} %get-tuple-element.48.rest_table, f32[80,2048]{1,0:T(8,128)} %turn.1.turned, f32[3,80,256]{2,1,0:T(8,128)S(1)} %collective-permute-done.4.up, f32[3,80,256]{2,1,0:T(8,128)S(1)} %collective-permute-done.5.down, ...), custom_call_target="tpu_custom_call" | custom-call | bytes 52800000 | tf_op jit(solution)/shard_map/image/pallas_call | solution.py:542
  110.3 16.2 %all-to-all-start = ((f32[32,1,128]{2,1,0:T(1,128)}), f32[32,1,128]{2,1,0:T(1,128)S(1)}, u32[]{:S(2)}, u32[]{:S(2)}) async-start(f32[32,1,128]{2,1,0:T(1,128)} %bitcast.15), calls=%async_computation | async-start | bytes 32768 | tf_op jit(solution)/shard_map/all_to_all | solution.py:568
  126.5 7.3 %lift.1.lifted = f32[2,120,1024]{2,1,0:T(8,128)} custom-call(f32[4104,128]{1,0:T(8,128)} %get-tuple-element.60.slots_in, bf16[2048,256]{1,0:T(8,128)(2,1)} %get-tuple-element.53.matrix, s32[4096]{0:T(1024)S(1)} %bitcast.26), custom_call_target="tpu_custom_call" | custom-call | bytes 23100000 | tf_op jit(solution)/shard_map/lift/pallas_call | solution.py:542
  133.9 4.4 %all-to-all-done = f32[32,1,128]{2,1,0:T(1,128)S(1)} async-done(((f32[32,1,128]{2,1,0:T(1,128)}), f32[32,1,128]{2,1,0:T(1,128)S(1)}, u32[]{:S(2)}, u32[]{:S(2)}) %all-to-all-start) | async-done | bytes 16416 | tf_op jit(solution)/shard_map/all_to_all | solution.py:568
  138.3 15.0 %all_to_all.20 = f32[16,1,128]{2,1,0:T(1,128)S(1)} all-to-all(f32[16,1,128]{2,1,0:T(1,128)S(1)} %broadcast_in_dim.2), channel_id=1, replica_groups=mesh['gx'=16,'gy'=32] {'gx'}, dimensions={0} | all-to-all | bytes 16384 | tf_op jit(solution)/shard_map/all_to_all | solution.py:568
  154.5 1.5 finish.1
  (23 shorter events, 4.6 us)
Async XLA Ops:
  0.6 38.1 %copy-start.6 = (s32[6,2048]{1,0:T(8,128)S(1)}, s32[6,2048]{1,0:T(8,128)}, u32[]{:S(2)}) copy-start(s32[6,2048]{1,0:T(8,128)} %param.22) | copy-start | bytes 147460
  12.2 10.7 %collective-permute-start = (f32[6,80,256]{2,1,0:T(8,128)S(1)}, f32[6,80,256]{2,1,0:T(8,128)S(1)}, u32[]{:S(2)}, u32[]{:S(2)}) collective-permute-start(f32[6,80,256]{2,1,0:T(8,128)S(1)} %get-tuple-element.36), channel_id=1, source_target_pairs={{0,32},{32,64},{64,96},{96,128},{128,160},{160,192},{192,224},{224... | collective-permute-start | bytes 1474568 | tf_op jit(solution)/shard_map/ppermute | solution.py:564
  16.3 10.5 %collective-permute-start.1 = (f32[6,80,256]{2,1,0:T(8,128)S(1)}, f32[6,80,256]{2,1,0:T(8,128)S(1)}, u32[]{:S(2)}, u32[]{:S(2)}) collective-permute-start(f32[6,80,256]{2,1,0:T(8,128)S(1)} %get-tuple-element.37), channel_id=1, source_target_pairs={{32,0},{64,32},{96,64},{128,96},{160,128},{192,160},{224,192},{256... | collective-permute-start | bytes 1474568 | tf_op jit(solution)/shard_map/ppermute | solution.py:564
  28.1 14.2 %collective-permute-start.2 = (f32[6,80,256]{2,1,0:T(8,128)S(1)}, f32[6,80,256]{2,1,0:T(8,128)S(1)}, u32[]{:S(2)}, u32[]{:S(2)}) collective-permute-start(f32[6,80,256]{2,1,0:T(8,128)S(1)} %get-tuple-element.44), channel_id=1, source_target_pairs={{0,1},{1,2},{2,3},{3,4},{4,5},{5,6},{6,7},{7,8},{8,9},{9,10},{10,1... | collective-permute-start | bytes 1474568 | tf_op jit(solution)/shard_map/ppermute | solution.py:564
  36.6 10.1 %collective-permute-start.3 = (f32[6,80,256]{2,1,0:T(8,128)S(1)}, f32[6,80,256]{2,1,0:T(8,128)S(1)}, u32[]{:S(2)}, u32[]{:S(2)}) collective-permute-start(f32[6,80,256]{2,1,0:T(8,128)S(1)} %get-tuple-element.45), channel_id=1, source_target_pairs={{1,0},{2,1},{3,2},{4,3},{5,4},{6,5},{7,6},{8,7},{9,8},{10,9},{11,1... | collective-permute-start | bytes 1474568 | tf_op jit(solution)/shard_map/ppermute | solution.py:564
  46.8 16.7 %copy-start.5 = (s32[8,256]{1,0:T(8,128)S(1)}, s32[8,256]{1,0:T(8,128)}, u32[]{:S(2)}) copy-start(s32[8,256]{1,0:T(8,128)} %param.23) | copy-start | bytes 24580
  63.5 12.5 %copy-start.4 = (s32[4,1024]{1,0:T(4,128)S(1)}, s32[4,1024]{1,0:T(4,128)}, u32[]{:S(2)}) copy-start(s32[4,1024]{1,0:T(4,128)} %param.21) | copy-start | bytes 49156
  71.5 12.0 %collective-permute-start.4 = (f32[3,80,256]{2,1,0:T(8,128)S(1)}, f32[3,80,256]{2,1,0:T(8,128)S(1)}, u32[]{:S(2)}, u32[]{:S(2)}) collective-permute-start(f32[3,80,256]{2,1,0:T(8,128)S(1)} %get-tuple-element.49), channel_id=1, source_target_pairs={{0,32},{32,64},{64,96},{96,128},{128,160},{160,192},{192,224},{224... | collective-permute-start | bytes 737288 | tf_op jit(solution)/shard_map/ppermute | solution.py:564
  74.7 8.8 %collective-permute-start.5 = (f32[3,80,256]{2,1,0:T(8,128)S(1)}, f32[3,80,256]{2,1,0:T(8,128)S(1)}, u32[]{:S(2)}, u32[]{:S(2)}) collective-permute-start(f32[3,80,256]{2,1,0:T(8,128)S(1)} %get-tuple-element.50), channel_id=1, source_target_pairs={{32,0},{64,32},{96,64},{128,96},{160,128},{192,160},{224,192},{256... | collective-permute-start | bytes 737288 | tf_op jit(solution)/shard_map/ppermute | solution.py:564
  84.2 7.5 %collective-permute-start.6 = (f32[3,80,256]{2,1,0:T(8,128)S(1)}, f32[3,80,256]{2,1,0:T(8,128)S(1)}, u32[]{:S(2)}, u32[]{:S(2)}) collective-permute-start(f32[3,80,256]{2,1,0:T(8,128)S(1)} %get-tuple-element.57), channel_id=1, source_target_pairs={{0,1},{1,2},{2,3},{3,4},{4,5},{5,6},{6,7},{7,8},{8,9},{9,10},{10,1... | collective-permute-start | bytes 737288 | tf_op jit(solution)/shard_map/ppermute | solution.py:564
  87.2 7.5 %collective-permute-start.7 = (f32[3,80,256]{2,1,0:T(8,128)S(1)}, f32[3,80,256]{2,1,0:T(8,128)S(1)}, u32[]{:S(2)}, u32[]{:S(2)}) collective-permute-start(f32[3,80,256]{2,1,0:T(8,128)S(1)} %get-tuple-element.58), channel_id=1, source_target_pairs={{1,0},{2,1},{3,2},{4,3},{5,4},{6,5},{7,6},{8,7},{9,8},{10,9},{11,1... | collective-permute-start | bytes 737288 | tf_op jit(solution)/shard_map/ppermute | solution.py:564
  110.3 27.9 %all-to-all-start = ((f32[32,1,128]{2,1,0:T(1,128)}), f32[32,1,128]{2,1,0:T(1,128)S(1)}, u32[]{:S(2)}, u32[]{:S(2)}) async-start(f32[32,1,128]{2,1,0:T(1,128)} %bitcast.15), calls=%async_computation | async-start | bytes 32768 | tf_op jit(solution)/shard_map/all_to_all | solution.py:568
  126.5 26.8 %copy-start = (f32[80,2048]{1,0:T(8,128)S(1)}, f32[80,2048]{1,0:T(8,128)}, u32[]{:S(2)}) copy-start(f32[80,2048]{1,0:T(8,128)} %turn.1.turned) | copy-start | bytes 1966084
  126.5 26.7 %copy-start.1 = (f32[2,120,1024]{2,1,0:T(8,128)S(1)}, f32[2,120,1024]{2,1,0:T(8,128)}, u32[]{:S(2)}) copy-start(f32[2,120,1024]{2,1,0:T(8,128)} %base.1) | copy-start | bytes 2949124
  126.5 26.7 %copy-start.3 = (f32[2,36,2048]{2,0,1:T(2,128)S(1)}, f32[2,36,2048]{2,0,1:T(2,128)}, u32[]{:S(2)}) copy-start(f32[2,36,2048]{2,0,1:T(2,128)} %param.13) | copy-start | bytes 1769476
  153.3 1.2 copy-start.2
